TPU v7x, 32 devices: a whole 2x2x4 slice. The times are simulated.
32 devices in a mesh: gx: 8 (over z, y), gy: 4 (over x, core).
Axes of the slice: x: 2, y: 2, z: 4, core: 2. Of those that a mesh axis runs over, the one named last changes fastest.
Arguments:
- stream: bfloat16 [64, 18432], P(('gx', 'gy')), may hold values from -6 to 6
- norm_gain: float32 [18432], replicated, may hold values from 0.1 to 1.9
- w_gate: bfloat16 [18432, 36864], P('gx', 'gy'), may hold values from -0.046875 to 0.046875
- w_up: bfloat16 [18432, 36864], P('gx', 'gy'), may hold values from -0.046875 to 0.046875
- w_query: bfloat16 [18432, 6144], P('gx', 'gy'), may hold values from -0.046875 to 0.046875
- w_keyval: bfloat16 [18432, 512], P('gx', 'gy'), may hold values from -0.046875 to 0.046875
- k_cache: bfloat16 [64, 512, 256], P(('gx', 'gy')), may hold values from -200 to 200
- v_cache: bfloat16 [64, 512, 256], P(('gx', 'gy')), may hold values from -6 to 6
- lengths: int32 [64], P(('gx', 'gy')), may hold values from 1 to 512, 16384 in all
Outputs:
- hidden: bfloat16 [64, 36864], P('gx', 'gy')
- context: bfloat16 [64, 6144], P(('gx', 'gy'))
Inputs may be any that keep to these rules, and one draw needn't show every extreme that they name: `lengths`: some row has 512 filled slots.
All inputs are finite; a program needn't handle non-finite values. No bound on the sum of `lengths` on one device may be relied on, other than what follows from the above.
Results may differ from a plain program's by a relative error of at most 0.017.
The roundings to bfloat16 on the way count: a program that leaves them out, or rounds other values in their place, can miss the bound.
Values may be sent and summed in bfloat16 or wider, within the bound.
No kernel may reach another device: no remote copies, remote signals or barrier semaphores. Data moves between devices by JAX's collectives and lax.ppermute only.
A program may use at most 192 MiB of HBM per device.

v0:
```python
import jax
import jax.numpy as jnp
from jax import lax
from jax.sharding import PartitionSpec as P

HEADS = 24
DH = 256


def body(stream, norm_gain, w_gate, w_up, w_query, w_keyval, k_cache, v_cache, lengths):
    values = stream.astype(jnp.float32)
    mean = jnp.mean(values, axis=1, keepdims=True)
    centred = values - mean
    variance = jnp.mean(centred * centred, axis=1, keepdims=True)
    normed = (centred / jnp.sqrt(variance + 1e-05) * norm_gain[None, :]).astype(jnp.bfloat16)
    grouped = lax.all_gather(normed, "gy", axis=0, tiled=True)
    rows_in = lax.all_to_all(grouped, "gx", split_axis=1, concat_axis=0, tiled=True)
    ff_local = w_gate.shape[1]
    block = rows_in
    attn_part = lax.psum_scatter(
        jnp.concatenate(
            [
                jnp.dot(block, w_query, preferred_element_type=jnp.float32),
                jnp.dot(block, w_keyval, preferred_element_type=jnp.float32),
            ],
            axis=1,
        ),
        "gx",
        scatter_dimension=0,
        tiled=True,
    )
    block = rows_in
    ffn_part = lax.psum_scatter(
        jnp.concatenate(
            [
                jnp.dot(block, w_gate, preferred_element_type=jnp.float32),
                jnp.dot(block, w_up, preferred_element_type=jnp.float32),
            ],
            axis=1,
        ),
        "gx",
        scatter_dimension=0,
        tiled=True,
    )
    hidden = (jax.nn.silu(ffn_part[:, :ff_local]) * ffn_part[:, ff_local:]).astype(jnp.bfloat16)
    projected = attn_part.astype(jnp.bfloat16)
    row_major = lax.all_to_all(projected, "gy", split_axis=0, concat_axis=1, tiled=True)
    groups = lax.axis_size("gy")
    query_cols = w_query.shape[1]
    keyval_cols = w_keyval.shape[1]
    rows = row_major.shape[0]
    pieces = row_major.reshape(rows, groups, query_cols + keyval_cols)
    query = pieces[:, :, :query_cols].reshape(rows, HEADS, DH)
    keyval = pieces[:, :, query_cols:].reshape(rows, groups * keyval_cols)
    new_key = keyval[:, :DH]
    new_value = keyval[:, DH:]
    scale = DH ** (-0.5)
    scores = jnp.einsum("bhd,bld->bhl", query, k_cache, preferred_element_type=jnp.float32) * scale
    score_new = jnp.einsum("bhd,bd->bh", query, new_key, preferred_element_type=jnp.float32) * scale
    mask = (jnp.arange(k_cache.shape[1], dtype=jnp.int32)[None, :] < lengths[:, None])[:, None, :]
    top = jnp.maximum(jnp.max(jnp.where(mask, scores, -1e30), axis=2), score_new)
    exponent = jnp.where(mask, jnp.exp(scores - top[:, :, None]), 0.0)
    exponent_new = jnp.exp(score_new - top)
    total = jnp.sum(exponent, axis=2) + exponent_new
    weights = (exponent / total[:, :, None]).astype(jnp.bfloat16)
    weights_new = (exponent_new / total).astype(jnp.bfloat16)
    context = jnp.einsum("bhl,bld->bhd", weights, v_cache, preferred_element_type=jnp.float32)
    context = (
        context
        + weights_new.astype(jnp.float32)[:, :, None] * new_value.astype(jnp.float32)[:, None, :]
    )
    return (hidden, context.reshape(rows, HEADS * DH).astype(jnp.bfloat16))


def solution(mesh):
    return jax.shard_map(
        body,
        mesh=mesh,
        in_specs=(
            P(("gx", "gy"), None),
            P(),
            P("gx", "gy"),
            P("gx", "gy"),
            P("gx", "gy"),
            P("gx", "gy"),
            P(("gx", "gy"), None, None),
            P(("gx", "gy"), None, None),
            P(("gx", "gy")),
        ),
        out_specs=(P("gx", "gy"), P(("gx", "gy"), None)),
        check_vma=False,
    )
```

profile of v0, /device:TPU:0, one launch (start us, length us, event | category | flops | bytes accessed | tf_op | source)
XLA Modules:
  0.0 182.5 jit_solution(7730566105599755743)
XLA Ops:
  7.2 0.0 copy-start
  7.2 0.0 reduce-scatter.2.cloned.1.call-start
  7.2 1.2 convert_reduce_fusion
  8.4 1.2 fusion.15
  9.7 1.1 fusion.17
  10.8 7.4 %all-gather = bf16[4,2,18432]{2,1,0:T(2,128)(2,1)S(1)} all-gather(bf16[1,2,18432]{2,1,0:T(2,128)(2,1)S(1)} %fusion.17), channel_id=1, replica_groups=mesh['gx'=8,'gy'=4] {'gy'}, dimensions={0}, use_global_device_ids=true | all-gather | bytes 368640 | tf_op jit(solution)/shard_map/all_gather | solution.py:16
  18.1 0.2 all_to_all.26
  18.3 0.1 copy.17
  18.4 16.5 %all_to_all.35 = bf16[8,8,2304]{2,0,1:T(8,128)(2,1)S(1)} all-to-all(bf16[8,8,2304]{2,0,1:T(8,128)(2,1)S(1)} %copy.17), channel_id=1, replica_groups=mesh['gx'=8,'gy'=4] {'gx'}, dimensions={1} | all-to-all | bytes 589824 | tf_op jit(solution)/shard_map/all_to_all | solution.py:17
  34.9 16.9 %fusion.7 = f32[64,9216]{1,0:T(8,128)S(1)} fusion(bf16[2304,9216]{1,0:T(8,128)(2,1)} %param.12, bf16[8,8,2304]{2,0,1:T(8,128)(2,1)S(1)} %all_to_all.35), kind=kOutput, calls=%fused_computation.12 | convolution fusion | flops 2717908992 | bytes 45121536 | tf_op jit(solution)/shard_map/dot_general | solution.py:37
  51.7 16.9 %fusion.9 = f32[64,9216]{1,0:T(8,128)S(1)} fusion(bf16[2304,9216]{1,0:T(8,128)(2,1)} %param.11, bf16[8,8,2304]{2,0,1:T(8,128)(2,1)S(1)} %all_to_all.35), kind=kOutput, calls=%fused_computation.14 | convolution fusion | flops 2717908992 | bytes 45121536 | tf_op jit(solution)/shard_map/dot_general | solution.py:36
  68.6 0.0 copy-start.4
  68.6 2.5 %pad_maximum_fusion = f32[64,18432]{1,0:T(8,128)} fusion(f32[64,9216]{1,0:T(8,128)S(1)} %fusion.7, f32[64,9216]{1,0:T(8,128)S(1)} %fusion.9), kind=kLoop, calls=%fused_computation | loop fusion | flops 1179648 | bytes 9437184 | tf_op jit(solution)/shard_map/concatenate | solution.py:34
  71.1 0.0 copy-start.2
  71.1 0.0 copy-start.1
  71.1 0.0 copy-start.3
  71.1 0.0 reduce-scatter.2.cloned.1.call-update
  71.1 0.0 copy-done.4
  71.1 0.6 dynamic-slice
  72.4 0.0 copy-done
  72.4 0.2 fusion.3
  72.6 4.4 %fusion.5 = f32[64,1536]{1,0:T(8,128)S(1)} fusion(bf16[2304,1536]{1,0:T(8,128)(2,1)} %param.13, bf16[8,8,2304]{2,0,1:T(8,128)(2,1)S(1)} %all_to_all.35), kind=kOutput, calls=%fused_computation.10 | convolution fusion | flops 452984832 | bytes 7766016 | tf_op jit(solution)/shard_map/dot_general | solution.py:23
  77.0 48.9 %all-reduce.2 = bf16[64,1664]{1,0:T(8,128)(2,1)S(1)} all-reduce(f32[64,1664]{1,0:T(8,128)S(1)} %pad_maximum_fusion.1), channel_id=3, replica_groups=mesh['gx'=8,'gy'=4] {'gx'}, use_global_device_ids=true, to_apply=%region_3.0.clone | all-reduce | flops 106496 | bytes 638976
  126.0 0.6 all_to_all.30
  126.6 3.3 %all-to-all-start.1 = ((bf16[4,2,1664]{2,1,0:T(2,128)(2,1)}), bf16[4,2,1664]{2,1,0:T(2,128)(2,1)S(1)}, u32[]{:S(2)}, u32[]{:S(2)}) async-start(bf16[4,2,1664]{2,1,0:T(2,128)(2,1)} %all_to_all.30), calls=%async_computation.2 | async-start | bytes 53248 | tf_op jit(solution)/shard_map/all_to_all | solution.py:47
  129.9 0.0 copy-done.2
  129.9 0.1 iota_compare_fusion
  130.0 3.8 %all-to-all-done.1 = bf16[4,2,1664]{2,1,0:T(2,128)(2,1)S(1)} async-done(((bf16[4,2,1664]{2,1,0:T(2,128)(2,1)}), bf16[4,2,1664]{2,1,0:T(2,128)(2,1)S(1)}, u32[]{:S(2)}, u32[]{:S(2)}) %all-to-all-start.1) | async-done | bytes 26656 | tf_op jit(solution)/shard_map/all_to_all | solution.py:47
  133.9 0.1 fusion.22
  134.0 0.0 copy-done.1
  134.0 0.3 select_reduce_fusion
  134.3 0.2 fusion.16
  134.5 0.0 copy-done.3
  134.5 0.2 fusion.1
  134.8 0.6 copy.21
  135.4 38.5 %reduce-scatter.2.cloned.1.call-done = f32[8,18432]{1,0:T(8,128)} async-done(((f32[64,18432]{1,0:T(8,128)}), f32[8,18432]{1,0:T(8,128)}) %reduce-scatter.2.cloned.1.call-update) | async-done | bytes 589840 | tf_op jit(solution)/shard_map/reduce_scatter | solution.py:33
  173.9 1.8 fusion.2
  (11 shorter events, 0.1 us)
Async XLA Ops:
  7.2 65.2 %copy-start = (bf16[2304,128]{1,0:T(8,128)(2,1)S(1)}, bf16[2304,128]{1,0:T(8,128)(2,1)}, u32[]{:S(2)}) copy-start(bf16[2304,128]{1,0:T(8,128)(2,1)} %param.14) | copy-start | bytes 1769476
  7.2 166.7 %reduce-scatter.2.cloned.1.call-start = ((), (), s32[]{:S(2)}) async-start(), calls=%async_computation.3 | async-start | bytes 5308416 | tf_op jit(solution)/shard_map/reduce_scatter | solution.py:33
  68.6 2.5 %copy-start.4 = (u32[32]{0:T(128)S(1)}, u32[32]{0:T(128)}, u32[]{:S(2)}) copy-start(u32[32]{0:T(128)} %constant.24) | copy-start | bytes 388
  71.1 58.8 %copy-start.2 = (s32[2]{0:T(128)S(1)}, s32[2]{0:T(128)}, u32[]{:S(2)}) copy-start(s32[2]{0:T(128)} %param.17) | copy-start | bytes 28
  71.1 62.9 %copy-start.1 = (bf16[2,512,256]{2,1,0:T(8,128)(2,1)S(1)}, bf16[2,512,256]{2,1,0:T(8,128)(2,1)}, u32[]{:S(2)}) copy-start(bf16[2,512,256]{2,1,0:T(8,128)(2,1)} %param.15) | copy-start | bytes 1572868
  71.1 63.4 %copy-start.3 = (bf16[2,512,256]{2,1,0:T(8,128)(2,1)S(1)}, bf16[2,512,256]{2,1,0:T(8,128)(2,1)}, u32[]{:S(2)}) copy-start(bf16[2,512,256]{2,1,0:T(8,128)(2,1)} %param.16) | copy-start | bytes 1572868
  126.6 7.1 %all-to-all-start.1 = ((bf16[4,2,1664]{2,1,0:T(2,128)(2,1)}), bf16[4,2,1664]{2,1,0:T(2,128)(2,1)S(1)}, u32[]{:S(2)}, u32[]{:S(2)}) async-start(bf16[4,2,1664]{2,1,0:T(2,128)(2,1)} %all_to_all.30), calls=%async_computation.2 | async-start | bytes 53248 | tf_op jit(solution)/shard_map/all_to_all | solution.py:47
Sparse Core Ops, SparseCore 0:
  71.2 102.5 reduce-scatter.1
where the time goes:
time: 183 us
  blocking collectives  72.8 us (40%)
  waiting for transfers between devices  42.3 us (23%)
  matrix products  39 us (21%)
  between operations  14.8 us (8%)
  other arithmetic  8.1 us (4%)
  starting transfers between devices  3.3 us (2%)
  local copies, waits for them, and re-layouts  2.19 us (1%)
    unnamed x1, blocking collectives  48.9 us
    reduce_scatter x1, waiting for transfers between devices, body(): lax.psum_scatter(jnp.concatenate([jnp.dot(block, w_gate, preferred_elemen...  38.5 us
    dot_general x1, matrix products, body(): jnp.dot(block, w_gate, preferred_element_type=jnp.float32)  16.9 us
    dot_general x1, matrix products, body(): jnp.dot(block, w_up, preferred_element_type=jnp.float32)  16.9 us
    all_to_all x1, blocking collectives, body(): lax.all_to_all(grouped, 'gx', split_axis=1, concat_axis=0, tiled=True)  16.5 us
    all_gather x1, blocking collectives, body(): grouped = lax.all_gather(normed, 'gy', axis=0, tiled=True)  7.37 us
    dot_general x1, matrix products, body(): jnp.dot(block, w_query, preferred_element_type=jnp.float32)  4.37 us
    all_to_all x1, waiting for transfers between devices, body(): lax.all_to_all(projected, 'gy', split_axis=0, concat_axis=1, tiled=True)  3.79 us
  transfers between devices with their start and end apart: 2, of which 2 were waited for; matrix products, arithmetic and copies ran while one was open for 4% of the time, Pallas kernels for 0%

commit v1 on v0

v1 whole, which is shorter than its diff:
```python
import functools

import jax
import jax.numpy as jnp
from jax import lax
from jax.experimental import pallas as pl
from jax.experimental.pallas import tpu as pltpu
from jax.sharding import PartitionSpec as P

HEADS = 24
DH = 256
EPS = 1e-05
PORTIONS = (3, 5, 4)

BF16 = jnp.bfloat16
F32 = jnp.float32
VMEM = pl.BlockSpec(memory_space=pltpu.VMEM)
ANY = pl.BlockSpec(memory_space=pl.ANY)
SMEM = pl.BlockSpec(memory_space=pltpu.SMEM)


def shape(dims, dtype):
    return jax.ShapeDtypeStruct(tuple(dims), dtype)


def matmul(a, b):
    return jnp.dot(a, b, preferred_element_type=F32)


def swap(x, axis, bit):
    size = lax.axis_size(axis)
    return lax.ppermute(x, axis, [(i, i ^ bit) for i in range(size)])


def bits_of(size):
    return [1 << t for t in range(size.bit_length() - 1)]


def norm_kernel(blocks, where_ref, x_ref, gain_ref, keep_ref, send_ref):
    values = x_ref[...].astype(F32)
    width = values.shape[1]
    mean = jnp.sum(values, axis=1, keepdims=True) / width
    centred = values - mean
    variance = jnp.sum(centred * centred, axis=1, keepdims=True) / width
    root = jnp.sqrt(variance + EPS)
    part = width // blocks
    for k in range(blocks):
        start = pl.multiple_of((where_ref[0] ^ k) * part, 128)
        piece = x_ref[:, pl.ds(start, part)].astype(F32)
        normed = ((piece - mean) / root * gain_ref[:, pl.ds(start, part)]).astype(BF16)
        (send_ref if k % 2 else keep_ref)[k // 2] = normed


def normalise(stream, norm_gain, where, blocks):
    rows, width = stream.shape
    out = shape((blocks // 2, rows, width // blocks), BF16)
    return pl.pallas_call(
        functools.partial(norm_kernel, blocks),
        out_shape=(out, out),
        in_specs=[SMEM, VMEM, VMEM],
        out_specs=(VMEM, VMEM),
        cost_estimate=pl.CostEstimate(flops=20 * 10**9, bytes_accessed=10**6, transcendentals=0),
        compiler_params=pltpu.CompilerParams(vmem_limit_bytes=4 << 20),
        name="layer_norm",
    )(where, stream, norm_gain.reshape(1, width))


def attn_kernel(slots, order, where_ref, x_ref, wq_ref, wkv_ref, x_out, send_ref, keep_ref):
    total = x_ref.shape[0]
    groups = len(order)
    per = total // (groups * slots)
    row = lax.broadcasted_iota(jnp.int32, (total, total), 0)
    col = lax.broadcasted_iota(jnp.int32, (total, total), 1)
    base = (row // (per * groups)) * per + row % per
    slot = (row // per) % groups
    x = x_ref[...]

    def placed(want):
        source = jnp.zeros_like(row)
        for position, j in enumerate(order):
            source = jnp.where(want == j, position * (slots * per) + base, source)
        return matmul((col == source).astype(BF16), x).astype(BF16)

    x_out[...] = placed(slot ^ where_ref[1])
    relative = placed(slot)
    wide = wq_ref.shape[1]
    both = groups * per
    for lanes, w_ref in ((slice(0, wide), wq_ref), (slice(wide, wide + wkv_ref.shape[1]), wkv_ref)):
        part = matmul(relative, w_ref[...])
        for k in range(slots):
            (send_ref if k % 2 else keep_ref)[k // 2, :, lanes] = part[k * both : (k + 1) * both]


def attn_partials(x, w_query, w_keyval, where, slots, order):
    total, depth = x.shape
    cols = w_query.shape[1] + w_keyval.shape[1]
    out = shape((slots // 2, total // slots, cols), F32)
    return pl.pallas_call(
        functools.partial(attn_kernel, slots, order),
        out_shape=(shape(x.shape, BF16), out, out),
        in_specs=[SMEM, VMEM, VMEM, VMEM],
        out_specs=(VMEM, VMEM, VMEM),
        cost_estimate=pl.CostEstimate(
            flops=2 * total * depth * cols, bytes_accessed=2 * depth * cols, transcendentals=0
        ),
        compiler_params=pltpu.CompilerParams(vmem_limit_bytes=6 << 20),
        name="attn_partials",
    )(where, x, w_query, w_keyval)


def ffn_kernel(slots, first, count, x_ref, gate_ref, up_ref, send_ref, keep_ref, held, sems):
    tile = held.shape[2]
    rows = x_ref.shape[0] // slots

    def fetch(step, slot):
        columns = pl.ds(pl.multiple_of((first + step) * tile, tile), tile)
        return pltpu.make_async_copy(up_ref.at[:, columns], held.at[slot], sems.at[slot])

    for step in range(min(2, count)):
        fetch(step, step).start()

    def body(step, carry):
        slot = lax.rem(step, 2)
        x = x_ref[...]
        gate = matmul(x, gate_ref[:, pl.ds(pl.multiple_of((first + step) * tile, tile), tile)])
        fetch(step, slot).wait()
        up = matmul(x, held[slot])
        lanes = pl.ds(pl.multiple_of(step * tile, tile), tile)
        for k in range(slots):
            mine = slice(k * rows, (k + 1) * rows)
            both = jnp.concatenate([gate[mine], up[mine]], axis=0)
            ref = send_ref if k % 2 else keep_ref
            ref[k // 2, :, lanes] = both.astype(ref.dtype)

        @pl.when(step + 2 < count)
        def _():
            fetch(step + 2, slot).start()

        return carry

    lax.fori_loop(0, count, body, 0)


def ffn_partials(x, w_gate, w_up, slots, tile, first, count):
    total, depth = x.shape
    cols = count * tile
    dims = (slots // 2, 2 * total // slots, cols)
    return pl.pallas_call(
        functools.partial(ffn_kernel, slots, first, count),
        out_shape=(shape(dims, BF16), shape(dims, F32)),
        in_specs=[VMEM, VMEM, ANY],
        out_specs=(VMEM, VMEM),
        scratch_shapes=[pltpu.VMEM((2, depth, tile), BF16), pltpu.SemaphoreType.DMA((2,))],
        cost_estimate=pl.CostEstimate(
            flops=4 * total * depth * cols, bytes_accessed=2 * depth * cols, transcendentals=0
        ),
        compiler_params=pltpu.CompilerParams(vmem_limit_bytes=10 << 20),
        name="ffn_partials_%d" % first,
    )(x, w_gate, w_up)


def scatter_sum(send, keep, size, dtype):
    for bit in bits_of(size):
        keep = keep + swap(send, "gx", bit).astype(F32)
        if keep.shape[0] > 1:
            send, keep = keep[1::2].astype(dtype), keep[0::2]
    return keep[0]


def attention_kernel(order, where_ref, lengths_ref, pieces_ref, k_ref, v_ref, out_ref, q_ref):
    rows, cache, _ = k_ref.shape
    groups = len(order)
    keyval_cols = 2 * DH // groups
    query_cols = pieces_ref.shape[2] - keyval_cols
    per = query_cols // DH
    heads = groups * per
    scale = DH ** (-0.5)
    contexts = []
    for b in range(rows):
        halves = []
        for g in range(groups):
            slot = where_ref[1] ^ g
            position = jnp.int32(0)
            for p, j in enumerate(order):
                position = jnp.where(slot == j, p, position)
            piece = pieces_ref[position].astype(F32)[b : b + 1]
            for h in range(per):
                q_ref[g * per + h : g * per + h + 1] = piece[:, h * DH : (h + 1) * DH]
            halves.append(piece[:, query_cols:])
        keyval = jnp.concatenate(halves, axis=1)
        new_key, new_value = keyval[:, :DH], keyval[:, DH:]
        query = q_ref[...]
        scores = lax.dot_general(
            query.astype(BF16), k_ref[b], (((1,), (1,)), ((), ())), preferred_element_type=F32
        ) * scale
        score_new = jnp.sum(query * new_key, axis=1, keepdims=True) * scale
        mask = lax.broadcasted_iota(jnp.int32, (heads, cache), 1) < lengths_ref[b]
        top = jnp.maximum(jnp.max(jnp.where(mask, scores, -1e30), axis=1, keepdims=True), score_new)
        exponent = jnp.where(mask, jnp.exp(scores - top), 0.0)
        exponent_new = jnp.exp(score_new - top)
        total = jnp.sum(exponent, axis=1, keepdims=True) + exponent_new
        weights = (exponent / total).astype(BF16)
        weights_new = (exponent_new / total).astype(BF16).astype(F32)
        contexts.append(matmul(weights, v_ref[b]) + weights_new * new_value)
    for h in range(heads):
        both = jnp.concatenate([c[h : h + 1] for c in contexts], axis=0)
        out_ref[:, h * DH : (h + 1) * DH] = both.astype(BF16)


def attention(pieces, k_cache, v_cache, lengths, where, order):
    rows, cache, _ = k_cache.shape
    return pl.pallas_call(
        functools.partial(attention_kernel, order),
        out_shape=shape((rows, HEADS * DH), BF16),
        in_specs=[SMEM, SMEM, VMEM, VMEM, VMEM],
        out_specs=VMEM,
        scratch_shapes=[pltpu.VMEM((HEADS, DH), F32)],
        cost_estimate=pl.CostEstimate(
            flops=4 * rows * HEADS * cache * DH, bytes_accessed=4 * rows * cache * DH, transcendentals=0
        ),
        compiler_params=pltpu.CompilerParams(vmem_limit_bytes=6 << 20),
        name="attention",
    )(where, lengths, pieces, k_cache, v_cache)


def body(stream, norm_gain, w_gate, w_up, w_query, w_keyval, k_cache, v_cache, lengths):
    size, groups = lax.axis_size("gx"), lax.axis_size("gy")
    where = jnp.stack([lax.axis_index("gx"), lax.axis_index("gy")]).astype(jnp.int32)
    rows = stream.shape[0]
    depth, ff = w_gate.shape

    keep, send = normalise(stream, norm_gain, where, size)
    keep = keep[:, None]
    send = send[:, None]
    for bit in bits_of(size):
        keep = jnp.concatenate([keep, swap(send, "gx", bit)], axis=1)
        if keep.shape[0] > 1:
            send, keep = keep[1::2], keep[0::2]
    x = keep.reshape(size * rows, depth)
    order = [0]
    for bit in bits_of(groups)[::-1]:
        x = jnp.concatenate([x, swap(x, "gy", bit)], axis=0)
        order = order + [j ^ bit for j in order]

    x, send, keep = attn_partials(x, w_query, w_keyval, where, size, order)

    tile = max(t for t in range(128, 769, 128) if ff % t == 0)
    blocks = ff // tile
    edges = [round(blocks * sum(PORTIONS[:i]) / sum(PORTIONS)) for i in range(len(PORTIONS) + 1)]
    halves = []
    for first, last in zip(edges[:-1], edges[1:]):
        if last > first:
            halves.append(ffn_partials(x, w_gate, w_up, size, tile, first, last - first))

    projected = scatter_sum(send, keep, size, F32).astype(BF16)
    pieces = projected.reshape(groups, 1, rows, projected.shape[1])
    for bit in bits_of(groups)[::-1]:
        middle = pieces.shape[0] // 2
        pieces = jnp.concatenate([pieces[:middle], swap(pieces[middle:], "gy", bit)], axis=1)
    context = attention(pieces[0], k_cache, v_cache, lengths, where, order)

    hidden = []
    for send, keep in halves:
        both = scatter_sum(send, keep, size, BF16)
        middle = both.shape[0] // 2
        hidden.append((jax.nn.silu(both[:middle]) * both[middle:]).astype(BF16))
    return jnp.concatenate(hidden, axis=1), context


def solution(mesh):
    return jax.shard_map(
        body,
        mesh=mesh,
        in_specs=(
            P(("gx", "gy"), None),
            P(),
            P("gx", "gy"),
            P("gx", "gy"),
            P("gx", "gy"),
            P("gx", "gy"),
            P(("gx", "gy"), None, None),
            P(("gx", "gy"), None, None),
            P(("gx", "gy")),
        ),
        out_specs=(P("gx", "gy"), P(("gx", "gy"), None)),
        check_vma=False,
    )
```

time: 183 us -> 125 us (0.68)
  blocking collectives: 72.8 us -> 0 us
  matrix products: 39 us -> 0 us
  Pallas kernels: 0 us -> 30.2 us
  local copies, waits for them, and re-layouts: 2.19 us -> 31.3 us
  starting transfers between devices: 3.3 us -> 32.3 us
  waiting for transfers between devices: 42.3 us -> 23.9 us
  between operations: 14.8 us -> 0.94 us
  other arithmetic: 8.1 us -> 5.62 us
    unnamed x1 -> x0, blocking collectives: 48.9 us -> none
    dot_general x7 -> x0, matrix products: 39 us -> none  [the longest x1 16.9 us: body(): jnp.dot(block, w_gate, preferred_element_type=jnp.float32)]
    reduce_scatter x1 -> x0, waiting for transfers between devices: 38.5 us -> none  [body(): lax.psum_scatter(jnp.concatenate([jnp.dot(block, w_gate, preferred_elemen...]
    ppermute x0 -> x19, starting transfers between devices: none -> 32.3 us  [swap(): return lax.ppermute(x, axis, [(i, i ^ bit) for i in range(size)])]
    pallas_call x0 -> x6, Pallas kernels: none -> 30.2 us  [the longest x3 24.8 us: ffn_partials(): pl.pallas_call(functools.partial(ffn_kernel, slots, first, count), out_sh...]
    unnamed x12 -> x19, local copies, waits for them, and re-layouts: 1.25 us -> 31 us
    ppermute x0 -> x19, waiting for transfers between devices: none -> 23.9 us  [swap(): return lax.ppermute(x, axis, [(i, i ^ bit) for i in range(size)])]
    all_to_all x1 -> x0, blocking collectives: 16.5 us -> none  [body(): lax.all_to_all(grouped, 'gx', split_axis=1, concat_axis=0, tiled=True)]
  transfers between devices with their start and end apart: 2 -> 19, of which waited for: 2 -> 10; matrix products, arithmetic and copies ran while one was open for 4% -> 4% of each run, Pallas kernels for 0% -> 22%
where the time goes in v1:
time: 125 us; the launch traced here: 124 us
  starting transfers between devices  32.3 us (26%)
  local copies, waits for them, and re-layouts  31.3 us (25%)
  Pallas kernels  30.2 us (24%)
  waiting for transfers between devices  23.9 us (19%)
  other arithmetic  5.62 us (4%)
    ppermute x19, starting transfers between devices, swap(): return lax.ppermute(x, axis, [(i, i ^ bit) for i in range(size)])  32.3 us
    unnamed x19, local copies, waits for them, and re-layouts  31 us
    pallas_call x3, Pallas kernels, ffn_partials(): pl.pallas_call(functools.partial(ffn_kernel, slots, first, count), out_sh...  24.8 us
    ppermute x19, waiting for transfers between devices, swap(): return lax.ppermute(x, axis, [(i, i ^ bit) for i in range(size)])  23.9 us
    another operation x3, other arithmetic  3.12 us
  transfers between devices with their start and end apart: 19, of which 10 were waited for; matrix products, arithmetic and copies ran while one was open for 4% of the time, Pallas kernels for 22%

profile of v1, /device:TPU:0, one launch (start us, length us, event | category | flops | bytes accessed | tf_op | source)
XLA Modules:
  0.0 124.2 jit_solution(13656072231948527391)
XLA Ops:
  0.6 0.0 copy-start.3
  0.6 0.1 pad_add_fusion.where_ref
  0.7 0.9 copy-done.7
  1.7 0.9 copy-done.8
  2.5 1.1 layer_norm.1
  3.6 3.0 %collective-permute-start = (bf16[4,1,2,2304]{3,2,0,1:T(2,128)(2,1)S(1)}, bf16[4,1,2,2304]{3,2,0,1:T(2,128)(2,1)S(1)}, u32[]{:S(2)}, u32[]{:S(2)}) collective-permute-start(bf16[4,1,2,2304]{3,2,0,1:T(2,128)(2,1)S(1)} %bitcast.41), channel_id=1, source_target_pairs={{0,4},{4,0},{8,12},{12,8},{16,20},{20,16},{24,28},{28,24},{1,5},{5... | collective-permute-start | bytes 110600 | tf_op jit(solution)/shard_map/ppermute | solution.py:32
  6.7 1.9 %collective-permute-done = bf16[4,1,2,2304]{3,2,0,1:T(2,128)(2,1)S(1)} collective-permute-done((bf16[4,1,2,2304]{3,2,0,1:T(2,128)(2,1)S(1)}, bf16[4,1,2,2304]{3,2,0,1:T(2,128)(2,1)S(1)}, u32[]{:S(2)}, u32[]{:S(2)}) %collective-permute-start) | collective-permute-done | bytes 36896 | tf_op jit(solution)/shard_map/ppermute | solution.py:32
  8.6 0.1 pad_maximum_fusion.3
  8.7 0.1 fusion.11
  8.8 2.1 %collective-permute-start.1 = (bf16[2,2,2,2304]{3,2,0,1:T(2,128)(2,1)S(1)}, bf16[2,2,2,2304]{3,2,0,1:T(2,128)(2,1)S(1)}, u32[]{:S(2)}, u32[]{:S(2)}) collective-permute-start(bf16[2,2,2,2304]{3,2,0,1:T(2,128)(2,1)S(1)} %get-tuple-element.33), channel_id=1, source_target_pairs={{0,8},{4,12},{8,0},{12,4},{16,24},{20,28},{24,16},{28,20},{1,9},{5... | collective-permute-start | bytes 110600 | tf_op jit(solution)/shard_map/ppermute | solution.py:32
  10.9 1.9 %collective-permute-done.1 = bf16[2,2,2,2304]{3,2,0,1:T(2,128)(2,1)S(1)} collective-permute-done((bf16[2,2,2,2304]{3,2,0,1:T(2,128)(2,1)S(1)}, bf16[2,2,2,2304]{3,2,0,1:T(2,128)(2,1)S(1)}, u32[]{:S(2)}, u32[]{:S(2)}) %collective-permute-start.1) | collective-permute-done | bytes 36896 | tf_op jit(solution)/shard_map/ppermute | solution.py:32
  12.9 0.1 fusion.7
  13.0 3.1 %collective-permute-start.2 = (bf16[1,4,2,2304]{3,2,0,1:T(2,128)(2,1)S(1)}, bf16[1,4,2,2304]{3,2,0,1:T(2,128)(2,1)S(1)}, u32[]{:S(2)}, u32[]{:S(2)}) collective-permute-start(bf16[1,4,2,2304]{3,2,0,1:T(2,128)(2,1)S(1)} %get-tuple-element.31), channel_id=1, source_target_pairs={{0,16},{4,20},{8,24},{12,28},{16,0},{20,4},{24,8},{28,12},{1,17},{... | collective-permute-start | bytes 110600 | tf_op jit(solution)/shard_map/ppermute | solution.py:32
  16.1 1.9 %collective-permute-done.2 = bf16[1,4,2,2304]{3,2,0,1:T(2,128)(2,1)S(1)} collective-permute-done((bf16[1,4,2,2304]{3,2,0,1:T(2,128)(2,1)S(1)}, bf16[1,4,2,2304]{3,2,0,1:T(2,128)(2,1)S(1)}, u32[]{:S(2)}, u32[]{:S(2)}) %collective-permute-start.2) | collective-permute-done | bytes 36896 | tf_op jit(solution)/shard_map/ppermute | solution.py:32
  18.0 0.1 pad_maximum_fusion.4
  18.1 1.9 %collective-permute-start.3 = (bf16[16,2304]{1,0:T(8,128)(2,1)S(1)}, bf16[16,2304]{1,0:T(8,128)(2,1)S(1)}, u32[]{:S(2)}, u32[]{:S(2)}) collective-permute-start(bf16[16,2304]{1,0:T(8,128)(2,1)S(1)} %reshape.25), channel_id=1, source_target_pairs={{0,2},{1,3},{2,0},{3,1},{4,6},{5,7},{6,4},{7,5},{8,10},{9,11},{10,... | collective-permute-start | bytes 221192 | tf_op jit(solution)/shard_map/ppermute | solution.py:32
  20.0 2.5 %collective-permute-done.3 = bf16[16,2304]{1,0:T(8,128)(2,1)S(1)} collective-permute-done((bf16[16,2304]{1,0:T(8,128)(2,1)S(1)}, bf16[16,2304]{1,0:T(8,128)(2,1)S(1)}, u32[]{:S(2)}, u32[]{:S(2)}) %collective-permute-start.3) | collective-permute-done | bytes 73760 | tf_op jit(solution)/shard_map/ppermute | solution.py:32
  22.6 0.1 collective-permute-start.4
  22.6 1.4 %collective-permute-done.4 = bf16[32,2304]{1,0:T(8,128)(2,1)S(1)} collective-permute-done((bf16[32,2304]{1,0:T(8,128)(2,1)S(1)}, bf16[32,2304]{1,0:T(8,128)(2,1)S(1)}, u32[]{:S(2)}, u32[]{:S(2)}) %collective-permute-start.4) | collective-permute-done | bytes 147488 | tf_op jit(solution)/shard_map/ppermute | solution.py:32
  24.0 0.0 copy-done.3
  24.0 0.0 copy-start.2
  24.1 3.0 %copy-done.2 = bf16[2304,1536]{1,0:T(8,128)(2,1)S(1)} copy-done((bf16[2304,1536]{1,0:T(8,128)(2,1)S(1)}, bf16[2304,1536]{1,0:T(8,128)(2,1)}, u32[]{:S(2)}) %copy-start.2) | copy-done | bytes 7077912
  27.1 2.2 %attn_partials.1 = (bf16[64,2304]{1,0:T(8,128)(2,1)S(1)}, f32[4,8,1664]{2,1,0:T(8,128)S(1)}, f32[4,8,1664]{2,1,0:T(8,128)S(1)}) custom-call(s32[2]{0:T(128)S(1)} %pad_add_fusion.where_ref, bf16[64,2304]{1,0:T(8,128)(2,1)S(1)} %pad_maximum_fusion.x_ref, bf16[2304,1536]{1,0:T(8,128)(2,1)S(1)} %copy-done.2, bf16[2304,128]{1,0:T(8,128)(2,1)S(1)} %copy-done.3), custom_call_target="tpu_custom_call" | custom-call | flops 490733568 | bytes 7667712 | tf_op jit(solution)/shard_map/attn_partials/pallas_call | solution.py:98
  29.3 1.9 %collective-permute-start.14 = (f32[4,8,1664]{2,1,0:T(8,128)S(1)}, f32[4,8,1664]{2,1,0:T(8,128)S(1)}, u32[]{:S(2)}, u32[]{:S(2)}) collective-permute-start(f32[4,8,1664]{2,1,0:T(8,128)S(1)} %get-tuple-element.23), channel_id=1, source_target_pairs={{0,4},{4,0},{8,12},{12,8},{16,20},{20,16},{24,28},{28,24},{1,5},{5... | collective-permute-start | bytes 638984 | tf_op jit(solution)/shard_map/ppermute | solution.py:32
  31.2 13.1 %copy-done = bf16[2304,9216]{1,0:T(8,128)(2,1)S(1)} copy-done((bf16[2304,9216]{1,0:T(8,128)(2,1)S(1)}, bf16[2304,9216]{1,0:T(8,128)(2,1)}, u32[]{:S(2)}) %copy-start) | copy-done | bytes 42467352
  44.3 6.3 %ffn_partials_0.1 = (bf16[4,16,2304]{2,1,0:T(8,128)(2,1)S(1)}, f32[4,16,2304]{2,1,0:T(8,128)S(1)}) custom-call(bf16[64,2304]{1,0:T(8,128)(2,1)S(1)} %get-tuple-element.15.x_ref, bf16[2304,9216]{1,0:T(8,128)(2,1)S(1)} %copy-done, bf16[2304,9216]{1,0:T(8,128)(2,1)} %up_ref.5), custom_call_target="tpu_custom_call" | custom-call | flops 1358954496 | bytes 10616832 | tf_op jit(solution)/shard_map/ffn_partials_0/pallas_call | solution.py:148
  50.6 0.2 collective-permute-start.5
  50.8 8.7 %ffn_partials_8.1 = (bf16[4,16,3072]{2,1,0:T(8,128)(2,1)}, f32[4,16,3072]{2,1,0:T(8,128)S(1)}) custom-call(bf16[64,2304]{1,0:T(8,128)(2,1)S(1)} %get-tuple-element.15.x_ref, bf16[2304,9216]{1,0:T(8,128)(2,1)S(1)} %copy-done, bf16[2304,9216]{1,0:T(8,128)(2,1)} %up_ref.5), custom_call_target="tpu_custom_call" | custom-call | flops 1811939328 | bytes 14155776 | tf_op jit(solution)/shard_map/ffn_partials_8/pallas_call | solution.py:148
  59.6 1.9 %collective-permute-start.11 = (bf16[4,16,3072]{2,1,0:T(8,128)(2,1)}, bf16[4,16,3072]{2,1,0:T(8,128)(2,1)}, u32[]{:S(2)}, u32[]{:S(2)}) collective-permute-start(bf16[4,16,3072]{2,1,0:T(8,128)(2,1)} %get-tuple-element.21), channel_id=1, source_target_pairs={{0,4},{4,0},{8,12},{12,8},{16,20},{20,16},{24,28},{28,24},{1,5},{5... | collective-permute-start | bytes 1179656 | tf_op jit(solution)/shard_map/ppermute | solution.py:32
  61.5 0.0 collective-permute-done.14
  61.5 1.6 %collective-permute-start.15 = (f32[2,8,1664]{2,1,0:T(8,128)S(1)}, f32[2,8,1664]{2,1,0:T(8,128)S(1)}, u32[]{:S(2)}, u32[]{:S(2)}) collective-permute-start(f32[2,8,1664]{2,1,0:T(8,128)S(1)} %slice.161), channel_id=1, source_target_pairs={{0,8},{4,12},{8,0},{12,4},{16,24},{20,28},{24,16},{28,20},{1,9},{5... | collective-permute-start | bytes 319496 | tf_op jit(solution)/shard_map/ppermute | solution.py:32
  63.2 13.1 %copy-done.1 = bf16[2304,9216]{1,0:T(8,128)(2,1)S(1)} copy-done((bf16[2304,9216]{1,0:T(8,128)(2,1)S(1)}, bf16[2304,9216]{1,0:T(8,128)(2,1)}, u32[]{:S(2)}) %copy-start.1) | copy-done | bytes 42467352
  76.3 9.8 %ffn_partials_3.1 = (bf16[4,16,3840]{2,1,0:T(8,128)(2,1)S(1)}, f32[4,16,3840]{2,1,0:T(8,128)S(1)}) custom-call(bf16[64,2304]{1,0:T(8,128)(2,1)S(1)} %get-tuple-element.15.x_ref, bf16[2304,9216]{1,0:T(8,128)(2,1)S(1)} %copy-done.1, bf16[2304,9216]{1,0:T(8,128)(2,1)} %up_ref.5), custom_call_target="tpu_custom_call" | custom-call | flops 2264924160 | bytes 17694720 | tf_op jit(solution)/shard_map/ffn_partials_3/pallas_call | solution.py:148
  86.1 0.6 collective-permute-start.8
  86.6 0.0 collective-permute-done.15
  86.7 2.9 %collective-permute-start.16 = (f32[1,8,1664]{2,1,0:T(8,128)S(1)}, f32[1,8,1664]{2,1,0:T(8,128)S(1)}, u32[]{:S(2)}, u32[]{:S(2)}) collective-permute-start(f32[1,8,1664]{2,1,0:T(8,128)S(1)} %slice.185), channel_id=1, source_target_pairs={{0,16},{4,20},{8,24},{12,28},{16,0},{20,4},{24,8},{28,12},{1,17},{... | collective-permute-start | bytes 159752 | tf_op jit(solution)/shard_map/ppermute | solution.py:32
  89.6 0.0 collective-permute-done.5
  89.6 0.9 fusion.8
  90.5 0.3 collective-permute-start.6
  90.8 1.2 collective-permute-done.16
  92.0 1.9 %collective-permute-start.17 = (bf16[2,1,2,1664]{3,2,1,0:T(2,128)(2,1)S(1)}, bf16[2,1,2,1664]{3,2,1,0:T(2,128)(2,1)S(1)}, u32[]{:S(2)}, u32[]{:S(2)}) collective-permute-start(bf16[2,1,2,1664]{3,2,1,0:T(2,128)(2,1)S(1)} %slice.167), channel_id=1, source_target_pairs={{0,2},{1,3},{2,0},{3,1},{4,6},{5,7},{6,4},{7,5},{8,10},{9,11},{10,... | collective-permute-start | bytes 39944 | tf_op jit(solution)/shard_map/ppermute | solution.py:32
  94.0 1.8 %collective-permute-done.17 = bf16[2,1,2,1664]{3,2,1,0:T(2,128)(2,1)S(1)} collective-permute-done((bf16[2,1,2,1664]{3,2,1,0:T(2,128)(2,1)S(1)}, bf16[2,1,2,1664]{3,2,1,0:T(2,128)(2,1)S(1)}, u32[]{:S(2)}, u32[]{:S(2)}) %collective-permute-start.17) | collective-permute-done | bytes 13344 | tf_op jit(solution)/shard_map/ppermute | solution.py:32
  95.9 0.1 collective-permute-start.18
  95.9 0.0 collective-permute-done.11
  95.9 1.1 fusion.10
  97.1 0.7 collective-permute-start.12
  97.8 0.0 collective-permute-done.18
  97.8 0.0 copy-done.4
  97.8 0.0 copy-done.5
  97.9 2.1 %attention.1 = bf16[2,6144]{1,0:T(2,128)(2,1)} custom-call(s32[2]{0:T(128)S(1)} %pad_add_fusion.where_ref, s32[2]{0:T(128)S(1)} %copy-done.6, bf16[4,2,1664]{2,1,0:T(2,128)(2,1)S(1)} %maximum_bitcast_fusion.pieces_ref, bf16[2,512,256]{2,1,0:T(8,128)(2,1)S(1)} %copy-done.4, bf16[2,512,256]{2,1,0:T(8,128)(2,1)S(1)} %copy-done.5), custom_call_target="tpu_custom_call" | custom-call | flops 25165824 | bytes 1048576 | tf_op jit(solution)/shard_map/attention/pallas_call | solution.py:212
  100.0 0.0 collective-permute-done.6
  100.0 1.1 convert_add_fusion.5
  101.0 2.5 %collective-permute-start.7 = (bf16[1,16,2304]{2,1,0:T(8,128)(2,1)S(1)}, bf16[1,16,2304]{2,1,0:T(8,128)(2,1)S(1)}, u32[]{:S(2)}, u32[]{:S(2)}) collective-permute-start(bf16[1,16,2304]{2,1,0:T(8,128)(2,1)S(1)} %slice.235), channel_id=1, source_target_pairs={{0,16},{4,20},{8,24},{12,28},{16,0},{20,4},{24,8},{28,12},{1,17},{... | collective-permute-start | bytes 221192 | tf_op jit(solution)/shard_map/ppermute | solution.py:32
  103.5 0.0 collective-permute-done.8
  103.5 1.1 fusion.9
  104.7 2.1 %collective-permute-start.9 = (bf16[2,16,3840]{2,1,0:T(8,128)(2,1)S(1)}, bf16[2,16,3840]{2,1,0:T(8,128)(2,1)S(1)}, u32[]{:S(2)}, u32[]{:S(2)}) collective-permute-start(bf16[2,16,3840]{2,1,0:T(8,128)(2,1)S(1)} %slice.145), channel_id=1, source_target_pairs={{0,8},{4,12},{8,0},{12,4},{16,24},{20,28},{24,16},{28,20},{1,9},{5... | collective-permute-start | bytes 737288 | tf_op jit(solution)/shard_map/ppermute | solution.py:32
  106.8 0.0 collective-permute-done.7
  106.8 0.0 collective-permute-done.12
  106.9 2.5 %collective-permute-start.13 = (bf16[1,16,3072]{2,1,0:T(8,128)(2,1)S(1)}, bf16[1,16,3072]{2,1,0:T(8,128)(2,1)S(1)}, u32[]{:S(2)}, u32[]{:S(2)}) collective-permute-start(bf16[1,16,3072]{2,1,0:T(8,128)(2,1)S(1)} %slice.234), channel_id=1, source_target_pairs={{0,16},{4,20},{8,24},{12,28},{16,0},{20,4},{24,8},{28,12},{1,17},{... | collective-permute-start | bytes 294920 | tf_op jit(solution)/shard_map/ppermute | solution.py:32
  109.4 4.8 %collective-permute-done.13 = bf16[1,16,3072]{2,1,0:T(8,128)(2,1)S(1)} collective-permute-done((bf16[1,16,3072]{2,1,0:T(8,128)(2,1)S(1)}, bf16[1,16,3072]{2,1,0:T(8,128)(2,1)S(1)}, u32[]{:S(2)}, u32[]{:S(2)}) %collective-permute-start.13) | collective-permute-done | bytes 98336 | tf_op jit(solution)/shard_map/ppermute | solution.py:32
  114.2 0.7 collective-permute-done.9
  115.0 2.8 %collective-permute-start.10 = (bf16[1,16,3840]{2,1,0:T(8,128)(2,1)S(1)}, bf16[1,16,3840]{2,1,0:T(8,128)(2,1)S(1)}, u32[]{:S(2)}, u32[]{:S(2)}) collective-permute-start(bf16[1,16,3840]{2,1,0:T(8,128)(2,1)S(1)} %slice.233), channel_id=1, source_target_pairs={{0,16},{4,20},{8,24},{12,28},{16,0},{20,4},{24,8},{28,12},{1,17},{... | collective-permute-start | bytes 368648 | tf_op jit(solution)/shard_map/ppermute | solution.py:32
  117.9 5.6 %collective-permute-done.10 = bf16[1,16,3840]{2,1,0:T(8,128)(2,1)S(1)} collective-permute-done((bf16[1,16,3840]{2,1,0:T(8,128)(2,1)S(1)}, bf16[1,16,3840]{2,1,0:T(8,128)(2,1)S(1)}, u32[]{:S(2)}, u32[]{:S(2)}) %collective-permute-start.10) | collective-permute-done | bytes 122912 | tf_op jit(solution)/shard_map/ppermute | solution.py:32
  123.6 0.7 pad_maximum_fusion.2
  (37 shorter events, 0.7 us)
Async XLA Ops:
  0.6 23.4 %copy-start.3 = (bf16[2304,128]{1,0:T(8,128)(2,1)S(1)}, bf16[2304,128]{1,0:T(8,128)(2,1)}, u32[]{:S(2)}) copy-start(bf16[2304,128]{1,0:T(8,128)(2,1)} %wkv_ref.1) | copy-start | bytes 1769476
  0.7 0.9 copy-start.7
  1.7 0.9 copy-start.8
  3.6 5.0 %collective-permute-start = (bf16[4,1,2,2304]{3,2,0,1:T(2,128)(2,1)S(1)}, bf16[4,1,2,2304]{3,2,0,1:T(2,128)(2,1)S(1)}, u32[]{:S(2)}, u32[]{:S(2)}) collective-permute-start(bf16[4,1,2,2304]{3,2,0,1:T(2,128)(2,1)S(1)} %bitcast.41), channel_id=1, source_target_pairs={{0,4},{4,0},{8,12},{12,8},{16,20},{20,16},{24,28},{28,24},{1,5},{5... | collective-permute-start | bytes 110600 | tf_op jit(solution)/shard_map/ppermute | solution.py:32
  8.8 4.1 %collective-permute-start.1 = (bf16[2,2,2,2304]{3,2,0,1:T(2,128)(2,1)S(1)}, bf16[2,2,2,2304]{3,2,0,1:T(2,128)(2,1)S(1)}, u32[]{:S(2)}, u32[]{:S(2)}) collective-permute-start(bf16[2,2,2,2304]{3,2,0,1:T(2,128)(2,1)S(1)} %get-tuple-element.33), channel_id=1, source_target_pairs={{0,8},{4,12},{8,0},{12,4},{16,24},{20,28},{24,16},{28,20},{1,9},{5... | collective-permute-start | bytes 110600 | tf_op jit(solution)/shard_map/ppermute | solution.py:32
  13.0 5.0 %collective-permute-start.2 = (bf16[1,4,2,2304]{3,2,0,1:T(2,128)(2,1)S(1)}, bf16[1,4,2,2304]{3,2,0,1:T(2,128)(2,1)S(1)}, u32[]{:S(2)}, u32[]{:S(2)}) collective-permute-start(bf16[1,4,2,2304]{3,2,0,1:T(2,128)(2,1)S(1)} %get-tuple-element.31), channel_id=1, source_target_pairs={{0,16},{4,20},{8,24},{12,28},{16,0},{20,4},{24,8},{28,12},{1,17},{... | collective-permute-start | bytes 110600 | tf_op jit(solution)/shard_map/ppermute | solution.py:32
  18.1 4.4 %collective-permute-start.3 = (bf16[16,2304]{1,0:T(8,128)(2,1)S(1)}, bf16[16,2304]{1,0:T(8,128)(2,1)S(1)}, u32[]{:S(2)}, u32[]{:S(2)}) collective-permute-start(bf16[16,2304]{1,0:T(8,128)(2,1)S(1)} %reshape.25), channel_id=1, source_target_pairs={{0,2},{1,3},{2,0},{3,1},{4,6},{5,7},{6,4},{7,5},{8,10},{9,11},{10,... | collective-permute-start | bytes 221192 | tf_op jit(solution)/shard_map/ppermute | solution.py:32
  22.6 1.4 %collective-permute-start.4 = (bf16[32,2304]{1,0:T(8,128)(2,1)S(1)}, bf16[32,2304]{1,0:T(8,128)(2,1)S(1)}, u32[]{:S(2)}, u32[]{:S(2)}) collective-permute-start(bf16[32,2304]{1,0:T(8,128)(2,1)S(1)} %pad_maximum_fusion.1), channel_id=1, source_target_pairs={{0,1},{1,0},{2,3},{3,2},{4,5},{5,4},{6,7},{7,6},{8,9},{9,8},{10,11... | collective-permute-start | bytes 442376 | tf_op jit(solution)/shard_map/ppermute | solution.py:32
  24.0 3.0 %copy-start.2 = (bf16[2304,1536]{1,0:T(8,128)(2,1)S(1)}, bf16[2304,1536]{1,0:T(8,128)(2,1)}, u32[]{:S(2)}) copy-start(bf16[2304,1536]{1,0:T(8,128)(2,1)} %wq_ref.1) | copy-start | bytes 21233668
  29.3 32.2 %collective-permute-start.14 = (f32[4,8,1664]{2,1,0:T(8,128)S(1)}, f32[4,8,1664]{2,1,0:T(8,128)S(1)}, u32[]{:S(2)}, u32[]{:S(2)}) collective-permute-start(f32[4,8,1664]{2,1,0:T(8,128)S(1)} %get-tuple-element.23), channel_id=1, source_target_pairs={{0,4},{4,0},{8,12},{12,8},{16,20},{20,16},{24,28},{28,24},{1,5},{5... | collective-permute-start | bytes 638984 | tf_op jit(solution)/shard_map/ppermute | solution.py:32
  31.2 13.1 %copy-start = (bf16[2304,9216]{1,0:T(8,128)(2,1)S(1)}, bf16[2304,9216]{1,0:T(8,128)(2,1)}, u32[]{:S(2)}) copy-start(bf16[2304,9216]{1,0:T(8,128)(2,1)} %gate_ref.5) | copy-start | bytes 127401984
  50.6 39.0 %collective-permute-start.5 = (bf16[4,16,2304]{2,1,0:T(8,128)(2,1)S(1)}, bf16[4,16,2304]{2,1,0:T(8,128)(2,1)S(1)}, u32[]{:S(2)}, u32[]{:S(2)}) collective-permute-start(bf16[4,16,2304]{2,1,0:T(8,128)(2,1)S(1)} %get-tuple-element.17), channel_id=1, source_target_pairs={{0,4},{4,0},{8,12},{12,8},{16,20},{20,16},{24,28},{28,24},{1,5},{5... | collective-permute-start | bytes 884744 | tf_op jit(solution)/shard_map/ppermute | solution.py:32
  59.6 36.4 %collective-permute-start.11 = (bf16[4,16,3072]{2,1,0:T(8,128)(2,1)}, bf16[4,16,3072]{2,1,0:T(8,128)(2,1)}, u32[]{:S(2)}, u32[]{:S(2)}) collective-permute-start(bf16[4,16,3072]{2,1,0:T(8,128)(2,1)} %get-tuple-element.21), channel_id=1, source_target_pairs={{0,4},{4,0},{8,12},{12,8},{16,20},{20,16},{24,28},{28,24},{1,5},{5... | collective-permute-start | bytes 1179656 | tf_op jit(solution)/shard_map/ppermute | solution.py:32
  61.5 25.1 %collective-permute-start.15 = (f32[2,8,1664]{2,1,0:T(8,128)S(1)}, f32[2,8,1664]{2,1,0:T(8,128)S(1)}, u32[]{:S(2)}, u32[]{:S(2)}) collective-permute-start(f32[2,8,1664]{2,1,0:T(8,128)S(1)} %slice.161), channel_id=1, source_target_pairs={{0,8},{4,12},{8,0},{12,4},{16,24},{20,28},{24,16},{28,20},{1,9},{5... | collective-permute-start | bytes 319496 | tf_op jit(solution)/shard_map/ppermute | solution.py:32
  63.2 13.1 %copy-start.1 = (bf16[2304,9216]{1,0:T(8,128)(2,1)S(1)}, bf16[2304,9216]{1,0:T(8,128)(2,1)}, u32[]{:S(2)}) copy-start(bf16[2304,9216]{1,0:T(8,128)(2,1)} %gate_ref.5) | copy-start | bytes 127401984
  76.3 21.6 %copy-start.4 = (bf16[2,512,256]{2,1,0:T(8,128)(2,1)S(1)}, bf16[2,512,256]{2,1,0:T(8,128)(2,1)}, u32[]{:S(2)}) copy-start(bf16[2,512,256]{2,1,0:T(8,128)(2,1)} %k_ref.1) | copy-start | bytes 1572868
  76.3 21.6 %copy-start.5 = (bf16[2,512,256]{2,1,0:T(8,128)(2,1)S(1)}, bf16[2,512,256]{2,1,0:T(8,128)(2,1)}, u32[]{:S(2)}) copy-start(bf16[2,512,256]{2,1,0:T(8,128)(2,1)} %v_ref.1) | copy-start | bytes 1572868
  76.3 21.6 %copy-start.6 = (s32[2]{0:T(128)S(1)}, s32[2]{0:T(128)}, u32[]{:S(2)}) copy-start(s32[2]{0:T(128)} %lengths_ref.1) | copy-start | bytes 28
  86.1 17.5 %collective-permute-start.8 = (bf16[4,16,3840]{2,1,0:T(8,128)(2,1)S(1)}, bf16[4,16,3840]{2,1,0:T(8,128)(2,1)}, u32[]{:S(2)}, u32[]{:S(2)}) collective-permute-start(bf16[4,16,3840]{2,1,0:T(8,128)(2,1)S(1)} %get-tuple-element.19), channel_id=1, source_target_pairs={{0,4},{4,0},{8,12},{12,8},{16,20},{20,16},{24,28},{28,24},{1,5},{5... | collective-permute-start | bytes 1474568 | tf_op jit(solution)/shard_map/ppermute | solution.py:32
  86.7 5.3 %collective-permute-start.16 = (f32[1,8,1664]{2,1,0:T(8,128)S(1)}, f32[1,8,1664]{2,1,0:T(8,128)S(1)}, u32[]{:S(2)}, u32[]{:S(2)}) collective-permute-start(f32[1,8,1664]{2,1,0:T(8,128)S(1)} %slice.185), channel_id=1, source_target_pairs={{0,16},{4,20},{8,24},{12,28},{16,0},{20,4},{24,8},{28,12},{1,17},{... | collective-permute-start | bytes 159752 | tf_op jit(solution)/shard_map/ppermute | solution.py:32
  90.5 9.5 %collective-permute-start.6 = (bf16[2,16,2304]{2,1,0:T(8,128)(2,1)S(1)}, bf16[2,16,2304]{2,1,0:T(8,128)(2,1)}, u32[]{:S(2)}, u32[]{:S(2)}) collective-permute-start(bf16[2,16,2304]{2,1,0:T(8,128)(2,1)S(1)} %slice.137), channel_id=1, source_target_pairs={{0,8},{4,12},{8,0},{12,4},{16,24},{20,28},{24,16},{28,20},{1,9},{5... | collective-permute-start | bytes 442376 | tf_op jit(solution)/shard_map/ppermute | solution.py:32
  92.0 3.8 %collective-permute-start.17 = (bf16[2,1,2,1664]{3,2,1,0:T(2,128)(2,1)S(1)}, bf16[2,1,2,1664]{3,2,1,0:T(2,128)(2,1)S(1)}, u32[]{:S(2)}, u32[]{:S(2)}) collective-permute-start(bf16[2,1,2,1664]{3,2,1,0:T(2,128)(2,1)S(1)} %slice.167), channel_id=1, source_target_pairs={{0,2},{1,3},{2,0},{3,1},{4,6},{5,7},{6,4},{7,5},{8,10},{9,11},{10,... | collective-permute-start | bytes 39944 | tf_op jit(solution)/shard_map/ppermute | solution.py:32
  95.9 1.9 %collective-permute-start.18 = (bf16[1,2,2,1664]{3,2,1,0:T(2,128)(2,1)S(1)}, bf16[1,2,2,1664]{3,2,1,0:T(2,128)(2,1)S(1)}, u32[]{:S(2)}, u32[]{:S(2)}) collective-permute-start(bf16[1,2,2,1664]{3,2,1,0:T(2,128)(2,1)S(1)} %get-tuple-element.35), channel_id=1, source_target_pairs={{0,1},{1,0},{2,3},{3,2},{4,5},{5,4},{6,7},{7,6},{8,9},{9,8},{10,11... | collective-permute-start | bytes 39944 | tf_op jit(solution)/shard_map/ppermute | solution.py:32
  97.1 9.7 %collective-permute-start.12 = (bf16[2,16,3072]{2,1,0:T(8,128)(2,1)S(1)}, bf16[2,16,3072]{2,1,0:T(8,128)(2,1)S(1)}, u32[]{:S(2)}, u32[]{:S(2)}) collective-permute-start(bf16[2,16,3072]{2,1,0:T(8,128)(2,1)S(1)} %slice.153), channel_id=1, source_target_pairs={{0,8},{4,12},{8,0},{12,4},{16,24},{20,28},{24,16},{28,20},{1,9},{5... | collective-permute-start | bytes 589832 | tf_op jit(solution)/shard_map/ppermute | solution.py:32
  101.0 5.7 %collective-permute-start.7 = (bf16[1,16,2304]{2,1,0:T(8,128)(2,1)S(1)}, bf16[1,16,2304]{2,1,0:T(8,128)(2,1)S(1)}, u32[]{:S(2)}, u32[]{:S(2)}) collective-permute-start(bf16[1,16,2304]{2,1,0:T(8,128)(2,1)S(1)} %slice.235), channel_id=1, source_target_pairs={{0,16},{4,20},{8,24},{12,28},{16,0},{20,4},{24,8},{28,12},{1,17},{... | collective-permute-start | bytes 221192 | tf_op jit(solution)/shard_map/ppermute | solution.py:32
  104.7 10.2 %collective-permute-start.9 = (bf16[2,16,3840]{2,1,0:T(8,128)(2,1)S(1)}, bf16[2,16,3840]{2,1,0:T(8,128)(2,1)S(1)}, u32[]{:S(2)}, u32[]{:S(2)}) collective-permute-start(bf16[2,16,3840]{2,1,0:T(8,128)(2,1)S(1)} %slice.145), channel_id=1, source_target_pairs={{0,8},{4,12},{8,0},{12,4},{16,24},{20,28},{24,16},{28,20},{1,9},{5... | collective-permute-start | bytes 737288 | tf_op jit(solution)/shard_map/ppermute | solution.py:32
  106.9 7.4 %collective-permute-start.13 = (bf16[1,16,3072]{2,1,0:T(8,128)(2,1)S(1)}, bf16[1,16,3072]{2,1,0:T(8,128)(2,1)S(1)}, u32[]{:S(2)}, u32[]{:S(2)}) collective-permute-start(bf16[1,16,3072]{2,1,0:T(8,128)(2,1)S(1)} %slice.234), channel_id=1, source_target_pairs={{0,16},{4,20},{8,24},{12,28},{16,0},{20,4},{24,8},{28,12},{1,17},{... | collective-permute-start | bytes 294920 | tf_op jit(solution)/shard_map/ppermute | solution.py:32
  115.0 8.5 %collective-permute-start.10 = (bf16[1,16,3840]{2,1,0:T(8,128)(2,1)S(1)}, bf16[1,16,3840]{2,1,0:T(8,128)(2,1)S(1)}, u32[]{:S(2)}, u32[]{:S(2)}) collective-permute-start(bf16[1,16,3840]{2,1,0:T(8,128)(2,1)S(1)} %slice.233), channel_id=1, source_target_pairs={{0,16},{4,20},{8,24},{12,28},{16,0},{20,4},{24,8},{28,12},{1,17},{... | collective-permute-start | bytes 368648 | tf_op jit(solution)/shard_map/ppermute | solution.py:32

commit v2 on v1

v2 whole, which is shorter than its diff:
```python
import functools

import jax
import jax.numpy as jnp
from jax import lax
from jax.experimental import pallas as pl
from jax.experimental.pallas import tpu as pltpu
from jax.sharding import PartitionSpec as P

HEADS = 24
DH = 256
EPS = 1e-05
PORTIONS = ((1, 4), (5,), (2,))
TILE = 768
AHEAD = 1
SLOTS = 3

BF16 = jnp.bfloat16
F32 = jnp.float32
VMEM = pl.BlockSpec(memory_space=pltpu.VMEM)
HBM = pl.BlockSpec(memory_space=pltpu.HBM)
ANY = pl.BlockSpec(memory_space=pl.ANY)
SMEM = pl.BlockSpec(memory_space=pltpu.SMEM)


def shape(dims, dtype):
    return jax.ShapeDtypeStruct(tuple(dims), dtype)


def matmul(a, b):
    return jnp.dot(a, b, preferred_element_type=F32)


def in_hbm(x):
    return pltpu.with_memory_space_constraint(x, pltpu.HBM)


def in_vmem(x):
    return pltpu.with_memory_space_constraint(x, pltpu.VMEM)


def swap(x, axis, bit):
    size = lax.axis_size(axis)
    return lax.ppermute(x, axis, [(i, i ^ bit) for i in range(size)])


def bits_of(size):
    return [1 << t for t in range(size.bit_length() - 1)]


def norm_kernel(blocks, x_hbm, gain_hbm, keep_ref, send_ref, x_ref, gain_ref, sems):
    copies = [
        pltpu.make_async_copy(source, target, sems.at[i])
        for i, (source, target) in enumerate(((x_hbm, x_ref), (gain_hbm, gain_ref)))
    ]
    for copy in copies:
        copy.start()
    copies[0].wait()
    values = x_ref[...].astype(F32)
    width = values.shape[1]
    mean = jnp.sum(values, axis=1, keepdims=True) / width
    centred = values - mean
    variance = jnp.sum(centred * centred, axis=1, keepdims=True) / width
    root = jnp.sqrt(variance + EPS)
    part = width // blocks
    copies[1].wait()
    for k in range(blocks):
        start = pl.multiple_of((lax.axis_index("gx") ^ k) * part, 128)
        piece = x_ref[:, pl.ds(start, part)].astype(F32)
        normed = ((piece - mean) / root * gain_ref[:, pl.ds(start, part)]).astype(BF16)
        (send_ref if k % 2 else keep_ref)[k // 2, 0] = normed


def normalise(stream, norm_gain, blocks):
    rows, width = stream.shape
    out = shape((blocks // 2, 1, rows, width // blocks), BF16)
    return pl.pallas_call(
        functools.partial(norm_kernel, blocks),
        out_shape=(out, out),
        in_specs=[HBM, HBM],
        out_specs=(VMEM, VMEM),
        scratch_shapes=[
            pltpu.VMEM((rows, width), BF16),
            pltpu.VMEM((1, width), F32),
            pltpu.SemaphoreType.DMA((2,)),
        ],
        cost_estimate=pl.CostEstimate(flops=20 * 10**9, bytes_accessed=10**6, transcendentals=0),
        compiler_params=pltpu.CompilerParams(vmem_limit_bytes=2 << 20),
        name="layer_norm",
    )(in_hbm(stream), in_hbm(norm_gain.reshape(1, width)))


def join_kernel(sent, keep_ref, arrived_ref, *outs):
    slots, count = keep_ref.shape[:2]
    if slots == 1:
        pieces = [ref[0, i].astype(F32) for ref in (keep_ref, arrived_ref) for i in range(count)]
        outs[0][...] = jnp.concatenate(pieces, axis=0).astype(BF16)
        return
    send_out, keep_out = outs
    places = [0, 0]
    for s in range(slots):
        way = s in sent
        out = send_out if way else keep_out
        for i in range(count):
            out[places[way], i] = keep_ref[s, i]
            out[places[way], count + i] = arrived_ref[s, i]
        places[way] += 1


def join(keep, arrived, sent):
    slots, count, rows, cols = keep.shape
    if slots == 1:
        out_shape = (shape((2 * count * rows, cols), BF16),)
    else:
        out_shape = (shape((slots // 2, 2 * count, rows, cols), BF16),) * 2
    return pl.pallas_call(
        functools.partial(join_kernel, tuple(sent)),
        out_shape=out_shape,
        in_specs=[VMEM, VMEM],
        out_specs=(VMEM,) * len(out_shape),
        compiler_params=pltpu.CompilerParams(vmem_limit_bytes=2 << 20),
        name="join_%d_%d" % (slots, cols),
    )(keep, arrived)


def split(value):
    high = value.astype(BF16).astype(F32)
    return jnp.concatenate([high, value - high], axis=0).astype(BF16)


def heads_part(slots, order, x_ref, wq_ref, wkv_ref, x_out, send_ref, keep_ref):
    total = x_ref.shape[0]
    groups = len(order)
    per = total // (groups * slots)
    row = lax.broadcasted_iota(jnp.int32, (total, total), 0)
    col = lax.broadcasted_iota(jnp.int32, (total, total), 1)
    base = (row // (per * groups)) * per + row % per
    slot = (row // per) % groups
    x = x_ref[...]

    def placed(want):
        source = jnp.zeros_like(row)
        for position, j in enumerate(order):
            source = jnp.where(want == j, position * (slots * per) + base, source)
        return matmul((col == source).astype(BF16), x).astype(BF16)

    x_out[...] = placed(slot ^ lax.axis_index("gy"))
    relative = placed(slot)
    both = groups * per
    at = 0
    for w_ref in (wq_ref, wkv_ref):
        lanes = slice(at, at + w_ref.shape[1])
        part = matmul(relative, w_ref[...])
        for k in range(slots):
            mine = part[k * both : (k + 1) * both]
            if k % 2:
                send_ref[k // 2, :, lanes] = split(mine)
            else:
                keep_ref[k // 2, :, lanes] = jnp.concatenate([mine, jnp.zeros_like(mine)], axis=0)
        at += w_ref.shape[1]
    return at


def fetch_kernel(first, w_ref, after_ref, out_ref, sem):
    copy = pltpu.make_async_copy(w_ref.at[:, pl.ds(first, out_ref.shape[1])], out_ref, sem)
    copy.start()
    copy.wait()


def fetch(weights, first, cols, after):
    depth = weights.shape[0]
    return pl.pallas_call(
        functools.partial(fetch_kernel, first),
        out_shape=pltpu.VMEM((depth, cols), BF16),
        in_specs=[HBM, ANY],
        out_specs=VMEM,
        scratch_shapes=[pltpu.SemaphoreType.DMA],
        cost_estimate=pl.CostEstimate(flops=0, bytes_accessed=2 * depth * cols, transcendentals=0),
        compiler_params=pltpu.CompilerParams(vmem_limit_bytes=1 << 20),
        name="fetch_%d" % first,
    )(in_hbm(weights), after)


def partials_kernel(slots, first, count, tile, ready, order, *refs):
    x_ref, gate_ref, up_ref = refs[:3]
    resident = []
    for piece in refs[3 : 3 + ready]:
        resident += [piece.at[:, pl.ds(i * tile, tile)] for i in range(piece.shape[1] // tile)]
    held, gates, sems = refs[-3:]
    rest = refs[3 + ready : -3]
    rows = x_ref.shape[0] // slots
    room = held.shape[0]
    sources = []
    for step in range(count):
        columns = pl.ds((first + step) * tile, tile)
        if step >= len(resident):
            sources.append(gate_ref.at[:, columns])
        sources.append(up_ref.at[:, columns])
    copies = [pltpu.make_async_copy(source, held.at[i % room], sems.at[i % room]) for i, source in enumerate(sources)]
    for copy in copies[:room]:
        copy.start()
    if order is None:
        send_ref, keep_ref = rest[-2:]
        base = 0
        x = x_ref[...]
    else:
        wq_ref, wkv_ref = rest[:2]
        x_out, send_ref, keep_ref = rest[-3:]
        base = heads_part(slots, order, x_ref, wq_ref, wkv_ref, x_out, send_ref, keep_ref)
        x = x_out[...]
    at = 0

    def from_stream():
        nonlocal at
        copies[at].wait()
        out = matmul(x, held[at % room])
        if at + room < len(copies):
            copies[at + room].start()
        at += 1
        return out

    if resident:
        gates[0] = matmul(x, resident[0][...])
    for step in range(count):
        if step + 1 < len(resident):
            gates[(step + 1) % 2] = matmul(x, resident[step + 1][...])
        gate = gates[step % 2] if step < len(resident) else from_stream()
        up = from_stream()
        lanes = slice(base + step * tile, base + (step + 1) * tile)
        for k in range(slots):
            mine = slice(k * rows, (k + 1) * rows)
            both = jnp.concatenate([gate[mine], up[mine]], axis=0)
            ref = send_ref if k % 2 else keep_ref
            ref[k // 2, :, lanes] = both.astype(ref.dtype)


def partials(x, w_gate, w_up, pieces, slots, tile, first, count, heads=(), order=None, after=()):
    total, depth = x.shape
    cols = count * tile + sum(w.shape[1] for w in heads)
    out_shape = [shape(x.shape, BF16)] if heads else []
    dims = (slots // 2, 2 * total // slots, cols)
    out_shape += [shape(dims, BF16), shape(dims, F32)]
    room = max(1, min(SLOTS, 2 * count - sum(p.shape[1] for p in pieces) // tile))
    return pl.pallas_call(
        functools.partial(partials_kernel, slots, first, count, tile, len(pieces), order),
        out_shape=tuple(out_shape),
        in_specs=[VMEM, HBM, HBM] + [VMEM] * (len(pieces) + len(heads)) + [ANY] * len(after),
        out_specs=(VMEM,) * len(out_shape),
        scratch_shapes=[
            pltpu.VMEM((room, depth, tile), BF16),
            pltpu.VMEM((2, total, tile), F32),
            pltpu.SemaphoreType.DMA((room,)),
        ],
        cost_estimate=pl.CostEstimate(
            flops=4 * total * depth * cols, bytes_accessed=4 * depth * cols, transcendentals=0
        ),
        compiler_params=pltpu.CompilerParams(vmem_limit_bytes=2 * room * depth * tile + (3 << 20)),
        name="partials_%d" % first,
    )(x, in_hbm(w_gate), in_hbm(w_up), *[in_vmem(w) for w in (*pieces, *heads)], *after)


def combine_kernel(wide, count, *refs):
    send_ref, keep_ref = refs[-2:]
    at = 0
    for keep, arrived in zip(refs[: 2 * count : 2], refs[1 : 2 * count : 2]):
        for s in range(keep.shape[0]):
            both = keep[s] + arrived[s].astype(F32)
            lanes = slice(at, at + keep.shape[2])
            if s % 2 == 0:
                keep_ref[s // 2, :, lanes] = both
                continue
            send_ref[s // 2, :, lanes] = both.astype(BF16)
            if at == 0 and wide:
                rows = both.shape[0] // 2
                send_ref[s // 2, :, :wide] = split(both[:rows, :wide] + both[rows:, :wide])
        at += keep.shape[2]


def combine(parts, wide, after=()):
    slots, rows, _ = parts[0][0].shape
    cols = sum(keep.shape[2] for keep, _ in parts)
    dims = (slots // 2, rows, cols)
    return pl.pallas_call(
        functools.partial(combine_kernel, wide, len(parts)),
        out_shape=(shape(dims, BF16), shape(dims, F32)),
        in_specs=[VMEM] * (2 * len(parts)) + [ANY] * len(after),
        out_specs=(VMEM, VMEM),
        compiler_params=pltpu.CompilerParams(vmem_limit_bytes=2 << 20),
        name="combine_%d" % cols,
    )(*[a for part in parts for a in part], *after)


def finish_kernel(wide, keep_ref, arrived_ref, *refs):
    both = keep_ref[0] + arrived_ref[0].astype(F32)
    rows = both.shape[0] // 2
    if wide:
        earlier, (send_ref, own_ref, hidden_ref) = refs[:-3], refs[-3:]
        middle, _, per, _ = own_ref.shape
        heads = both[:rows, :wide] + both[rows:, :wide]
        for j in range(2 * middle):
            piece = heads[j * per : (j + 1) * per].astype(BF16)
            (own_ref if j < middle else send_ref)[j % middle, 0] = piece
    else:
        earlier, hidden_ref = refs[:-1], refs[-1]
    at = 0
    for ref in earlier:
        hidden_ref[:, at : at + ref.shape[1]] = ref[...]
        at += ref.shape[1]
    gate, up = both[:rows, wide:], both[rows:, wide:]
    hidden_ref[:, at:] = (gate * (1.0 / (1.0 + jnp.exp(-gate))) * up).astype(BF16)


def finish(keep, arrived, wide, groups, earlier):
    _, rows, cols = keep.shape
    out = [shape((rows // 2, cols - wide + sum(e.shape[1] for e in earlier)), BF16)]
    if wide:
        out = [shape((groups // 2, 1, rows // 2 // groups, wide), BF16)] * 2 + out
    return pl.pallas_call(
        functools.partial(finish_kernel, wide),
        out_shape=tuple(out),
        in_specs=[VMEM] * (2 + len(earlier)),
        out_specs=(VMEM,) * len(out),
        compiler_params=pltpu.CompilerParams(vmem_limit_bytes=4 << 20),
        name="finish_%d" % cols,
    )(keep, arrived, *earlier)


def attention_kernel(order, lengths_ref, own_ref, arrived_ref, k_ref, v_ref, out_ref, q_ref, pieces_ref):
    rows, cache, _ = k_ref.shape
    groups = len(order)
    keyval_cols = 2 * DH // groups
    query_cols = own_ref.shape[3] - keyval_cols
    per = query_cols // DH
    heads = groups * per
    scale = DH ** (-0.5)
    for i in range(groups // 2):
        pieces_ref[i] = own_ref[0, i].astype(F32)
        pieces_ref[groups // 2 + i] = arrived_ref[0, i].astype(F32)
    contexts = []
    for b in range(rows):
        halves = []
        for g in range(groups):
            slot = lax.axis_index("gy") ^ g
            position = jnp.int32(0)
            for p, j in enumerate(order):
                position = jnp.where(slot == j, p, position)
            piece = pieces_ref[position][b : b + 1]
            for h in range(per):
                q_ref[g * per + h : g * per + h + 1] = piece[:, h * DH : (h + 1) * DH]
            halves.append(piece[:, query_cols:])
        keyval = jnp.concatenate(halves, axis=1)
        new_key, new_value = keyval[:, :DH], keyval[:, DH:]
        query = q_ref[...]
        scores = lax.dot_general(
            query.astype(BF16), k_ref[b], (((1,), (1,)), ((), ())), preferred_element_type=F32
        ) * scale
        score_new = jnp.sum(query * new_key, axis=1, keepdims=True) * scale
        mask = lax.broadcasted_iota(jnp.int32, (heads, cache), 1) < lengths_ref[b]
        top = jnp.maximum(jnp.max(jnp.where(mask, scores, -1e30), axis=1, keepdims=True), score_new)
        exponent = jnp.where(mask, jnp.exp(scores - top), 0.0)
        exponent_new = jnp.exp(score_new - top)
        total = jnp.sum(exponent, axis=1, keepdims=True) + exponent_new
        weights = (exponent / total).astype(BF16)
        weights_new = (exponent_new / total).astype(BF16).astype(F32)
        contexts.append(matmul(weights, v_ref[b]) + weights_new * new_value)
    for h in range(heads):
        both = jnp.concatenate([c[h : h + 1] for c in contexts], axis=0)
        out_ref[:, h * DH : (h + 1) * DH] = both.astype(BF16)


def attention(own, arrived, k_cache, v_cache, lengths, order):
    rows, cache, _ = k_cache.shape
    return pl.pallas_call(
        functools.partial(attention_kernel, order),
        out_shape=shape((rows, HEADS * DH), BF16),
        in_specs=[SMEM, VMEM, VMEM, VMEM, VMEM],
        out_specs=VMEM,
        scratch_shapes=[pltpu.VMEM((HEADS, DH), F32), pltpu.VMEM((len(order), rows, own.shape[3]), F32)],
        cost_estimate=pl.CostEstimate(
            flops=4 * rows * HEADS * cache * DH, bytes_accessed=4 * rows * cache * DH, transcendentals=0
        ),
        compiler_params=pltpu.CompilerParams(vmem_limit_bytes=6 << 20),
        name="attention",
    )(lengths, own, arrived, k_cache, v_cache)


def body(stream, norm_gain, w_gate, w_up, w_query, w_keyval, k_cache, v_cache, lengths):
    size, groups = lax.axis_size("gx"), lax.axis_size("gy")
    ff = w_gate.shape[1]
    wide = w_query.shape[1] + w_keyval.shape[1]
    tile = max(t for t in range(128, TILE + 1, 128) if ff % t == 0)
    blocks = ff // tile
    flat = [p for group in PORTIONS for p in group]
    edges = [round(blocks * sum(flat[:i]) / sum(flat)) for i in range(len(flat) + 1)]

    pieces = [[] for _ in flat]

    def swap_and_fetch(send, keep, axis, bit):
        arrived = swap(send, axis, bit)
        taken = [sum(p.shape[1] for p in held) // tile for held in pieces]
        left = [edges[i + 1] - edges[i] - taken[i] for i in range(len(flat))]
        portion = max(range(len(flat)), key=lambda i: left[i])
        count = min(AHEAD, left[portion])
        if count:
            piece = fetch(w_gate, (edges[portion] + taken[portion]) * tile, count * tile, send)
            piece, keep = lax.optimization_barrier((piece, keep))
            pieces[portion].append(piece)
        return keep, arrived

    bits = bits_of(size)
    keep, send = normalise(stream, norm_gain, size)
    for bit in bits[:-1]:
        keep, arrived = swap_and_fetch(send, keep, "gx", bit)
        send, keep = join(keep, arrived, range(1, keep.shape[0], 2))
    keep, arrived = swap_and_fetch(send, keep, "gx", bits[-1])
    (x,) = join(keep, arrived, ())
    order = [0]
    for bit in bits_of(groups)[::-1]:
        keep, arrived = swap_and_fetch(x, x, "gy", bit)
        x = jnp.concatenate([keep, arrived], axis=0)
        order = order + [j ^ bit for j in order]

    parts = []
    for i in range(len(flat)):
        first, count = edges[i], edges[i + 1] - edges[i]
        if i == 0:
            heads = (w_query, w_keyval)
            x, send, keep = partials(x, w_gate, w_up, pieces[i], size, tile, first, count, heads, tuple(order))
        else:
            after = (parts[i - 2][1],) if i > 1 else ()
            send, keep = partials(x, w_gate, w_up, pieces[i], size, tile, first, count, after=after)
        parts.append((keep, swap(send, "gx", bits[0])))

    hidden = []
    context = None
    at = 0
    for number, group in enumerate(PORTIONS):
        columns = 0 if number else wide
        here = parts[at : at + len(group)]
        at += len(group)
        after = (parts[at][0],) if at < len(flat) else ()
        for bit in bits[1:]:
            send, keep = combine(here, columns, after)
            after = ()
            here = [(keep, swap(send, "gx", bit))]
        *heads, part = finish(*here[0], columns, groups, hidden if at == len(flat) else [])
        hidden.append(part)
        if number:
            continue
        send, keep = heads
        for bit in bits_of(groups)[:0:-1]:
            send, keep = join(keep, swap(send, "gy", bit), range(keep.shape[0] // 2, keep.shape[0]))
        context = attention(keep, swap(send, "gy", 1), k_cache, v_cache, lengths, tuple(order))
    return hidden[-1], context


def solution(mesh):
    return jax.shard_map(
        body,
        mesh=mesh,
        in_specs=(
            P(("gx", "gy"), None),
            P(),
            P("gx", "gy"),
            P("gx", "gy"),
            P("gx", "gy"),
            P("gx", "gy"),
            P(("gx", "gy"), None, None),
            P(("gx", "gy"), None, None),
            P(("gx", "gy")),
        ),
        out_specs=(P("gx", "gy"), P(("gx", "gy"), None)),
        check_vma=False,
    )
```

time: 125 us -> 85.7 us (0.69)
  local copies, waits for them, and re-layouts: 31.3 us -> 0.85 us
  waiting for transfers between devices: 23.9 us -> 9.36 us
  Pallas kernels: 30.2 us -> 43.4 us
  other arithmetic: 5.62 us -> 0.02 us
  starting transfers between devices: 32.3 us -> 30.8 us
    unnamed x19 -> x13, local copies, waits for them, and re-layouts: 31 us -> 0.84 us
    ppermute x19 -> x17, waiting for transfers between devices: 23.9 us -> 9.36 us  [swap(): return lax.ppermute(x, axis, [(i, i ^ bit) for i in range(size)])]
    pallas_call x4 -> x22, Pallas kernels: 27 us -> 39.9 us  [the longest x4 28.2 us: partials(): pl.pallas_call(functools.partial(partials_kernel, slots, first, count, ti...]
    another operation x4 -> x0, other arithmetic: 3.19 us -> none
    ppermute x19 -> x17, starting transfers between devices: 32.3 us -> 30.8 us  [swap(): return lax.ppermute(x, axis, [(i, i ^ bit) for i in range(size)])]
    add x8 -> x0, other arithmetic: 1.25 us -> none  [scatter_sum(): keep = keep + swap(send, 'gx', bit).astype(F32)]
  transfers between devices with their start and end apart: 19 -> 17, of which waited for: 10 -> 7; matrix products, arithmetic and copies ran while one was open for 4% -> 0% of each run, Pallas kernels for 22% -> 44%
where the time goes in v2:
time: 85.7 us; the launch traced here: 85.3 us
  Pallas kernels  43.4 us (51%)
  starting transfers between devices  30.8 us (36%)
  waiting for transfers between devices  9.36 us (11%)
  between operations  0.88 us (1%)
    ppermute x17, starting transfers between devices, swap(): return lax.ppermute(x, axis, [(i, i ^ bit) for i in range(size)])  30.8 us
    pallas_call x4, Pallas kernels, partials(): pl.pallas_call(functools.partial(partials_kernel, slots, first, count, ti...  28.2 us
    pallas_call x5, Pallas kernels, fetch(): pl.pallas_call(functools.partial(fetch_kernel, first), out_shape=pltpu.VM...  10.3 us
    ppermute x17, waiting for transfers between devices, swap(): return lax.ppermute(x, axis, [(i, i ^ bit) for i in range(size)])  9.36 us
    pallas_call x1, Pallas kernels, attention(): pl.pallas_call(functools.partial(attention_kernel, order), out_shape=shap...  2.09 us
  transfers between devices with their start and end apart: 17, of which 7 were waited for; matrix products, arithmetic and copies ran while one was open for 0% of the time, Pallas kernels for 44%

profile of v2, /device:TPU:0, one launch (start us, length us, event | category | flops | bytes accessed | tf_op | source)
XLA Modules:
  0.0 85.3 jit_solution(6773205066992207364)
XLA Ops:
  0.6 1.5 %layer_norm.1 = (bf16[4,1,2,2304]{3,2,1,0:T(2,128)(2,1)S(1)}, bf16[4,1,2,2304]{3,2,1,0:T(2,128)(2,1)S(1)}) custom-call(bf16[2,18432]{1,0:T(2,128)(2,1)} %x_hbm.1, f32[1,18432]{1,0:T(1,128)} %bitcast.3), custom_call_target="tpu_custom_call" | custom-call | flops 20000000000 | bytes 1000000 | tf_op jit(solution)/shard_map/layer_norm/pallas_call | solution.py:77
  2.1 3.0 %collective-permute-start = (bf16[4,1,2,2304]{3,2,1,0:T(2,128)(2,1)S(1)}, bf16[4,1,2,2304]{3,2,1,0:T(2,128)(2,1)S(1)}, u32[]{:S(2)}, u32[]{:S(2)}) collective-permute-start(bf16[4,1,2,2304]{3,2,1,0:T(2,128)(2,1)S(1)} %get-tuple-element.44.after_ref), channel_id=1, source_target_pairs={{0,4},{4,0},{8,12},{12,8},{16,20},{20,16},{24,28},{28,24},{1,5},{5... | collective-permute-start | bytes 110600 | tf_op jit(solution)/shard_map/ppermute | solution.py:44
  5.2 2.0 %fetch_3840.1.refs_3_ = bf16[2304,768]{1,0:T(8,128)(2,1)S(1)} custom-call(bf16[2304,9216]{1,0:T(8,128)(2,1)} %refs_1_.7, bf16[4,1,2,2304]{3,2,1,0:T(2,128)(2,1)S(1)} %get-tuple-element.44.after_ref), custom_call_target="tpu_custom_call" | custom-call | bytes 3538944 | tf_op jit(solution)/shard_map/fetch_3840/pallas_call | solution.py:172
  7.2 0.0 collective-permute-done.arrived_ref
  7.2 2.0 %collective-permute-start.1 = (bf16[2,2,2,2304]{3,2,1,0:T(2,128)(2,1)S(1)}, bf16[2,2,2,2304]{3,2,1,0:T(2,128)(2,1)S(1)}, u32[]{:S(2)}, u32[]{:S(2)}) collective-permute-start(bf16[2,2,2,2304]{3,2,1,0:T(2,128)(2,1)S(1)} %get-tuple-element.47.after_ref), channel_id=1, source_target_pairs={{0,8},{4,12},{8,0},{12,4},{16,24},{20,28},{24,16},{28,20},{1,9},{5... | collective-permute-start | bytes 110600 | tf_op jit(solution)/shard_map/ppermute | solution.py:44
  9.2 2.0 %fetch_768.1.refs_3_ = bf16[2304,768]{1,0:T(8,128)(2,1)S(1)} custom-call(bf16[2304,9216]{1,0:T(8,128)(2,1)} %refs_1_.7, bf16[2,2,2,2304]{3,2,1,0:T(2,128)(2,1)S(1)} %get-tuple-element.47.after_ref), custom_call_target="tpu_custom_call" | custom-call | bytes 3538944 | tf_op jit(solution)/shard_map/fetch_768/pallas_call | solution.py:172
  11.3 0.0 collective-permute-done.1.arrived_ref
  11.3 3.0 %collective-permute-start.2 = (bf16[1,4,2,2304]{3,2,1,0:T(2,128)(2,1)S(1)}, bf16[1,4,2,2304]{3,2,1,0:T(2,128)(2,1)S(1)}, u32[]{:S(2)}, u32[]{:S(2)}) collective-permute-start(bf16[1,4,2,2304]{3,2,1,0:T(2,128)(2,1)S(1)} %get-tuple-element.50.after_ref), channel_id=1, source_target_pairs={{0,16},{4,20},{8,24},{12,28},{16,0},{20,4},{24,8},{28,12},{1,17},{... | collective-permute-start | bytes 110600 | tf_op jit(solution)/shard_map/ppermute | solution.py:44
  14.3 2.0 %fetch_4608.1.refs_4_ = bf16[2304,768]{1,0:T(8,128)(2,1)S(1)} custom-call(bf16[2304,9216]{1,0:T(8,128)(2,1)} %refs_1_.7, bf16[1,4,2,2304]{3,2,1,0:T(2,128)(2,1)S(1)} %get-tuple-element.50.after_ref), custom_call_target="tpu_custom_call" | custom-call | bytes 3538944 | tf_op jit(solution)/shard_map/fetch_4608/pallas_call | solution.py:172
  16.3 0.0 collective-permute-done.2.arrived_ref
  16.3 0.1 join_1_2304.1.after_ref
  16.4 1.8 %collective-permute-start.3 = (bf16[16,2304]{1,0:T(8,128)(2,1)S(1)}, bf16[16,2304]{1,0:T(8,128)(2,1)S(1)}, u32[]{:S(2)}, u32[]{:S(2)}) collective-permute-start(bf16[16,2304]{1,0:T(8,128)(2,1)S(1)} %join_1_2304.1.after_ref), channel_id=1, source_target_pairs={{0,2},{1,3},{2,0},{3,1},{4,6},{5,7},{6,4},{7,5},{8,10},{9,11},{10,... | collective-permute-start | bytes 221192 | tf_op jit(solution)/shard_map/ppermute | solution.py:44
  18.2 0.0 slice-start
  18.2 2.2 %fetch_1536.1.refs_4_ = bf16[2304,768]{1,0:T(8,128)(2,1)S(1)} custom-call(bf16[2304,9216]{1,0:T(8,128)(2,1)} %refs_1_.7, bf16[16,2304]{1,0:T(8,128)(2,1)S(1)} %join_1_2304.1.after_ref), custom_call_target="tpu_custom_call" | custom-call | bytes 3538944 | tf_op jit(solution)/shard_map/fetch_1536/pallas_call | solution.py:172
  20.4 0.4 collective-permute-done.3
  20.8 0.0 slice-start.1
  20.8 0.0 copy-start
  20.8 0.1 collective-permute-start.4
  20.9 2.2 %fetch_5376.1.refs_5_ = bf16[2304,768]{1,0:T(8,128)(2,1)S(1)} custom-call(bf16[2304,9216]{1,0:T(8,128)(2,1)} %refs_1_.7, bf16[32,2304]{1,0:T(8,128)(2,1)S(1)} %constant_dynamic-update-slice_fusion.after_ref), custom_call_target="tpu_custom_call" | custom-call | bytes 3538944 | tf_op jit(solution)/shard_map/fetch_5376/pallas_call | solution.py:172
  23.1 0.0 collective-permute-done.4
  23.1 0.0 slice-done
  23.1 0.7 slice-done.1
  23.9 0.1 copy-done
  23.9 4.1 %partials_0.1 = (bf16[64,2304]{1,0:T(8,128)(2,1)S(1)}, bf16[4,16,2432]{2,1,0:T(8,128)(2,1)S(1)}, f32[4,16,2432]{2,1,0:T(8,128)S(1)}) custom-call(bf16[64,2304]{1,0:T(8,128)(2,1)S(1)} %pad_maximum_fusion.refs_0_, bf16[2304,9216]{1,0:T(8,128)(2,1)} %refs_1_.7, bf16[2304,9216]{1,0:T(8,128)(2,1)} %refs_2_.7, bf16[2304,1536]{1,0:T(8,128)(2,1)S(1)} %bitcast.2, ...), custom_call_target="tpu_custom_call" | custom-call | flops 1434451968 | bytes 22413312 | tf_op jit(solution)/shard_map/partials_0/pallas_call | solution.py:244
  28.0 1.8 %collective-permute-start.9 = (bf16[4,16,2432]{2,1,0:T(8,128)(2,1)S(1)}, bf16[4,16,2432]{2,1,0:T(8,128)(2,1)S(1)}, u32[]{:S(2)}, u32[]{:S(2)}) collective-permute-start(bf16[4,16,2432]{2,1,0:T(8,128)(2,1)S(1)} %get-tuple-element.66), channel_id=1, source_target_pairs={{0,4},{4,0},{8,12},{12,8},{16,20},{20,16},{24,28},{28,24},{1,5},{5... | collective-permute-start | bytes 933896 | tf_op jit(solution)/shard_map/ppermute | solution.py:44
  29.8 8.4 %partials_1.1 = (bf16[4,16,3072]{2,1,0:T(8,128)(2,1)S(1)}, f32[4,16,3072]{2,1,0:T(8,128)S(1)}) custom-call(bf16[64,2304]{1,0:T(8,128)(2,1)S(1)} %get-tuple-element.55.refs_0_, bf16[2304,9216]{1,0:T(8,128)(2,1)} %refs_1_.7, bf16[2304,9216]{1,0:T(8,128)(2,1)} %refs_2_.7, bf16[2304,768]{1,0:T(8,128)(2,1)S(1)} %fetch_768.1.refs_3_, ...), custom_call_target="tpu_custom_call" | custom-call | flops 1811939328 | bytes 28311552 | tf_op jit(solution)/shard_map/partials_1/pallas_call | solution.py:244
  38.2 0.4 collective-permute-start.5
  38.6 0.0 collective-permute-done.9.refs_6_.refs_1_
  38.6 9.5 %partials_5.1 = (bf16[4,16,3840]{2,1,0:T(8,128)(2,1)S(1)}, f32[4,16,3840]{2,1,0:T(8,128)S(1)}) custom-call(bf16[64,2304]{1,0:T(8,128)(2,1)S(1)} %get-tuple-element.55.refs_0_, bf16[2304,9216]{1,0:T(8,128)(2,1)} %refs_1_.7, bf16[2304,9216]{1,0:T(8,128)(2,1)} %refs_2_.7, bf16[2304,768]{1,0:T(8,128)(2,1)S(1)} %fetch_3840.1.refs_3_, ...), custom_call_target="tpu_custom_call" | custom-call | flops 2264924160 | bytes 35389440 | tf_op jit(solution)/shard_map/partials_5/pallas_call | solution.py:244
  48.1 1.9 %collective-permute-start.12 = (bf16[4,16,3840]{2,1,0:T(8,128)(2,1)S(1)}, bf16[4,16,3840]{2,1,0:T(8,128)(2,1)S(1)}, u32[]{:S(2)}, u32[]{:S(2)}) collective-permute-start(bf16[4,16,3840]{2,1,0:T(8,128)(2,1)S(1)} %get-tuple-element.77), channel_id=1, source_target_pairs={{0,4},{4,0},{8,12},{12,8},{16,20},{20,16},{24,28},{28,24},{1,5},{5... | collective-permute-start | bytes 1474568 | tf_op jit(solution)/shard_map/ppermute | solution.py:44
  50.0 0.0 collective-permute-done.5.refs_3_
  50.0 0.1 combine_5504.2
  50.2 1.6 %collective-permute-start.10 = (bf16[2,16,5504]{2,1,0:T(8,128)(2,1)S(1)}, bf16[2,16,5504]{2,1,0:T(8,128)(2,1)S(1)}, u32[]{:S(2)}, u32[]{:S(2)}) collective-permute-start(bf16[2,16,5504]{2,1,0:T(8,128)(2,1)S(1)} %get-tuple-element.73), channel_id=1, source_target_pairs={{0,8},{4,12},{8,0},{12,4},{16,24},{20,28},{24,16},{28,20},{1,9},{5... | collective-permute-start | bytes 1056776 | tf_op jit(solution)/shard_map/ppermute | solution.py:44
  51.8 6.2 %partials_10.1 = (bf16[4,16,1536]{2,1,0:T(8,128)(2,1)S(1)}, f32[4,16,1536]{2,1,0:T(8,128)S(1)}) custom-call(bf16[64,2304]{1,0:T(8,128)(2,1)S(1)} %get-tuple-element.55.refs_0_, bf16[2304,9216]{1,0:T(8,128)(2,1)} %refs_1_.7, bf16[2304,9216]{1,0:T(8,128)(2,1)} %refs_2_.7, bf16[4,16,3072]{2,1,0:T(8,128)(2,1)S(1)} %collective-permute-done.5.refs_3_), custom_call_target="tpu_custom_call" | custom-call | flops 905969664 | bytes 14155776 | tf_op jit(solution)/shard_map/partials_10/pallas_call | solution.py:244
  58.1 0.0 copy-start.1
  58.1 0.0 copy-start.2
  58.1 0.0 copy-start.3
  58.1 2.4 %collective-permute-done.12.refs_1_ = bf16[4,16,3840]{2,1,0:T(8,128)(2,1)S(1)} collective-permute-done((bf16[4,16,3840]{2,1,0:T(8,128)(2,1)S(1)}, bf16[4,16,3840]{2,1,0:T(8,128)(2,1)S(1)}, u32[]{:S(2)}, u32[]{:S(2)}) %collective-permute-start.12) | collective-permute-done | bytes 491552 | tf_op jit(solution)/shard_map/ppermute | solution.py:44
  60.5 0.1 combine_3840.2
  60.6 1.8 %collective-permute-start.13 = (bf16[2,16,3840]{2,1,0:T(8,128)(2,1)S(1)}, bf16[2,16,3840]{2,1,0:T(8,128)(2,1)S(1)}, u32[]{:S(2)}, u32[]{:S(2)}) collective-permute-start(bf16[2,16,3840]{2,1,0:T(8,128)(2,1)S(1)} %get-tuple-element.79), channel_id=1, source_target_pairs={{0,8},{4,12},{8,0},{12,4},{16,24},{20,28},{24,16},{28,20},{1,9},{5... | collective-permute-start | bytes 737288 | tf_op jit(solution)/shard_map/ppermute | solution.py:44
  62.4 1.5 %collective-permute-start.6 = (bf16[4,16,1536]{2,1,0:T(8,128)(2,1)S(1)}, bf16[4,16,1536]{2,1,0:T(8,128)(2,1)S(1)}, u32[]{:S(2)}, u32[]{:S(2)}) collective-permute-start(bf16[4,16,1536]{2,1,0:T(8,128)(2,1)S(1)} %get-tuple-element.60), channel_id=1, source_target_pairs={{0,4},{4,0},{8,12},{12,8},{16,20},{20,16},{24,28},{28,24},{1,5},{5... | collective-permute-start | bytes 589832 | tf_op jit(solution)/shard_map/ppermute | solution.py:44
  64.0 0.0 collective-permute-done.10.refs_1_
  64.0 0.1 combine_5504.3
  64.0 2.9 %collective-permute-start.11 = (bf16[1,16,5504]{2,1,0:T(8,128)(2,1)S(1)}, bf16[1,16,5504]{2,1,0:T(8,128)(2,1)S(1)}, u32[]{:S(2)}, u32[]{:S(2)}) collective-permute-start(bf16[1,16,5504]{2,1,0:T(8,128)(2,1)S(1)} %get-tuple-element.75), channel_id=1, source_target_pairs={{0,16},{4,20},{8,24},{12,28},{16,0},{20,4},{24,8},{28,12},{1,17},{... | collective-permute-start | bytes 528392 | tf_op jit(solution)/shard_map/ppermute | solution.py:44
  67.0 1.1 %collective-permute-done.6.refs_1_ = bf16[4,16,1536]{2,1,0:T(8,128)(2,1)S(1)} collective-permute-done((bf16[4,16,1536]{2,1,0:T(8,128)(2,1)S(1)}, bf16[4,16,1536]{2,1,0:T(8,128)(2,1)S(1)}, u32[]{:S(2)}, u32[]{:S(2)}) %collective-permute-start.6) | collective-permute-done | bytes 196640 | tf_op jit(solution)/shard_map/ppermute | solution.py:44
  68.2 0.3 collective-permute-start.7
  68.5 1.7 %collective-permute-done.13.refs_1_ = bf16[2,16,3840]{2,1,0:T(8,128)(2,1)S(1)} collective-permute-done((bf16[2,16,3840]{2,1,0:T(8,128)(2,1)S(1)}, bf16[2,16,3840]{2,1,0:T(8,128)(2,1)S(1)}, u32[]{:S(2)}, u32[]{:S(2)}) %collective-permute-start.13) | collective-permute-done | bytes 245792 | tf_op jit(solution)/shard_map/ppermute | solution.py:44
  70.3 3.1 %collective-permute-start.14 = (bf16[1,16,3840]{2,1,0:T(8,128)(2,1)S(1)}, bf16[1,16,3840]{2,1,0:T(8,128)(2,1)S(1)}, u32[]{:S(2)}, u32[]{:S(2)}) collective-permute-start(bf16[1,16,3840]{2,1,0:T(8,128)(2,1)S(1)} %get-tuple-element.81), channel_id=1, source_target_pairs={{0,16},{4,20},{8,24},{12,28},{16,0},{20,4},{24,8},{28,12},{1,17},{... | collective-permute-start | bytes 368648 | tf_op jit(solution)/shard_map/ppermute | solution.py:44
  73.4 0.3 collective-permute-done.7.refs_1_
  73.7 3.8 %collective-permute-start.8 = (bf16[1,16,1536]{2,1,0:T(8,128)(2,1)S(1)}, bf16[1,16,1536]{2,1,0:T(8,128)(2,1)S(1)}, u32[]{:S(2)}, u32[]{:S(2)}) collective-permute-start(bf16[1,16,1536]{2,1,0:T(8,128)(2,1)S(1)} %get-tuple-element.64), channel_id=1, source_target_pairs={{0,16},{4,20},{8,24},{12,28},{16,0},{20,4},{24,8},{28,12},{1,17},{... | collective-permute-start | bytes 147464 | tf_op jit(solution)/shard_map/ppermute | solution.py:44
  77.4 0.0 collective-permute-done.11.arrived_ref
  77.4 0.1 finish_5504.1
  77.5 1.6 %collective-permute-start.15 = (bf16[2,1,2,1664]{3,2,1,0:T(2,128)(2,1)S(1)}, bf16[2,1,2,1664]{3,2,1,0:T(2,128)(2,1)S(1)}, u32[]{:S(2)}, u32[]{:S(2)}) collective-permute-start(bf16[2,1,2,1664]{3,2,1,0:T(2,128)(2,1)S(1)} %get-tuple-element.83), channel_id=1, source_target_pairs={{0,2},{1,3},{2,0},{3,1},{4,6},{5,7},{6,4},{7,5},{8,10},{9,11},{10,... | collective-permute-start | bytes 39944 | tf_op jit(solution)/shard_map/ppermute | solution.py:44
  79.1 2.1 %collective-permute-done.15.arrived_ref = bf16[2,1,2,1664]{3,2,1,0:T(2,128)(2,1)S(1)} collective-permute-done((bf16[2,1,2,1664]{3,2,1,0:T(2,128)(2,1)S(1)}, bf16[2,1,2,1664]{3,2,1,0:T(2,128)(2,1)S(1)}, u32[]{:S(2)}, u32[]{:S(2)}) %collective-permute-start.15) | collective-permute-done | bytes 13344 | tf_op jit(solution)/shard_map/ppermute | solution.py:44
  81.3 0.0 collective-permute-start.16
  81.3 1.2 %collective-permute-done.16.arrived_ref = bf16[1,2,2,1664]{3,2,1,0:T(2,128)(2,1)S(1)} collective-permute-done((bf16[1,2,2,1664]{3,2,1,0:T(2,128)(2,1)S(1)}, bf16[1,2,2,1664]{3,2,1,0:T(2,128)(2,1)S(1)}, u32[]{:S(2)}, u32[]{:S(2)}) %collective-permute-start.16) | collective-permute-done | bytes 13344 | tf_op jit(solution)/shard_map/ppermute | solution.py:44
  82.5 0.0 copy-done.1
  82.5 0.0 copy-done.2
  82.5 0.0 copy-done.3
  82.5 2.1 %attention.1 = bf16[2,6144]{1,0:T(2,128)(2,1)} custom-call(s32[2]{0:T(128)S(1)} %copy-done.3, bf16[1,2,2,1664]{3,2,1,0:T(2,128)(2,1)S(1)} %get-tuple-element.84.own_ref, bf16[1,2,2,1664]{3,2,1,0:T(2,128)(2,1)S(1)} %collective-permute-done.16.arrived_ref, bf16[2,512,256]{2,1,0:T(8,128)(2,1)S(1)} %copy-done.1, bf16[2,512,256]{2,1,0:T(8,128)(2,1)S(1)} %copy-done.2), custom_call_target="tpu_custom_call" | custom-call | flops 25165824 | bytes 1048576 | tf_op jit(solution)/shard_map/attention/pallas_call | solution.py:373
  84.6 0.0 collective-permute-done.14.arrived_ref
  84.6 0.1 finish_3840.1.refs_1_
  84.6 0.0 collective-permute-done.8.arrived_ref
  84.6 0.7 finish_1536.1
  (10 shorter events, 0.2 us)
Async XLA Ops:
  2.1 5.1 %collective-permute-start = (bf16[4,1,2,2304]{3,2,1,0:T(2,128)(2,1)S(1)}, bf16[4,1,2,2304]{3,2,1,0:T(2,128)(2,1)S(1)}, u32[]{:S(2)}, u32[]{:S(2)}) collective-permute-start(bf16[4,1,2,2304]{3,2,1,0:T(2,128)(2,1)S(1)} %get-tuple-element.44.after_ref), channel_id=1, source_target_pairs={{0,4},{4,0},{8,12},{12,8},{16,20},{20,16},{24,28},{28,24},{1,5},{5... | collective-permute-start | bytes 110600 | tf_op jit(solution)/shard_map/ppermute | solution.py:44
  7.2 4.1 %collective-permute-start.1 = (bf16[2,2,2,2304]{3,2,1,0:T(2,128)(2,1)S(1)}, bf16[2,2,2,2304]{3,2,1,0:T(2,128)(2,1)S(1)}, u32[]{:S(2)}, u32[]{:S(2)}) collective-permute-start(bf16[2,2,2,2304]{3,2,1,0:T(2,128)(2,1)S(1)} %get-tuple-element.47.after_ref), channel_id=1, source_target_pairs={{0,8},{4,12},{8,0},{12,4},{16,24},{20,28},{24,16},{28,20},{1,9},{5... | collective-permute-start | bytes 110600 | tf_op jit(solution)/shard_map/ppermute | solution.py:44
  11.3 5.0 %collective-permute-start.2 = (bf16[1,4,2,2304]{3,2,1,0:T(2,128)(2,1)S(1)}, bf16[1,4,2,2304]{3,2,1,0:T(2,128)(2,1)S(1)}, u32[]{:S(2)}, u32[]{:S(2)}) collective-permute-start(bf16[1,4,2,2304]{3,2,1,0:T(2,128)(2,1)S(1)} %get-tuple-element.50.after_ref), channel_id=1, source_target_pairs={{0,16},{4,20},{8,24},{12,28},{16,0},{20,4},{24,8},{28,12},{1,17},{... | collective-permute-start | bytes 110600 | tf_op jit(solution)/shard_map/ppermute | solution.py:44
  16.4 4.4 %collective-permute-start.3 = (bf16[16,2304]{1,0:T(8,128)(2,1)S(1)}, bf16[16,2304]{1,0:T(8,128)(2,1)S(1)}, u32[]{:S(2)}, u32[]{:S(2)}) collective-permute-start(bf16[16,2304]{1,0:T(8,128)(2,1)S(1)} %join_1_2304.1.after_ref), channel_id=1, source_target_pairs={{0,2},{1,3},{2,0},{3,1},{4,6},{5,7},{6,4},{7,5},{8,10},{9,11},{10,... | collective-permute-start | bytes 221192 | tf_op jit(solution)/shard_map/ppermute | solution.py:44
  18.2 4.9 %slice-start = ((s8[7077888]{0:T(1024)(128)(4,1)}), s8[4194304]{0:T(1024)(128)(4,1)S(1)}, s32[]{:S(2)}) async-start(s8[7077888]{0:T(1024)(128)(4,1)} %bitcast.1), calls=%async_computation | async-start | bytes 8388608
  20.8 3.1 %slice-start.1 = ((s8[7077888]{0:T(1024)(128)(4,1)}), s8[2883584]{0:T(1024)(128)(4,1)S(1)}, s32[]{:S(2)}) async-start(s8[7077888]{0:T(1024)(128)(4,1)} %bitcast.1), calls=%async_computation.1 | async-start | bytes 5767168
  20.8 3.1 %copy-start = (bf16[2304,128]{1,0:T(8,128)(2,1)S(1)}, bf16[2304,128]{1,0:T(8,128)(2,1)}, u32[]{:S(2)}) copy-start(bf16[2304,128]{1,0:T(8,128)(2,1)} %refs_4_.1) | copy-start | bytes 1769476
  20.8 2.3 %collective-permute-start.4 = (bf16[32,2304]{1,0:T(8,128)(2,1)S(1)}, bf16[32,2304]{1,0:T(8,128)(2,1)S(1)}, u32[]{:S(2)}, u32[]{:S(2)}) collective-permute-start(bf16[32,2304]{1,0:T(8,128)(2,1)S(1)} %constant_dynamic-update-slice_fusion.after_ref), channel_id=1, source_target_pairs={{0,1},{1,0},{2,3},{3,2},{4,5},{5,4},{6,7},{7,6},{8,9},{9,8},{10,11... | collective-permute-start | bytes 442376 | tf_op jit(solution)/shard_map/ppermute | solution.py:44
  28.0 10.6 %collective-permute-start.9 = (bf16[4,16,2432]{2,1,0:T(8,128)(2,1)S(1)}, bf16[4,16,2432]{2,1,0:T(8,128)(2,1)S(1)}, u32[]{:S(2)}, u32[]{:S(2)}) collective-permute-start(bf16[4,16,2432]{2,1,0:T(8,128)(2,1)S(1)} %get-tuple-element.66), channel_id=1, source_target_pairs={{0,4},{4,0},{8,12},{12,8},{16,20},{20,16},{24,28},{28,24},{1,5},{5... | collective-permute-start | bytes 933896 | tf_op jit(solution)/shard_map/ppermute | solution.py:44
  38.2 11.9 %collective-permute-start.5 = (bf16[4,16,3072]{2,1,0:T(8,128)(2,1)S(1)}, bf16[4,16,3072]{2,1,0:T(8,128)(2,1)S(1)}, u32[]{:S(2)}, u32[]{:S(2)}) collective-permute-start(bf16[4,16,3072]{2,1,0:T(8,128)(2,1)S(1)} %get-tuple-element.58), channel_id=1, source_target_pairs={{0,4},{4,0},{8,12},{12,8},{16,20},{20,16},{24,28},{28,24},{1,5},{5... | collective-permute-start | bytes 1179656 | tf_op jit(solution)/shard_map/ppermute | solution.py:44
  48.1 12.4 %collective-permute-start.12 = (bf16[4,16,3840]{2,1,0:T(8,128)(2,1)S(1)}, bf16[4,16,3840]{2,1,0:T(8,128)(2,1)S(1)}, u32[]{:S(2)}, u32[]{:S(2)}) collective-permute-start(bf16[4,16,3840]{2,1,0:T(8,128)(2,1)S(1)} %get-tuple-element.77), channel_id=1, source_target_pairs={{0,4},{4,0},{8,12},{12,8},{16,20},{20,16},{24,28},{28,24},{1,5},{5... | collective-permute-start | bytes 1474568 | tf_op jit(solution)/shard_map/ppermute | solution.py:44
  50.2 13.8 %collective-permute-start.10 = (bf16[2,16,5504]{2,1,0:T(8,128)(2,1)S(1)}, bf16[2,16,5504]{2,1,0:T(8,128)(2,1)S(1)}, u32[]{:S(2)}, u32[]{:S(2)}) collective-permute-start(bf16[2,16,5504]{2,1,0:T(8,128)(2,1)S(1)} %get-tuple-element.73), channel_id=1, source_target_pairs={{0,8},{4,12},{8,0},{12,4},{16,24},{20,28},{24,16},{28,20},{1,9},{5... | collective-permute-start | bytes 1056776 | tf_op jit(solution)/shard_map/ppermute | solution.py:44
  58.1 24.4 %copy-start.1 = (bf16[2,512,256]{2,1,0:T(8,128)(2,1)S(1)}, bf16[2,512,256]{2,1,0:T(8,128)(2,1)}, u32[]{:S(2)}) copy-start(bf16[2,512,256]{2,1,0:T(8,128)(2,1)} %k_ref.1) | copy-start | bytes 1572868
  58.1 24.4 %copy-start.2 = (bf16[2,512,256]{2,1,0:T(8,128)(2,1)S(1)}, bf16[2,512,256]{2,1,0:T(8,128)(2,1)}, u32[]{:S(2)}) copy-start(bf16[2,512,256]{2,1,0:T(8,128)(2,1)} %v_ref.1) | copy-start | bytes 1572868
  58.1 24.4 %copy-start.3 = (s32[2]{0:T(128)S(1)}, s32[2]{0:T(128)}, u32[]{:S(2)}) copy-start(s32[2]{0:T(128)} %lengths_ref.1) | copy-start | bytes 28
  60.6 9.6 %collective-permute-start.13 = (bf16[2,16,3840]{2,1,0:T(8,128)(2,1)S(1)}, bf16[2,16,3840]{2,1,0:T(8,128)(2,1)S(1)}, u32[]{:S(2)}, u32[]{:S(2)}) collective-permute-start(bf16[2,16,3840]{2,1,0:T(8,128)(2,1)S(1)} %get-tuple-element.79), channel_id=1, source_target_pairs={{0,8},{4,12},{8,0},{12,4},{16,24},{20,28},{24,16},{28,20},{1,9},{5... | collective-permute-start | bytes 737288 | tf_op jit(solution)/shard_map/ppermute | solution.py:44
  62.4 5.7 %collective-permute-start.6 = (bf16[4,16,1536]{2,1,0:T(8,128)(2,1)S(1)}, bf16[4,16,1536]{2,1,0:T(8,128)(2,1)S(1)}, u32[]{:S(2)}, u32[]{:S(2)}) collective-permute-start(bf16[4,16,1536]{2,1,0:T(8,128)(2,1)S(1)} %get-tuple-element.60), channel_id=1, source_target_pairs={{0,4},{4,0},{8,12},{12,8},{16,20},{20,16},{24,28},{28,24},{1,5},{5... | collective-permute-start | bytes 589832 | tf_op jit(solution)/shard_map/ppermute | solution.py:44
  64.0 13.4 %collective-permute-start.11 = (bf16[1,16,5504]{2,1,0:T(8,128)(2,1)S(1)}, bf16[1,16,5504]{2,1,0:T(8,128)(2,1)S(1)}, u32[]{:S(2)}, u32[]{:S(2)}) collective-permute-start(bf16[1,16,5504]{2,1,0:T(8,128)(2,1)S(1)} %get-tuple-element.75), channel_id=1, source_target_pairs={{0,16},{4,20},{8,24},{12,28},{16,0},{20,4},{24,8},{28,12},{1,17},{... | collective-permute-start | bytes 528392 | tf_op jit(solution)/shard_map/ppermute | solution.py:44
  68.2 5.5 %collective-permute-start.7 = (bf16[2,16,1536]{2,1,0:T(8,128)(2,1)S(1)}, bf16[2,16,1536]{2,1,0:T(8,128)(2,1)S(1)}, u32[]{:S(2)}, u32[]{:S(2)}) collective-permute-start(bf16[2,16,1536]{2,1,0:T(8,128)(2,1)S(1)} %get-tuple-element.62), channel_id=1, source_target_pairs={{0,8},{4,12},{8,0},{12,4},{16,24},{20,28},{24,16},{28,20},{1,9},{5... | collective-permute-start | bytes 294920 | tf_op jit(solution)/shard_map/ppermute | solution.py:44
  70.3 14.3 %collective-permute-start.14 = (bf16[1,16,3840]{2,1,0:T(8,128)(2,1)S(1)}, bf16[1,16,3840]{2,1,0:T(8,128)(2,1)S(1)}, u32[]{:S(2)}, u32[]{:S(2)}) collective-permute-start(bf16[1,16,3840]{2,1,0:T(8,128)(2,1)S(1)} %get-tuple-element.81), channel_id=1, source_target_pairs={{0,16},{4,20},{8,24},{12,28},{16,0},{20,4},{24,8},{28,12},{1,17},{... | collective-permute-start | bytes 368648 | tf_op jit(solution)/shard_map/ppermute | solution.py:44
  73.7 11.0 %collective-permute-start.8 = (bf16[1,16,1536]{2,1,0:T(8,128)(2,1)S(1)}, bf16[1,16,1536]{2,1,0:T(8,128)(2,1)S(1)}, u32[]{:S(2)}, u32[]{:S(2)}) collective-permute-start(bf16[1,16,1536]{2,1,0:T(8,128)(2,1)S(1)} %get-tuple-element.64), channel_id=1, source_target_pairs={{0,16},{4,20},{8,24},{12,28},{16,0},{20,4},{24,8},{28,12},{1,17},{... | collective-permute-start | bytes 147464 | tf_op jit(solution)/shard_map/ppermute | solution.py:44
  77.5 3.8 %collective-permute-start.15 = (bf16[2,1,2,1664]{3,2,1,0:T(2,128)(2,1)S(1)}, bf16[2,1,2,1664]{3,2,1,0:T(2,128)(2,1)S(1)}, u32[]{:S(2)}, u32[]{:S(2)}) collective-permute-start(bf16[2,1,2,1664]{3,2,1,0:T(2,128)(2,1)S(1)} %get-tuple-element.83), channel_id=1, source_target_pairs={{0,2},{1,3},{2,0},{3,1},{4,6},{5,7},{6,4},{7,5},{8,10},{9,11},{10,... | collective-permute-start | bytes 39944 | tf_op jit(solution)/shard_map/ppermute | solution.py:44
  81.3 1.2 %collective-permute-start.16 = (bf16[1,2,2,1664]{3,2,1,0:T(2,128)(2,1)S(1)}, bf16[1,2,2,1664]{3,2,1,0:T(2,128)(2,1)S(1)}, u32[]{:S(2)}, u32[]{:S(2)}) collective-permute-start(bf16[1,2,2,1664]{3,2,1,0:T(2,128)(2,1)S(1)} %get-tuple-element.85), channel_id=1, source_target_pairs={{0,1},{1,0},{2,3},{3,2},{4,5},{5,4},{6,7},{7,6},{8,9},{9,8},{10,11... | collective-permute-start | bytes 39944 | tf_op jit(solution)/shard_map/ppermute | solution.py:44

commit v3 on v2

--- a/solution.py
+++ b/solution.py
@@ -10,10 +10,15 @@
 HEADS = 24
 DH = 256
 EPS = 1e-05
-PORTIONS = ((1, 4), (5,), (2,))
+PORTIONS = ((1,), (4,), (4,), (3,))
+ORDER = (
+    "K0", "K1", "S0", "K2", "S0", "S1", "K3", "S2", "F0", "S1", "J", "S3", "S2", "A", "S3", "F1",
+    "F2", "F3",
+)
 TILE = 768
-AHEAD = 1
+AHEAD = 2
 SLOTS = 3
+WEIGHT = 2 * 10**9
 
 BF16 = jnp.bfloat16
 F32 = jnp.float32
@@ -90,8 +95,9 @@
     )(in_hbm(stream), in_hbm(norm_gain.reshape(1, width)))
 
 
-def join_kernel(sent, keep_ref, arrived_ref, *outs):
+def join_kernel(sent, keep_ref, arrived_ref, *refs):
     slots, count = keep_ref.shape[:2]
+    outs = refs[-1:] if slots == 1 else refs[-2:]
     if slots == 1:
         pieces = [ref[0, i].astype(F32) for ref in (keep_ref, arrived_ref) for i in range(count)]
         outs[0][...] = jnp.concatenate(pieces, axis=0).astype(BF16)
@@ -107,7 +113,7 @@
         places[way] += 1
 
 
-def join(keep, arrived, sent):
+def join(keep, arrived, sent, after=()):
     slots, count, rows, cols = keep.shape
     if slots == 1:
         out_shape = (shape((2 * count * rows, cols), BF16),)
@@ -116,11 +122,12 @@
     return pl.pallas_call(
         functools.partial(join_kernel, tuple(sent)),
         out_shape=out_shape,
-        in_specs=[VMEM, VMEM],
+        in_specs=[VMEM, VMEM] + [ANY] * len(after),
         out_specs=(VMEM,) * len(out_shape),
         compiler_params=pltpu.CompilerParams(vmem_limit_bytes=2 << 20),
+        cost_estimate=pl.CostEstimate(flops=WEIGHT, bytes_accessed=10**6, transcendentals=0),
         name="join_%d_%d" % (slots, cols),
-    )(keep, arrived)
+    )(keep, arrived, *after)
 
 
 def split(value):
@@ -286,46 +293,49 @@
         in_specs=[VMEM] * (2 * len(parts)) + [ANY] * len(after),
         out_specs=(VMEM, VMEM),
         compiler_params=pltpu.CompilerParams(vmem_limit_bytes=2 << 20),
+        cost_estimate=pl.CostEstimate(flops=WEIGHT, bytes_accessed=10**6, transcendentals=0),
         name="combine_%d" % cols,
     )(*[a for part in parts for a in part], *after)
 
 
-def finish_kernel(wide, keep_ref, arrived_ref, *refs):
+def finish_kernel(wide, ready, keep_ref, arrived_ref, *refs):
     both = keep_ref[0] + arrived_ref[0].astype(F32)
     rows = both.shape[0] // 2
     if wide:
-        earlier, (send_ref, own_ref, hidden_ref) = refs[:-3], refs[-3:]
+        send_ref, own_ref, hidden_ref = refs[-3:]
         middle, _, per, _ = own_ref.shape
         heads = both[:rows, :wide] + both[rows:, :wide]
         for j in range(2 * middle):
             piece = heads[j * per : (j + 1) * per].astype(BF16)
             (own_ref if j < middle else send_ref)[j % middle, 0] = piece
     else:
-        earlier, hidden_ref = refs[:-1], refs[-1]
+        hidden_ref = refs[-1]
     at = 0
-    for ref in earlier:
+    for ref in refs[:ready]:
         hidden_ref[:, at : at + ref.shape[1]] = ref[...]
         at += ref.shape[1]
     gate, up = both[:rows, wide:], both[rows:, wide:]
     hidden_ref[:, at:] = (gate * (1.0 / (1.0 + jnp.exp(-gate))) * up).astype(BF16)
 
 
-def finish(keep, arrived, wide, groups, earlier):
+def finish(keep, arrived, wide, groups, earlier, after=()):
     _, rows, cols = keep.shape
     out = [shape((rows // 2, cols - wide + sum(e.shape[1] for e in earlier)), BF16)]
     if wide:
         out = [shape((groups // 2, 1, rows // 2 // groups, wide), BF16)] * 2 + out
     return pl.pallas_call(
-        functools.partial(finish_kernel, wide),
+        functools.partial(finish_kernel, wide, len(earlier)),
         out_shape=tuple(out),
-        in_specs=[VMEM] * (2 + len(earlier)),
+        in_specs=[VMEM] * (2 + len(earlier)) + [ANY] * len(after),
         out_specs=(VMEM,) * len(out),
         compiler_params=pltpu.CompilerParams(vmem_limit_bytes=4 << 20),
+        cost_estimate=pl.CostEstimate(flops=WEIGHT, bytes_accessed=10**6, transcendentals=0),
         name="finish_%d" % cols,
-    )(keep, arrived, *earlier)
-
-
-def attention_kernel(order, lengths_ref, own_ref, arrived_ref, k_ref, v_ref, out_ref, q_ref, pieces_ref):
+    )(keep, arrived, *earlier, *after)
+
+
+def attention_kernel(order, lengths_ref, own_ref, arrived_ref, k_ref, v_ref, *refs):
+    out_ref, q_ref, pieces_ref = refs[-3:]
     rows, cache, _ = k_ref.shape
     groups = len(order)
     keyval_cols = 2 * DH // groups
@@ -368,12 +378,12 @@
         out_ref[:, h * DH : (h + 1) * DH] = both.astype(BF16)
 
 
-def attention(own, arrived, k_cache, v_cache, lengths, order):
+def attention(own, arrived, k_cache, v_cache, lengths, order, after=()):
     rows, cache, _ = k_cache.shape
     return pl.pallas_call(
         functools.partial(attention_kernel, order),
         out_shape=shape((rows, HEADS * DH), BF16),
-        in_specs=[SMEM, VMEM, VMEM, VMEM, VMEM],
+        in_specs=[SMEM, VMEM, VMEM, VMEM, VMEM] + [ANY] * len(after),
         out_specs=VMEM,
         scratch_shapes=[pltpu.VMEM((HEADS, DH), F32), pltpu.VMEM((len(order), rows, own.shape[3]), F32)],
         cost_estimate=pl.CostEstimate(
@@ -381,16 +391,16 @@
         ),
         compiler_params=pltpu.CompilerParams(vmem_limit_bytes=6 << 20),
         name="attention",
-    )(lengths, own, arrived, k_cache, v_cache)
+    )(lengths, own, arrived, k_cache, v_cache, *after)
 
 
 def body(stream, norm_gain, w_gate, w_up, w_query, w_keyval, k_cache, v_cache, lengths):
     size, groups = lax.axis_size("gx"), lax.axis_size("gy")
     ff = w_gate.shape[1]
     wide = w_query.shape[1] + w_keyval.shape[1]
-    tile = max(t for t in range(128, TILE + 1, 128) if ff % t == 0)
+    flat = [p for group in PORTIONS for p in group]
+    tile = max(t for t in range(128, TILE + 1, 128) if ff % t == 0 and ff // t >= sum(flat))
     blocks = ff // tile
-    flat = [p for group in PORTIONS for p in group]
     edges = [round(blocks * sum(flat[:i]) / sum(flat)) for i in range(len(flat) + 1)]
 
     pieces = [[] for _ in flat]
@@ -420,37 +430,51 @@
         x = jnp.concatenate([keep, arrived], axis=0)
         order = order + [j ^ bit for j in order]
 
-    parts = []
-    for i in range(len(flat)):
-        first, count = edges[i], edges[i + 1] - edges[i]
-        if i == 0:
-            heads = (w_query, w_keyval)
-            x, send, keep = partials(x, w_gate, w_up, pieces[i], size, tile, first, count, heads, tuple(order))
+    ways = [[] for _ in PORTIONS]
+    group_of = [g for g, group in enumerate(PORTIONS) for _ in group]
+    left = [list(bits[1:]) for _ in PORTIONS]
+    hidden = [None for _ in PORTIONS]
+    gather = bits_of(groups)[:0:-1]
+    context = None
+    arrived = []
+    after = ()
+    for step in ORDER:
+        what, i = step[0], int(step[1:] or 0)
+        if what == "K":
+            first, count = edges[i], edges[i + 1] - edges[i]
+            heads = () if i else (w_query, w_keyval)
+            after += tuple(arrived[i - 2 : i - 1]) if i > 1 else ()
+            *moved, send, keep = partials(
+                x, w_gate, w_up, pieces[i], size, tile, first, count, heads, None if i else tuple(order), after
+            )
+            x = moved[0] if moved else x
+            arrived.append(swap(send, "gx", bits[0]))
+            ways[group_of[i]].append((keep, arrived[-1]))
+        elif what == "S" or what == "F":
+            columns = 0 if i else wide
+            while left[i]:
+                bit = left[i].pop(0)
+                send, keep = combine(ways[i], columns, after)
+                ways[i] = [(keep, swap(send, "gx", bit))]
+                after = (keep,)
+                if what == "S":
+                    break
+            if what == "F":
+                earlier = hidden[:i] if i == len(PORTIONS) - 1 else []
+                *parted, keep = finish(*ways[i][0], columns, groups, earlier, after)
+                hidden[i] = keep
+                if parted:
+                    query = (parted[1], swap(parted[0], "gy", 1 << len(gather)))
+        elif what == "J":
+            for bit in gather:
+                own, other = query
+                send, keep = join(own, other, range(own.shape[0] // 2, own.shape[0]), after)
+                query = (keep, swap(send, "gy", bit // 2))
+                after = (keep,)
         else:
-            after = (parts[i - 2][1],) if i > 1 else ()
-            send, keep = partials(x, w_gate, w_up, pieces[i], size, tile, first, count, after=after)
-        parts.append((keep, swap(send, "gx", bits[0])))
-
-    hidden = []
-    context = None
-    at = 0
-    for number, group in enumerate(PORTIONS):
-        columns = 0 if number else wide
-        here = parts[at : at + len(group)]
-        at += len(group)
-        after = (parts[at][0],) if at < len(flat) else ()
-        for bit in bits[1:]:
-            send, keep = combine(here, columns, after)
-            after = ()
-            here = [(keep, swap(send, "gx", bit))]
-        *heads, part = finish(*here[0], columns, groups, hidden if at == len(flat) else [])
-        hidden.append(part)
-        if number:
+            context = attention(*query, k_cache, v_cache, lengths, tuple(order), after)
             continue
-        send, keep = heads
-        for bit in bits_of(groups)[:0:-1]:
-            send, keep = join(keep, swap(send, "gy", bit), range(keep.shape[0] // 2, keep.shape[0]))
-        context = attention(keep, swap(send, "gy", 1), k_cache, v_cache, lengths, tuple(order))
+        after = (keep,)
     return hidden[-1], context
 
 

time: 85.7 us -> 80.1 us (0.935)
  starting transfers between devices: 30.8 us -> 23.2 us
  local copies, waits for them, and re-layouts: 0.85 us -> 1.87 us
    ppermute x17 -> x19, starting transfers between devices: 30.8 us -> 23.2 us  [swap(): return lax.ppermute(x, axis, [(i, i ^ bit) for i in range(size)])]
    pallas_call x5, Pallas kernels: 10.3 us -> 15.3 us  [fetch(): pl.pallas_call(functools.partial(fetch_kernel, first), out_shape=pltpu.VM...]
    pallas_call x4, Pallas kernels: 28.2 us -> 23.4 us  [partials(): pl.pallas_call(functools.partial(partials_kernel, slots, first, count, ti...]
    unnamed x13, local copies, waits for them, and re-layouts: 0.84 us -> 1.86 us
    ppermute x17 -> x19, waiting for transfers between devices: 9.36 us -> 10.2 us  [swap(): return lax.ppermute(x, axis, [(i, i ^ bit) for i in range(size)])]
  transfers between devices with their start and end apart: 17 -> 19, of which waited for: 7 -> 6; matrix products, arithmetic and copies ran while one was open for 0% -> 0% of each run, Pallas kernels for 44% -> 47%
where the time goes in v3:
time: 80.1 us; the launch traced here: 79.7 us
  Pallas kernels  43.6 us (54%)
  starting transfers between devices  23.2 us (29%)
  waiting for transfers between devices  10.2 us (13%)
  local copies, waits for them, and re-layouts  1.87 us (2%)
  between operations  0.9 us (1%)
    pallas_call x4, Pallas kernels, partials(): pl.pallas_call(functools.partial(partials_kernel, slots, first, count, ti...  23.4 us
    ppermute x19, starting transfers between devices, swap(): return lax.ppermute(x, axis, [(i, i ^ bit) for i in range(size)])  23.2 us
    pallas_call x5, Pallas kernels, fetch(): pl.pallas_call(functools.partial(fetch_kernel, first), out_shape=pltpu.VM...  15.3 us
    ppermute x19, waiting for transfers between devices, swap(): return lax.ppermute(x, axis, [(i, i ^ bit) for i in range(size)])  10.2 us
    pallas_call x1, Pallas kernels, attention(): pl.pallas_call(functools.partial(attention_kernel, order), out_shape=shap...  2.09 us
    unnamed x13, local copies, waits for them, and re-layouts  1.86 us
  transfers between devices with their start and end apart: 19, of which 6 were waited for; matrix products, arithmetic and copies ran while one was open for 0% of the time, Pallas kernels for 47%

profile of v3, /device:TPU:0, one launch (start us, length us, event | category | flops | bytes accessed | tf_op | source)
XLA Modules:
  0.0 79.7 jit_solution(11402421487556549630)
XLA Ops:
  0.6 1.5 %layer_norm.1 = (bf16[4,1,2,2304]{3,2,1,0:T(2,128)(2,1)S(1)}, bf16[4,1,2,2304]{3,2,1,0:T(2,128)(2,1)S(1)}) custom-call(bf16[2,18432]{1,0:T(2,128)(2,1)} %x_hbm.1, f32[1,18432]{1,0:T(1,128)} %bitcast.3), custom_call_target="tpu_custom_call" | custom-call | flops 20000000000 | bytes 1000000 | tf_op jit(solution)/shard_map/layer_norm/pallas_call | solution.py:82
  2.1 3.0 %collective-permute-start = (bf16[4,1,2,2304]{3,2,1,0:T(2,128)(2,1)S(1)}, bf16[4,1,2,2304]{3,2,1,0:T(2,128)(2,1)S(1)}, u32[]{:S(2)}, u32[]{:S(2)}) collective-permute-start(bf16[4,1,2,2304]{3,2,1,0:T(2,128)(2,1)S(1)} %get-tuple-element.48.after_ref), channel_id=1, source_target_pairs={{0,4},{4,0},{8,12},{12,8},{16,20},{20,16},{24,28},{28,24},{1,5},{5... | collective-permute-start | bytes 110600 | tf_op jit(solution)/shard_map/ppermute | solution.py:49
  5.2 3.0 %fetch_768.1.refs_3_ = bf16[2304,1536]{1,0:T(8,128)(2,1)S(1)} custom-call(bf16[2304,9216]{1,0:T(8,128)(2,1)} %refs_1_.7, bf16[4,1,2,2304]{3,2,1,0:T(2,128)(2,1)S(1)} %get-tuple-element.48.after_ref), custom_call_target="tpu_custom_call" | custom-call | bytes 7077888 | tf_op jit(solution)/shard_map/fetch_768/pallas_call | solution.py:179
  8.2 0.0 collective-permute-done.arrived_ref
  8.2 1.6 %collective-permute-start.1 = (bf16[2,2,2,2304]{3,2,1,0:T(2,128)(2,1)S(1)}, bf16[2,2,2,2304]{3,2,1,0:T(2,128)(2,1)S(1)}, u32[]{:S(2)}, u32[]{:S(2)}) collective-permute-start(bf16[2,2,2,2304]{3,2,1,0:T(2,128)(2,1)S(1)} %get-tuple-element.51.after_ref), channel_id=1, source_target_pairs={{0,8},{4,12},{8,0},{12,4},{16,24},{20,28},{24,16},{28,20},{1,9},{5... | collective-permute-start | bytes 110600 | tf_op jit(solution)/shard_map/ppermute | solution.py:49
  9.8 3.0 %fetch_3840.1.refs_3_ = bf16[2304,1536]{1,0:T(8,128)(2,1)S(1)} custom-call(bf16[2304,9216]{1,0:T(8,128)(2,1)} %refs_1_.7, bf16[2,2,2,2304]{3,2,1,0:T(2,128)(2,1)S(1)} %get-tuple-element.51.after_ref), custom_call_target="tpu_custom_call" | custom-call | bytes 7077888 | tf_op jit(solution)/shard_map/fetch_3840/pallas_call | solution.py:179
  12.9 0.0 collective-permute-done.1.arrived_ref
  12.9 2.7 %collective-permute-start.2 = (bf16[1,4,2,2304]{3,2,1,0:T(2,128)(2,1)S(1)}, bf16[1,4,2,2304]{3,2,1,0:T(2,128)(2,1)S(1)}, u32[]{:S(2)}, u32[]{:S(2)}) collective-permute-start(bf16[1,4,2,2304]{3,2,1,0:T(2,128)(2,1)S(1)} %get-tuple-element.54.after_ref), channel_id=1, source_target_pairs={{0,16},{4,20},{8,24},{12,28},{16,0},{20,4},{24,8},{28,12},{1,17},{... | collective-permute-start | bytes 110600 | tf_op jit(solution)/shard_map/ppermute | solution.py:49
  15.6 3.0 %fetch_6912.1.refs_3_ = bf16[2304,1536]{1,0:T(8,128)(2,1)S(1)} custom-call(bf16[2304,9216]{1,0:T(8,128)(2,1)} %refs_1_.7, bf16[1,4,2,2304]{3,2,1,0:T(2,128)(2,1)S(1)} %get-tuple-element.54.after_ref), custom_call_target="tpu_custom_call" | custom-call | bytes 7077888 | tf_op jit(solution)/shard_map/fetch_6912/pallas_call | solution.py:179
  18.6 0.0 collective-permute-done.2.arrived_ref
  18.6 0.1 join_1_2304.1.after_ref
  18.7 1.6 %collective-permute-start.3 = (bf16[16,2304]{1,0:T(8,128)(2,1)S(1)}, bf16[16,2304]{1,0:T(8,128)(2,1)S(1)}, u32[]{:S(2)}, u32[]{:S(2)}) collective-permute-start(bf16[16,2304]{1,0:T(8,128)(2,1)S(1)} %join_1_2304.1.after_ref), channel_id=1, source_target_pairs={{0,2},{1,3},{2,0},{3,1},{4,6},{5,7},{6,4},{7,5},{8,10},{9,11},{10,... | collective-permute-start | bytes 221192 | tf_op jit(solution)/shard_map/ppermute | solution.py:49
  20.2 3.0 %fetch_2304.1.refs_4_ = bf16[2304,1536]{1,0:T(8,128)(2,1)S(1)} custom-call(bf16[2304,9216]{1,0:T(8,128)(2,1)} %refs_1_.7, bf16[16,2304]{1,0:T(8,128)(2,1)S(1)} %join_1_2304.1.after_ref), custom_call_target="tpu_custom_call" | custom-call | bytes 7077888 | tf_op jit(solution)/shard_map/fetch_2304/pallas_call | solution.py:179
  23.3 0.0 collective-permute-done.3
  23.3 0.0 slice-start
  23.3 0.0 slice-start.1
  23.3 0.0 copy-start
  23.3 0.1 collective-permute-start.4
  23.4 3.2 %fetch_5376.1.refs_4_ = bf16[2304,1536]{1,0:T(8,128)(2,1)S(1)} custom-call(bf16[2304,9216]{1,0:T(8,128)(2,1)} %refs_1_.7, bf16[32,2304]{1,0:T(8,128)(2,1)S(1)} %constant_dynamic-update-slice_fusion.after_ref), custom_call_target="tpu_custom_call" | custom-call | bytes 7077888 | tf_op jit(solution)/shard_map/fetch_5376/pallas_call | solution.py:179
  26.6 0.0 collective-permute-done.4
  26.6 0.9 %slice-done = s8[4194304]{0:T(1024)(128)(4,1)S(1)} async-done(((s8[7077888]{0:T(1024)(128)(4,1)}), s8[4194304]{0:T(1024)(128)(4,1)S(1)}, s32[]{:S(2)}) %slice-start) | async-done | bytes 4194328
  27.5 0.9 %slice-done.1 = s8[2883584]{0:T(1024)(128)(4,1)S(1)} async-done(((s8[7077888]{0:T(1024)(128)(4,1)}), s8[2883584]{0:T(1024)(128)(4,1)S(1)}, s32[]{:S(2)}) %slice-start.1) | async-done | bytes 2883608
  28.4 0.0 copy-done
  28.5 4.1 %partials_0.1 = (bf16[64,2304]{1,0:T(8,128)(2,1)S(1)}, bf16[4,16,2432]{2,1,0:T(8,128)(2,1)S(1)}, f32[4,16,2432]{2,1,0:T(8,128)S(1)}) custom-call(bf16[64,2304]{1,0:T(8,128)(2,1)S(1)} %pad_maximum_fusion.refs_0_, bf16[2304,9216]{1,0:T(8,128)(2,1)} %refs_1_.7, bf16[2304,9216]{1,0:T(8,128)(2,1)} %refs_2_.7, bf16[2304,1536]{1,0:T(8,128)(2,1)S(1)} %bitcast.2, ...), custom_call_target="tpu_custom_call" | custom-call | flops 1434451968 | bytes 22413312 | tf_op jit(solution)/shard_map/partials_0/pallas_call | solution.py:251
  32.5 1.0 %collective-permute-start.6 = (bf16[4,16,2432]{2,1,0:T(8,128)(2,1)S(1)}, bf16[4,16,2432]{2,1,0:T(8,128)(2,1)S(1)}, u32[]{:S(2)}, u32[]{:S(2)}) collective-permute-start(bf16[4,16,2432]{2,1,0:T(8,128)(2,1)S(1)} %get-tuple-element.66), channel_id=1, source_target_pairs={{0,4},{4,0},{8,12},{12,8},{16,20},{20,16},{24,28},{28,24},{1,5},{5... | collective-permute-start | bytes 933896 | tf_op jit(solution)/shard_map/ppermute | solution.py:49
  33.5 6.5 %partials_1.1 = (bf16[4,16,3072]{2,1,0:T(8,128)(2,1)S(1)}, f32[4,16,3072]{2,1,0:T(8,128)S(1)}) custom-call(bf16[64,2304]{1,0:T(8,128)(2,1)S(1)} %get-tuple-element.59.refs_0_, bf16[2304,9216]{1,0:T(8,128)(2,1)} %refs_1_.7, bf16[2304,9216]{1,0:T(8,128)(2,1)} %refs_2_.7, bf16[2304,1536]{1,0:T(8,128)(2,1)S(1)} %fetch_768.1.refs_3_, ...), custom_call_target="tpu_custom_call" | custom-call | flops 1811939328 | bytes 28311552 | tf_op jit(solution)/shard_map/partials_1/pallas_call | solution.py:251
  40.0 1.2 %collective-permute-start.5 = (bf16[4,16,3072]{2,1,0:T(8,128)(2,1)S(1)}, bf16[4,16,3072]{2,1,0:T(8,128)(2,1)S(1)}, u32[]{:S(2)}, u32[]{:S(2)}) collective-permute-start(bf16[4,16,3072]{2,1,0:T(8,128)(2,1)S(1)} %get-tuple-element.65), channel_id=1, source_target_pairs={{0,4},{4,0},{8,12},{12,8},{16,20},{20,16},{24,28},{28,24},{1,5},{5... | collective-permute-start | bytes 1179656 | tf_op jit(solution)/shard_map/ppermute | solution.py:49
  41.2 0.0 collective-permute-done.6.refs_1_.refs_6_
  41.2 0.1 combine_2432.2
  41.3 1.0 %collective-permute-start.7 = (bf16[2,16,2432]{2,1,0:T(8,128)(2,1)S(1)}, bf16[2,16,2432]{2,1,0:T(8,128)(2,1)S(1)}, u32[]{:S(2)}, u32[]{:S(2)}) collective-permute-start(bf16[2,16,2432]{2,1,0:T(8,128)(2,1)S(1)} %get-tuple-element.68), channel_id=1, source_target_pairs={{0,8},{4,12},{8,0},{12,4},{16,24},{20,28},{24,16},{28,20},{1,9},{5... | collective-permute-start | bytes 466952 | tf_op jit(solution)/shard_map/ppermute | solution.py:49
  42.2 6.5 %partials_5.1 = (bf16[4,16,3072]{2,1,0:T(8,128)(2,1)S(1)}, f32[4,16,3072]{2,1,0:T(8,128)S(1)}) custom-call(bf16[64,2304]{1,0:T(8,128)(2,1)S(1)} %get-tuple-element.59.refs_0_, bf16[2304,9216]{1,0:T(8,128)(2,1)} %refs_1_.7, bf16[2304,9216]{1,0:T(8,128)(2,1)} %refs_2_.7, bf16[2304,1536]{1,0:T(8,128)(2,1)S(1)} %fetch_3840.1.refs_3_, ...), custom_call_target="tpu_custom_call" | custom-call | flops 1811939328 | bytes 28311552 | tf_op jit(solution)/shard_map/partials_5/pallas_call | solution.py:251
  48.7 1.0 %collective-permute-start.10 = (bf16[4,16,3072]{2,1,0:T(8,128)(2,1)S(1)}, bf16[4,16,3072]{2,1,0:T(8,128)(2,1)S(1)}, u32[]{:S(2)}, u32[]{:S(2)}) collective-permute-start(bf16[4,16,3072]{2,1,0:T(8,128)(2,1)S(1)} %get-tuple-element.77), channel_id=1, source_target_pairs={{0,4},{4,0},{8,12},{12,8},{16,20},{20,16},{24,28},{28,24},{1,5},{5... | collective-permute-start | bytes 1179656 | tf_op jit(solution)/shard_map/ppermute | solution.py:49
  49.7 0.0 collective-permute-done.7.refs_1_
  49.8 1.9 %collective-permute-start.9 = (bf16[1,16,2432]{2,1,0:T(8,128)(2,1)S(1)}, bf16[1,16,2432]{2,1,0:T(8,128)(2,1)S(1)}, u32[]{:S(2)}, u32[]{:S(2)}) collective-permute-start(bf16[1,16,2432]{2,1,0:T(8,128)(2,1)S(1)} %get-tuple-element.76), channel_id=1, source_target_pairs={{0,16},{4,20},{8,24},{12,28},{16,0},{20,4},{24,8},{28,12},{1,17},{... | collective-permute-start | bytes 233480 | tf_op jit(solution)/shard_map/ppermute | solution.py:49
  51.6 0.0 collective-permute-done.5.refs_1_.refs_5_
  51.7 0.1 combine_3072.4
  51.7 1.2 %collective-permute-start.12 = (bf16[2,16,3072]{2,1,0:T(8,128)(2,1)S(1)}, bf16[2,16,3072]{2,1,0:T(8,128)(2,1)S(1)}, u32[]{:S(2)}, u32[]{:S(2)}) collective-permute-start(bf16[2,16,3072]{2,1,0:T(8,128)(2,1)S(1)} %get-tuple-element.81), channel_id=1, source_target_pairs={{0,8},{4,12},{8,0},{12,4},{16,24},{20,28},{24,16},{28,20},{1,9},{5... | collective-permute-start | bytes 589832 | tf_op jit(solution)/shard_map/ppermute | solution.py:49
  52.9 6.4 %partials_9.1 = (bf16[4,16,2304]{2,1,0:T(8,128)(2,1)S(1)}, f32[4,16,2304]{2,1,0:T(8,128)S(1)}) custom-call(bf16[64,2304]{1,0:T(8,128)(2,1)S(1)} %get-tuple-element.59.refs_0_, bf16[2304,9216]{1,0:T(8,128)(2,1)} %refs_1_.7, bf16[2304,9216]{1,0:T(8,128)(2,1)} %refs_2_.7, bf16[2304,1536]{1,0:T(8,128)(2,1)S(1)} %fetch_6912.1.refs_3_, ...), custom_call_target="tpu_custom_call" | custom-call | flops 1358954496 | bytes 21233664 | tf_op jit(solution)/shard_map/partials_9/pallas_call | solution.py:251
  59.3 1.2 %collective-permute-start.8 = (bf16[4,16,2304]{2,1,0:T(8,128)(2,1)S(1)}, bf16[4,16,2304]{2,1,0:T(8,128)(2,1)S(1)}, u32[]{:S(2)}, u32[]{:S(2)}) collective-permute-start(bf16[4,16,2304]{2,1,0:T(8,128)(2,1)S(1)} %get-tuple-element.75), channel_id=1, source_target_pairs={{0,4},{4,0},{8,12},{12,8},{16,20},{20,16},{24,28},{28,24},{1,5},{5... | collective-permute-start | bytes 884744 | tf_op jit(solution)/shard_map/ppermute | solution.py:49
  60.5 0.0 collective-permute-done.10.refs_1_
  60.5 0.1 combine_3072.5
  60.5 0.0 collective-permute-done.9.arrived_ref
  60.6 1.4 %collective-permute-start.11 = (bf16[2,1,2,1664]{3,2,1,0:T(2,128)(2,1)S(1)}, bf16[2,1,2,1664]{3,2,1,0:T(2,128)(2,1)S(1)}, u32[]{:S(2)}, u32[]{:S(2)}) collective-permute-start(bf16[2,1,2,1664]{3,2,1,0:T(2,128)(2,1)S(1)} %get-tuple-element.80), channel_id=1, source_target_pairs={{0,2},{1,3},{2,0},{3,1},{4,6},{5,7},{6,4},{7,5},{8,10},{9,11},{10,... | collective-permute-start | bytes 39944 | tf_op jit(solution)/shard_map/ppermute | solution.py:49
  61.9 0.9 %collective-permute-start.14 = (bf16[2,16,3072]{2,1,0:T(8,128)(2,1)S(1)}, bf16[2,16,3072]{2,1,0:T(8,128)(2,1)S(1)}, u32[]{:S(2)}, u32[]{:S(2)}) collective-permute-start(bf16[2,16,3072]{2,1,0:T(8,128)(2,1)S(1)} %get-tuple-element.87), channel_id=1, source_target_pairs={{0,8},{4,12},{8,0},{12,4},{16,24},{20,28},{24,16},{28,20},{1,9},{5... | collective-permute-start | bytes 589832 | tf_op jit(solution)/shard_map/ppermute | solution.py:49
  62.8 0.0 collective-permute-done.12.refs_1_
  62.9 1.2 %collective-permute-start.16 = (bf16[1,16,3072]{2,1,0:T(8,128)(2,1)S(1)}, bf16[1,16,3072]{2,1,0:T(8,128)(2,1)S(1)}, u32[]{:S(2)}, u32[]{:S(2)}) collective-permute-start(bf16[1,16,3072]{2,1,0:T(8,128)(2,1)S(1)} %get-tuple-element.91), channel_id=1, source_target_pairs={{0,16},{4,20},{8,24},{12,28},{16,0},{20,4},{24,8},{28,12},{1,17},{... | collective-permute-start | bytes 294920 | tf_op jit(solution)/shard_map/ppermute | solution.py:49
  64.1 0.3 collective-permute-done.11.arrived_ref
  64.4 0.0 collective-permute-start.18
  64.4 1.7 %collective-permute-done.8.refs_1_ = bf16[4,16,2304]{2,1,0:T(8,128)(2,1)S(1)} collective-permute-done((bf16[4,16,2304]{2,1,0:T(8,128)(2,1)S(1)}, bf16[4,16,2304]{2,1,0:T(8,128)(2,1)S(1)}, u32[]{:S(2)}, u32[]{:S(2)}) %collective-permute-start.8) | collective-permute-done | bytes 294944 | tf_op jit(solution)/shard_map/ppermute | solution.py:49
  66.1 1.0 %collective-permute-start.13 = (bf16[2,16,2304]{2,1,0:T(8,128)(2,1)S(1)}, bf16[2,16,2304]{2,1,0:T(8,128)(2,1)S(1)}, u32[]{:S(2)}, u32[]{:S(2)}) collective-permute-start(bf16[2,16,2304]{2,1,0:T(8,128)(2,1)S(1)} %get-tuple-element.86), channel_id=1, source_target_pairs={{0,8},{4,12},{8,0},{12,4},{16,24},{20,28},{24,16},{28,20},{1,9},{5... | collective-permute-start | bytes 442376 | tf_op jit(solution)/shard_map/ppermute | solution.py:49
  67.1 1.4 %collective-permute-done.14.refs_1_ = bf16[2,16,3072]{2,1,0:T(8,128)(2,1)S(1)} collective-permute-done((bf16[2,16,3072]{2,1,0:T(8,128)(2,1)S(1)}, bf16[2,16,3072]{2,1,0:T(8,128)(2,1)S(1)}, u32[]{:S(2)}, u32[]{:S(2)}) %collective-permute-start.14) | collective-permute-done | bytes 196640 | tf_op jit(solution)/shard_map/ppermute | solution.py:49
  68.5 0.1 combine_3072.7
  68.5 0.3 collective-permute-start.17
  68.8 0.0 collective-permute-done.18.arrived_ref
  68.8 0.0 copy-done.1
  68.9 2.1 %attention.1 = bf16[2,6144]{1,0:T(2,128)(2,1)} custom-call(s32[2]{0:T(128)S(1)} %copy-done.3, bf16[1,2,2,1664]{3,2,1,0:T(2,128)(2,1)S(1)} %get-tuple-element.84.refs_2_.own_ref, bf16[1,2,2,1664]{3,2,1,0:T(2,128)(2,1)S(1)} %collective-permute-done.18.arrived_ref, bf16[2,512,256]{2,1,0:T(8,128)(2,1)S(1)} %copy-done.1, bf16[2,512,256]{2,1,0:T(8,128)(2,1)S(1)} %copy-done.2, ...), custom_call_target="tpu_custom_call" | custom-call | flops 25165824 | bytes 1048576 | tf_op jit(solution)/shard_map/attention/pallas_call | solution.py:383
  70.9 1.9 %collective-permute-done.13.refs_1_ = bf16[2,16,2304]{2,1,0:T(8,128)(2,1)S(1)} collective-permute-done((bf16[2,16,2304]{2,1,0:T(8,128)(2,1)S(1)}, bf16[2,16,2304]{2,1,0:T(8,128)(2,1)S(1)}, u32[]{:S(2)}, u32[]{:S(2)}) %collective-permute-start.13) | collective-permute-done | bytes 147488 | tf_op jit(solution)/shard_map/ppermute | solution.py:49
  72.9 1.2 %collective-permute-start.15 = (bf16[1,16,2304]{2,1,0:T(8,128)(2,1)S(1)}, bf16[1,16,2304]{2,1,0:T(8,128)(2,1)S(1)}, u32[]{:S(2)}, u32[]{:S(2)}) collective-permute-start(bf16[1,16,2304]{2,1,0:T(8,128)(2,1)S(1)} %get-tuple-element.90), channel_id=1, source_target_pairs={{0,16},{4,20},{8,24},{12,28},{16,0},{20,4},{24,8},{28,12},{1,17},{... | collective-permute-start | bytes 221192 | tf_op jit(solution)/shard_map/ppermute | solution.py:49
  74.1 0.0 collective-permute-done.16.arrived_ref
  74.1 0.1 finish_3072.2.refs_0_.refs_1_
  74.1 2.3 %collective-permute-done.17.arrived_ref = bf16[1,16,3072]{2,1,0:T(8,128)(2,1)S(1)} collective-permute-done((bf16[1,16,3072]{2,1,0:T(8,128)(2,1)S(1)}, bf16[1,16,3072]{2,1,0:T(8,128)(2,1)S(1)}, u32[]{:S(2)}, u32[]{:S(2)}) %collective-permute-start.17) | collective-permute-done | bytes 98336 | tf_op jit(solution)/shard_map/ppermute | solution.py:49
  76.4 0.1 finish_3072.3.refs_2_.refs_3_
  76.5 2.5 %collective-permute-done.15.arrived_ref = bf16[1,16,2304]{2,1,0:T(8,128)(2,1)S(1)} collective-permute-done((bf16[1,16,2304]{2,1,0:T(8,128)(2,1)S(1)}, bf16[1,16,2304]{2,1,0:T(8,128)(2,1)S(1)}, u32[]{:S(2)}, u32[]{:S(2)}) %collective-permute-start.15) | collective-permute-done | bytes 73760 | tf_op jit(solution)/shard_map/ppermute | solution.py:49
  79.0 0.7 finish_2304.1
  (17 shorter events, 0.3 us)
Async XLA Ops:
  2.1 6.1 %collective-permute-start = (bf16[4,1,2,2304]{3,2,1,0:T(2,128)(2,1)S(1)}, bf16[4,1,2,2304]{3,2,1,0:T(2,128)(2,1)S(1)}, u32[]{:S(2)}, u32[]{:S(2)}) collective-permute-start(bf16[4,1,2,2304]{3,2,1,0:T(2,128)(2,1)S(1)} %get-tuple-element.48.after_ref), channel_id=1, source_target_pairs={{0,4},{4,0},{8,12},{12,8},{16,20},{20,16},{24,28},{28,24},{1,5},{5... | collective-permute-start | bytes 110600 | tf_op jit(solution)/shard_map/ppermute | solution.py:49
  8.2 4.7 %collective-permute-start.1 = (bf16[2,2,2,2304]{3,2,1,0:T(2,128)(2,1)S(1)}, bf16[2,2,2,2304]{3,2,1,0:T(2,128)(2,1)S(1)}, u32[]{:S(2)}, u32[]{:S(2)}) collective-permute-start(bf16[2,2,2,2304]{3,2,1,0:T(2,128)(2,1)S(1)} %get-tuple-element.51.after_ref), channel_id=1, source_target_pairs={{0,8},{4,12},{8,0},{12,4},{16,24},{20,28},{24,16},{28,20},{1,9},{5... | collective-permute-start | bytes 110600 | tf_op jit(solution)/shard_map/ppermute | solution.py:49
  12.9 5.7 %collective-permute-start.2 = (bf16[1,4,2,2304]{3,2,1,0:T(2,128)(2,1)S(1)}, bf16[1,4,2,2304]{3,2,1,0:T(2,128)(2,1)S(1)}, u32[]{:S(2)}, u32[]{:S(2)}) collective-permute-start(bf16[1,4,2,2304]{3,2,1,0:T(2,128)(2,1)S(1)} %get-tuple-element.54.after_ref), channel_id=1, source_target_pairs={{0,16},{4,20},{8,24},{12,28},{16,0},{20,4},{24,8},{28,12},{1,17},{... | collective-permute-start | bytes 110600 | tf_op jit(solution)/shard_map/ppermute | solution.py:49
  18.7 4.6 %collective-permute-start.3 = (bf16[16,2304]{1,0:T(8,128)(2,1)S(1)}, bf16[16,2304]{1,0:T(8,128)(2,1)S(1)}, u32[]{:S(2)}, u32[]{:S(2)}) collective-permute-start(bf16[16,2304]{1,0:T(8,128)(2,1)S(1)} %join_1_2304.1.after_ref), channel_id=1, source_target_pairs={{0,2},{1,3},{2,0},{3,1},{4,6},{5,7},{6,4},{7,5},{8,10},{9,11},{10,... | collective-permute-start | bytes 221192 | tf_op jit(solution)/shard_map/ppermute | solution.py:49
  23.3 4.2 %slice-start = ((s8[7077888]{0:T(1024)(128)(4,1)}), s8[4194304]{0:T(1024)(128)(4,1)S(1)}, s32[]{:S(2)}) async-start(s8[7077888]{0:T(1024)(128)(4,1)} %bitcast.1), calls=%async_computation | async-start | bytes 8388608
  23.3 5.1 %slice-start.1 = ((s8[7077888]{0:T(1024)(128)(4,1)}), s8[2883584]{0:T(1024)(128)(4,1)S(1)}, s32[]{:S(2)}) async-start(s8[7077888]{0:T(1024)(128)(4,1)} %bitcast.1), calls=%async_computation.1 | async-start | bytes 5767168
  23.3 5.1 %copy-start = (bf16[2304,128]{1,0:T(8,128)(2,1)S(1)}, bf16[2304,128]{1,0:T(8,128)(2,1)}, u32[]{:S(2)}) copy-start(bf16[2304,128]{1,0:T(8,128)(2,1)} %refs_4_.1) | copy-start | bytes 1769476
  23.3 3.3 %collective-permute-start.4 = (bf16[32,2304]{1,0:T(8,128)(2,1)S(1)}, bf16[32,2304]{1,0:T(8,128)(2,1)S(1)}, u32[]{:S(2)}, u32[]{:S(2)}) collective-permute-start(bf16[32,2304]{1,0:T(8,128)(2,1)S(1)} %constant_dynamic-update-slice_fusion.after_ref), channel_id=1, source_target_pairs={{0,1},{1,0},{2,3},{3,2},{4,5},{5,4},{6,7},{7,6},{8,9},{9,8},{10,11... | collective-permute-start | bytes 442376 | tf_op jit(solution)/shard_map/ppermute | solution.py:49
  32.5 8.7 %collective-permute-start.6 = (bf16[4,16,2432]{2,1,0:T(8,128)(2,1)S(1)}, bf16[4,16,2432]{2,1,0:T(8,128)(2,1)S(1)}, u32[]{:S(2)}, u32[]{:S(2)}) collective-permute-start(bf16[4,16,2432]{2,1,0:T(8,128)(2,1)S(1)} %get-tuple-element.66), channel_id=1, source_target_pairs={{0,4},{4,0},{8,12},{12,8},{16,20},{20,16},{24,28},{28,24},{1,5},{5... | collective-permute-start | bytes 933896 | tf_op jit(solution)/shard_map/ppermute | solution.py:49
  40.0 11.6 %collective-permute-start.5 = (bf16[4,16,3072]{2,1,0:T(8,128)(2,1)S(1)}, bf16[4,16,3072]{2,1,0:T(8,128)(2,1)S(1)}, u32[]{:S(2)}, u32[]{:S(2)}) collective-permute-start(bf16[4,16,3072]{2,1,0:T(8,128)(2,1)S(1)} %get-tuple-element.65), channel_id=1, source_target_pairs={{0,4},{4,0},{8,12},{12,8},{16,20},{20,16},{24,28},{28,24},{1,5},{5... | collective-permute-start | bytes 1179656 | tf_op jit(solution)/shard_map/ppermute | solution.py:49
  41.3 8.5 %collective-permute-start.7 = (bf16[2,16,2432]{2,1,0:T(8,128)(2,1)S(1)}, bf16[2,16,2432]{2,1,0:T(8,128)(2,1)S(1)}, u32[]{:S(2)}, u32[]{:S(2)}) collective-permute-start(bf16[2,16,2432]{2,1,0:T(8,128)(2,1)S(1)} %get-tuple-element.68), channel_id=1, source_target_pairs={{0,8},{4,12},{8,0},{12,4},{16,24},{20,28},{24,16},{28,20},{1,9},{5... | collective-permute-start | bytes 466952 | tf_op jit(solution)/shard_map/ppermute | solution.py:49
  48.7 11.7 %collective-permute-start.10 = (bf16[4,16,3072]{2,1,0:T(8,128)(2,1)S(1)}, bf16[4,16,3072]{2,1,0:T(8,128)(2,1)S(1)}, u32[]{:S(2)}, u32[]{:S(2)}) collective-permute-start(bf16[4,16,3072]{2,1,0:T(8,128)(2,1)S(1)} %get-tuple-element.77), channel_id=1, source_target_pairs={{0,4},{4,0},{8,12},{12,8},{16,20},{20,16},{24,28},{28,24},{1,5},{5... | collective-permute-start | bytes 1179656 | tf_op jit(solution)/shard_map/ppermute | solution.py:49
  49.8 10.8 %collective-permute-start.9 = (bf16[1,16,2432]{2,1,0:T(8,128)(2,1)S(1)}, bf16[1,16,2432]{2,1,0:T(8,128)(2,1)S(1)}, u32[]{:S(2)}, u32[]{:S(2)}) collective-permute-start(bf16[1,16,2432]{2,1,0:T(8,128)(2,1)S(1)} %get-tuple-element.76), channel_id=1, source_target_pairs={{0,16},{4,20},{8,24},{12,28},{16,0},{20,4},{24,8},{28,12},{1,17},{... | collective-permute-start | bytes 233480 | tf_op jit(solution)/shard_map/ppermute | solution.py:49
  51.7 11.1 %collective-permute-start.12 = (bf16[2,16,3072]{2,1,0:T(8,128)(2,1)S(1)}, bf16[2,16,3072]{2,1,0:T(8,128)(2,1)S(1)}, u32[]{:S(2)}, u32[]{:S(2)}) collective-permute-start(bf16[2,16,3072]{2,1,0:T(8,128)(2,1)S(1)} %get-tuple-element.81), channel_id=1, source_target_pairs={{0,8},{4,12},{8,0},{12,4},{16,24},{20,28},{24,16},{28,20},{1,9},{5... | collective-permute-start | bytes 589832 | tf_op jit(solution)/shard_map/ppermute | solution.py:49
  59.3 6.8 %collective-permute-start.8 = (bf16[4,16,2304]{2,1,0:T(8,128)(2,1)S(1)}, bf16[4,16,2304]{2,1,0:T(8,128)(2,1)S(1)}, u32[]{:S(2)}, u32[]{:S(2)}) collective-permute-start(bf16[4,16,2304]{2,1,0:T(8,128)(2,1)S(1)} %get-tuple-element.75), channel_id=1, source_target_pairs={{0,4},{4,0},{8,12},{12,8},{16,20},{20,16},{24,28},{28,24},{1,5},{5... | collective-permute-start | bytes 884744 | tf_op jit(solution)/shard_map/ppermute | solution.py:49
  60.6 3.8 %collective-permute-start.11 = (bf16[2,1,2,1664]{3,2,1,0:T(2,128)(2,1)S(1)}, bf16[2,1,2,1664]{3,2,1,0:T(2,128)(2,1)S(1)}, u32[]{:S(2)}, u32[]{:S(2)}) collective-permute-start(bf16[2,1,2,1664]{3,2,1,0:T(2,128)(2,1)S(1)} %get-tuple-element.80), channel_id=1, source_target_pairs={{0,2},{1,3},{2,0},{3,1},{4,6},{5,7},{6,4},{7,5},{8,10},{9,11},{10,... | collective-permute-start | bytes 39944 | tf_op jit(solution)/shard_map/ppermute | solution.py:49
  61.9 6.5 %collective-permute-start.14 = (bf16[2,16,3072]{2,1,0:T(8,128)(2,1)S(1)}, bf16[2,16,3072]{2,1,0:T(8,128)(2,1)S(1)}, u32[]{:S(2)}, u32[]{:S(2)}) collective-permute-start(bf16[2,16,3072]{2,1,0:T(8,128)(2,1)S(1)} %get-tuple-element.87), channel_id=1, source_target_pairs={{0,8},{4,12},{8,0},{12,4},{16,24},{20,28},{24,16},{28,20},{1,9},{5... | collective-permute-start | bytes 589832 | tf_op jit(solution)/shard_map/ppermute | solution.py:49
  62.9 11.2 %collective-permute-start.16 = (bf16[1,16,3072]{2,1,0:T(8,128)(2,1)S(1)}, bf16[1,16,3072]{2,1,0:T(8,128)(2,1)S(1)}, u32[]{:S(2)}, u32[]{:S(2)}) collective-permute-start(bf16[1,16,3072]{2,1,0:T(8,128)(2,1)S(1)} %get-tuple-element.91), channel_id=1, source_target_pairs={{0,16},{4,20},{8,24},{12,28},{16,0},{20,4},{24,8},{28,12},{1,17},{... | collective-permute-start | bytes 294920 | tf_op jit(solution)/shard_map/ppermute | solution.py:49
  64.4 4.5 %collective-permute-start.18 = (bf16[1,2,2,1664]{3,2,1,0:T(2,128)(2,1)S(1)}, bf16[1,2,2,1664]{3,2,1,0:T(2,128)(2,1)S(1)}, u32[]{:S(2)}, u32[]{:S(2)}) collective-permute-start(bf16[1,2,2,1664]{3,2,1,0:T(2,128)(2,1)S(1)} %get-tuple-element.93), channel_id=1, source_target_pairs={{0,1},{1,0},{2,3},{3,2},{4,5},{5,4},{6,7},{7,6},{8,9},{9,8},{10,11... | collective-permute-start | bytes 39944 | tf_op jit(solution)/shard_map/ppermute | solution.py:49
  66.1 2.8 %copy-start.1 = (bf16[2,512,256]{2,1,0:T(8,128)(2,1)S(1)}, bf16[2,512,256]{2,1,0:T(8,128)(2,1)}, u32[]{:S(2)}) copy-start(bf16[2,512,256]{2,1,0:T(8,128)(2,1)} %k_ref.1) | copy-start | bytes 1572868
  66.1 2.8 %copy-start.2 = (bf16[2,512,256]{2,1,0:T(8,128)(2,1)S(1)}, bf16[2,512,256]{2,1,0:T(8,128)(2,1)}, u32[]{:S(2)}) copy-start(bf16[2,512,256]{2,1,0:T(8,128)(2,1)} %v_ref.1) | copy-start | bytes 1572868
  66.1 2.8 %copy-start.3 = (s32[2]{0:T(128)S(1)}, s32[2]{0:T(128)}, u32[]{:S(2)}) copy-start(s32[2]{0:T(128)} %lengths_ref.1) | copy-start | bytes 28
  66.1 6.8 %collective-permute-start.13 = (bf16[2,16,2304]{2,1,0:T(8,128)(2,1)S(1)}, bf16[2,16,2304]{2,1,0:T(8,128)(2,1)S(1)}, u32[]{:S(2)}, u32[]{:S(2)}) collective-permute-start(bf16[2,16,2304]{2,1,0:T(8,128)(2,1)S(1)} %get-tuple-element.86), channel_id=1, source_target_pairs={{0,8},{4,12},{8,0},{12,4},{16,24},{20,28},{24,16},{28,20},{1,9},{5... | collective-permute-start | bytes 442376 | tf_op jit(solution)/shard_map/ppermute | solution.py:49
  68.5 7.9 %collective-permute-start.17 = (bf16[1,16,3072]{2,1,0:T(8,128)(2,1)S(1)}, bf16[1,16,3072]{2,1,0:T(8,128)(2,1)S(1)}, u32[]{:S(2)}, u32[]{:S(2)}) collective-permute-start(bf16[1,16,3072]{2,1,0:T(8,128)(2,1)S(1)} %get-tuple-element.92), channel_id=1, source_target_pairs={{0,16},{4,20},{8,24},{12,28},{16,0},{20,4},{24,8},{28,12},{1,17},{... | collective-permute-start | bytes 294920 | tf_op jit(solution)/shard_map/ppermute | solution.py:49
  72.9 6.1 %collective-permute-start.15 = (bf16[1,16,2304]{2,1,0:T(8,128)(2,1)S(1)}, bf16[1,16,2304]{2,1,0:T(8,128)(2,1)S(1)}, u32[]{:S(2)}, u32[]{:S(2)}) collective-permute-start(bf16[1,16,2304]{2,1,0:T(8,128)(2,1)S(1)} %get-tuple-element.90), channel_id=1, source_target_pairs={{0,16},{4,20},{8,24},{12,28},{16,0},{20,4},{24,8},{28,12},{1,17},{... | collective-permute-start | bytes 221192 | tf_op jit(solution)/shard_map/ppermute | solution.py:49

commit v4 on v3

--- a/solution.py
+++ b/solution.py
@@ -410,7 +410,7 @@
         taken = [sum(p.shape[1] for p in held) // tile for held in pieces]
         left = [edges[i + 1] - edges[i] - taken[i] for i in range(len(flat))]
         portion = max(range(len(flat)), key=lambda i: left[i])
-        count = min(AHEAD, left[portion])
+        count = min(1 if axis == "gy" and bit == 1 else AHEAD, left[portion])
         if count:
             piece = fetch(w_gate, (edges[portion] + taken[portion]) * tile, count * tile, send)
             piece, keep = lax.optimization_barrier((piece, keep))

time: 80.1 us -> 80 us (level)
    pallas_call x5, Pallas kernels: 15.3 us -> 14.2 us  [fetch(): pl.pallas_call(functools.partial(fetch_kernel, first), out_shape=pltpu.VM...]
    pallas_call x4, Pallas kernels: 23.4 us -> 24.3 us  [partials(): pl.pallas_call(functools.partial(partials_kernel, slots, first, count, ti...]
where the time goes in v4:
time: 80 us; the launch traced here: 79.7 us
  Pallas kernels  43.4 us (54%)
  starting transfers between devices  23.2 us (29%)
  waiting for transfers between devices  10.2 us (13%)
  local copies, waits for them, and re-layouts  1.93 us (2%)
  between operations  0.9 us (1%)
    pallas_call x4, Pallas kernels, partials(): pl.pallas_call(functools.partial(partials_kernel, slots, first, count, ti...  24.3 us
    ppermute x19, starting transfers between devices, swap(): return lax.ppermute(x, axis, [(i, i ^ bit) for i in range(size)])  23.2 us
    pallas_call x5, Pallas kernels, fetch(): pl.pallas_call(functools.partial(fetch_kernel, first), out_shape=pltpu.VM...  14.2 us
    ppermute x19, waiting for transfers between devices, swap(): return lax.ppermute(x, axis, [(i, i ^ bit) for i in range(size)])  10.2 us
    pallas_call x1, Pallas kernels, attention(): pl.pallas_call(functools.partial(attention_kernel, order), out_shape=shap...  2.09 us
    unnamed x13, local copies, waits for them, and re-layouts  1.92 us
  transfers between devices with their start and end apart: 19, of which 6 were waited for; matrix products, arithmetic and copies ran while one was open for 0% of the time, Pallas kernels for 47%

profile of v4, /device:TPU:0, one launch (start us, length us, event | category | flops | bytes accessed | tf_op | source)
XLA Modules:
  0.0 79.7 jit_solution(5433246849705530504)
XLA Ops:
  0.6 1.5 %layer_norm.1 = (bf16[4,1,2,2304]{3,2,1,0:T(2,128)(2,1)S(1)}, bf16[4,1,2,2304]{3,2,1,0:T(2,128)(2,1)S(1)}) custom-call(bf16[2,18432]{1,0:T(2,128)(2,1)} %x_hbm.1, f32[1,18432]{1,0:T(1,128)} %bitcast.3), custom_call_target="tpu_custom_call" | custom-call | flops 20000000000 | bytes 1000000 | tf_op jit(solution)/shard_map/layer_norm/pallas_call | solution.py:82
  2.1 3.0 %collective-permute-start = (bf16[4,1,2,2304]{3,2,1,0:T(2,128)(2,1)S(1)}, bf16[4,1,2,2304]{3,2,1,0:T(2,128)(2,1)S(1)}, u32[]{:S(2)}, u32[]{:S(2)}) collective-permute-start(bf16[4,1,2,2304]{3,2,1,0:T(2,128)(2,1)S(1)} %get-tuple-element.48.after_ref), channel_id=1, source_target_pairs={{0,4},{4,0},{8,12},{12,8},{16,20},{20,16},{24,28},{28,24},{1,5},{5... | collective-permute-start | bytes 110600 | tf_op jit(solution)/shard_map/ppermute | solution.py:49
  5.2 3.0 %fetch_768.1.refs_3_ = bf16[2304,1536]{1,0:T(8,128)(2,1)S(1)} custom-call(bf16[2304,9216]{1,0:T(8,128)(2,1)} %refs_1_.7, bf16[4,1,2,2304]{3,2,1,0:T(2,128)(2,1)S(1)} %get-tuple-element.48.after_ref), custom_call_target="tpu_custom_call" | custom-call | bytes 7077888 | tf_op jit(solution)/shard_map/fetch_768/pallas_call | solution.py:179
  8.2 0.0 collective-permute-done.arrived_ref
  8.2 1.6 %collective-permute-start.1 = (bf16[2,2,2,2304]{3,2,1,0:T(2,128)(2,1)S(1)}, bf16[2,2,2,2304]{3,2,1,0:T(2,128)(2,1)S(1)}, u32[]{:S(2)}, u32[]{:S(2)}) collective-permute-start(bf16[2,2,2,2304]{3,2,1,0:T(2,128)(2,1)S(1)} %get-tuple-element.51.after_ref), channel_id=1, source_target_pairs={{0,8},{4,12},{8,0},{12,4},{16,24},{20,28},{24,16},{28,20},{1,9},{5... | collective-permute-start | bytes 110600 | tf_op jit(solution)/shard_map/ppermute | solution.py:49
  9.8 3.0 %fetch_3840.1.refs_3_ = bf16[2304,1536]{1,0:T(8,128)(2,1)S(1)} custom-call(bf16[2304,9216]{1,0:T(8,128)(2,1)} %refs_1_.7, bf16[2,2,2,2304]{3,2,1,0:T(2,128)(2,1)S(1)} %get-tuple-element.51.after_ref), custom_call_target="tpu_custom_call" | custom-call | bytes 7077888 | tf_op jit(solution)/shard_map/fetch_3840/pallas_call | solution.py:179
  12.9 0.0 collective-permute-done.1.arrived_ref
  12.9 2.7 %collective-permute-start.2 = (bf16[1,4,2,2304]{3,2,1,0:T(2,128)(2,1)S(1)}, bf16[1,4,2,2304]{3,2,1,0:T(2,128)(2,1)S(1)}, u32[]{:S(2)}, u32[]{:S(2)}) collective-permute-start(bf16[1,4,2,2304]{3,2,1,0:T(2,128)(2,1)S(1)} %get-tuple-element.54.after_ref), channel_id=1, source_target_pairs={{0,16},{4,20},{8,24},{12,28},{16,0},{20,4},{24,8},{28,12},{1,17},{... | collective-permute-start | bytes 110600 | tf_op jit(solution)/shard_map/ppermute | solution.py:49
  15.6 3.0 %fetch_6912.1.refs_3_ = bf16[2304,1536]{1,0:T(8,128)(2,1)S(1)} custom-call(bf16[2304,9216]{1,0:T(8,128)(2,1)} %refs_1_.7, bf16[1,4,2,2304]{3,2,1,0:T(2,128)(2,1)S(1)} %get-tuple-element.54.after_ref), custom_call_target="tpu_custom_call" | custom-call | bytes 7077888 | tf_op jit(solution)/shard_map/fetch_6912/pallas_call | solution.py:179
  18.6 0.0 collective-permute-done.2.arrived_ref
  18.6 0.1 join_1_2304.1.after_ref
  18.7 1.6 %collective-permute-start.3 = (bf16[16,2304]{1,0:T(8,128)(2,1)S(1)}, bf16[16,2304]{1,0:T(8,128)(2,1)S(1)}, u32[]{:S(2)}, u32[]{:S(2)}) collective-permute-start(bf16[16,2304]{1,0:T(8,128)(2,1)S(1)} %join_1_2304.1.after_ref), channel_id=1, source_target_pairs={{0,2},{1,3},{2,0},{3,1},{4,6},{5,7},{6,4},{7,5},{8,10},{9,11},{10,... | collective-permute-start | bytes 221192 | tf_op jit(solution)/shard_map/ppermute | solution.py:49
  20.2 3.0 %fetch_2304.1.refs_4_ = bf16[2304,1536]{1,0:T(8,128)(2,1)S(1)} custom-call(bf16[2304,9216]{1,0:T(8,128)(2,1)} %refs_1_.7, bf16[16,2304]{1,0:T(8,128)(2,1)S(1)} %join_1_2304.1.after_ref), custom_call_target="tpu_custom_call" | custom-call | bytes 7077888 | tf_op jit(solution)/shard_map/fetch_2304/pallas_call | solution.py:179
  23.3 0.0 collective-permute-done.3
  23.3 0.0 slice-start
  23.3 0.0 slice-start.1
  23.3 0.0 copy-start
  23.3 0.1 collective-permute-start.4
  23.4 2.2 %fetch_5376.1.refs_4_ = bf16[2304,768]{1,0:T(8,128)(2,1)S(1)} custom-call(bf16[2304,9216]{1,0:T(8,128)(2,1)} %refs_1_.7, bf16[32,2304]{1,0:T(8,128)(2,1)S(1)} %constant_dynamic-update-slice_fusion.after_ref), custom_call_target="tpu_custom_call" | custom-call | bytes 3538944 | tf_op jit(solution)/shard_map/fetch_5376/pallas_call | solution.py:179
  25.6 0.0 collective-permute-done.4
  25.6 0.9 %slice-done = s8[4194304]{0:T(1024)(128)(4,1)S(1)} async-done(((s8[7077888]{0:T(1024)(128)(4,1)}), s8[4194304]{0:T(1024)(128)(4,1)S(1)}, s32[]{:S(2)}) %slice-start) | async-done | bytes 4194328
  26.5 0.9 %slice-done.1 = s8[2883584]{0:T(1024)(128)(4,1)S(1)} async-done(((s8[7077888]{0:T(1024)(128)(4,1)}), s8[2883584]{0:T(1024)(128)(4,1)S(1)}, s32[]{:S(2)}) %slice-start.1) | async-done | bytes 2883608
  27.5 0.0 copy-done
  27.5 4.1 %partials_0.1 = (bf16[64,2304]{1,0:T(8,128)(2,1)S(1)}, bf16[4,16,2432]{2,1,0:T(8,128)(2,1)S(1)}, f32[4,16,2432]{2,1,0:T(8,128)S(1)}) custom-call(bf16[64,2304]{1,0:T(8,128)(2,1)S(1)} %pad_maximum_fusion.refs_0_, bf16[2304,9216]{1,0:T(8,128)(2,1)} %refs_1_.7, bf16[2304,9216]{1,0:T(8,128)(2,1)} %refs_2_.7, bf16[2304,1536]{1,0:T(8,128)(2,1)S(1)} %bitcast.2, ...), custom_call_target="tpu_custom_call" | custom-call | flops 1434451968 | bytes 22413312 | tf_op jit(solution)/shard_map/partials_0/pallas_call | solution.py:251
  31.6 1.0 %collective-permute-start.6 = (bf16[4,16,2432]{2,1,0:T(8,128)(2,1)S(1)}, bf16[4,16,2432]{2,1,0:T(8,128)(2,1)S(1)}, u32[]{:S(2)}, u32[]{:S(2)}) collective-permute-start(bf16[4,16,2432]{2,1,0:T(8,128)(2,1)S(1)} %get-tuple-element.66), channel_id=1, source_target_pairs={{0,4},{4,0},{8,12},{12,8},{16,20},{20,16},{24,28},{28,24},{1,5},{5... | collective-permute-start | bytes 933896 | tf_op jit(solution)/shard_map/ppermute | solution.py:49
  32.6 6.5 %partials_1.1 = (bf16[4,16,3072]{2,1,0:T(8,128)(2,1)S(1)}, f32[4,16,3072]{2,1,0:T(8,128)S(1)}) custom-call(bf16[64,2304]{1,0:T(8,128)(2,1)S(1)} %get-tuple-element.59.refs_0_, bf16[2304,9216]{1,0:T(8,128)(2,1)} %refs_1_.7, bf16[2304,9216]{1,0:T(8,128)(2,1)} %refs_2_.7, bf16[2304,1536]{1,0:T(8,128)(2,1)S(1)} %fetch_768.1.refs_3_, ...), custom_call_target="tpu_custom_call" | custom-call | flops 1811939328 | bytes 28311552 | tf_op jit(solution)/shard_map/partials_1/pallas_call | solution.py:251
  39.1 1.2 %collective-permute-start.5 = (bf16[4,16,3072]{2,1,0:T(8,128)(2,1)S(1)}, bf16[4,16,3072]{2,1,0:T(8,128)(2,1)S(1)}, u32[]{:S(2)}, u32[]{:S(2)}) collective-permute-start(bf16[4,16,3072]{2,1,0:T(8,128)(2,1)S(1)} %get-tuple-element.65), channel_id=1, source_target_pairs={{0,4},{4,0},{8,12},{12,8},{16,20},{20,16},{24,28},{28,24},{1,5},{5... | collective-permute-start | bytes 1179656 | tf_op jit(solution)/shard_map/ppermute | solution.py:49
  40.2 0.0 collective-permute-done.6.refs_1_.refs_6_
  40.2 0.1 combine_2432.2
  40.3 1.0 %collective-permute-start.7 = (bf16[2,16,2432]{2,1,0:T(8,128)(2,1)S(1)}, bf16[2,16,2432]{2,1,0:T(8,128)(2,1)S(1)}, u32[]{:S(2)}, u32[]{:S(2)}) collective-permute-start(bf16[2,16,2432]{2,1,0:T(8,128)(2,1)S(1)} %get-tuple-element.68), channel_id=1, source_target_pairs={{0,8},{4,12},{8,0},{12,4},{16,24},{20,28},{24,16},{28,20},{1,9},{5... | collective-permute-start | bytes 466952 | tf_op jit(solution)/shard_map/ppermute | solution.py:49
  41.3 7.4 %partials_5.1 = (bf16[4,16,3072]{2,1,0:T(8,128)(2,1)S(1)}, f32[4,16,3072]{2,1,0:T(8,128)S(1)}) custom-call(bf16[64,2304]{1,0:T(8,128)(2,1)S(1)} %get-tuple-element.59.refs_0_, bf16[2304,9216]{1,0:T(8,128)(2,1)} %refs_1_.7, bf16[2304,9216]{1,0:T(8,128)(2,1)} %refs_2_.7, bf16[2304,1536]{1,0:T(8,128)(2,1)S(1)} %fetch_3840.1.refs_3_, ...), custom_call_target="tpu_custom_call" | custom-call | flops 1811939328 | bytes 28311552 | tf_op jit(solution)/shard_map/partials_5/pallas_call | solution.py:251
  48.7 1.0 %collective-permute-start.10 = (bf16[4,16,3072]{2,1,0:T(8,128)(2,1)S(1)}, bf16[4,16,3072]{2,1,0:T(8,128)(2,1)S(1)}, u32[]{:S(2)}, u32[]{:S(2)}) collective-permute-start(bf16[4,16,3072]{2,1,0:T(8,128)(2,1)S(1)} %get-tuple-element.77), channel_id=1, source_target_pairs={{0,4},{4,0},{8,12},{12,8},{16,20},{20,16},{24,28},{28,24},{1,5},{5... | collective-permute-start | bytes 1179656 | tf_op jit(solution)/shard_map/ppermute | solution.py:49
  49.7 0.0 collective-permute-done.7.refs_1_
  49.7 1.9 %collective-permute-start.9 = (bf16[1,16,2432]{2,1,0:T(8,128)(2,1)S(1)}, bf16[1,16,2432]{2,1,0:T(8,128)(2,1)S(1)}, u32[]{:S(2)}, u32[]{:S(2)}) collective-permute-start(bf16[1,16,2432]{2,1,0:T(8,128)(2,1)S(1)} %get-tuple-element.76), channel_id=1, source_target_pairs={{0,16},{4,20},{8,24},{12,28},{16,0},{20,4},{24,8},{28,12},{1,17},{... | collective-permute-start | bytes 233480 | tf_op jit(solution)/shard_map/ppermute | solution.py:49
  51.6 0.0 collective-permute-done.5.refs_1_.refs_5_
  51.6 0.1 combine_3072.4
  51.7 1.2 %collective-permute-start.12 = (bf16[2,16,3072]{2,1,0:T(8,128)(2,1)S(1)}, bf16[2,16,3072]{2,1,0:T(8,128)(2,1)S(1)}, u32[]{:S(2)}, u32[]{:S(2)}) collective-permute-start(bf16[2,16,3072]{2,1,0:T(8,128)(2,1)S(1)} %get-tuple-element.81), channel_id=1, source_target_pairs={{0,8},{4,12},{8,0},{12,4},{16,24},{20,28},{24,16},{28,20},{1,9},{5... | collective-permute-start | bytes 589832 | tf_op jit(solution)/shard_map/ppermute | solution.py:49
  52.8 6.4 %partials_9.1 = (bf16[4,16,2304]{2,1,0:T(8,128)(2,1)S(1)}, f32[4,16,2304]{2,1,0:T(8,128)S(1)}) custom-call(bf16[64,2304]{1,0:T(8,128)(2,1)S(1)} %get-tuple-element.59.refs_0_, bf16[2304,9216]{1,0:T(8,128)(2,1)} %refs_1_.7, bf16[2304,9216]{1,0:T(8,128)(2,1)} %refs_2_.7, bf16[2304,1536]{1,0:T(8,128)(2,1)S(1)} %fetch_6912.1.refs_3_, ...), custom_call_target="tpu_custom_call" | custom-call | flops 1358954496 | bytes 21233664 | tf_op jit(solution)/shard_map/partials_9/pallas_call | solution.py:251
  59.2 1.2 %collective-permute-start.8 = (bf16[4,16,2304]{2,1,0:T(8,128)(2,1)S(1)}, bf16[4,16,2304]{2,1,0:T(8,128)(2,1)S(1)}, u32[]{:S(2)}, u32[]{:S(2)}) collective-permute-start(bf16[4,16,2304]{2,1,0:T(8,128)(2,1)S(1)} %get-tuple-element.75), channel_id=1, source_target_pairs={{0,4},{4,0},{8,12},{12,8},{16,20},{20,16},{24,28},{28,24},{1,5},{5... | collective-permute-start | bytes 884744 | tf_op jit(solution)/shard_map/ppermute | solution.py:49
  60.4 0.0 collective-permute-done.10.refs_1_
  60.4 0.1 combine_3072.5
  60.5 0.0 collective-permute-done.9.arrived_ref
  60.5 1.4 %collective-permute-start.11 = (bf16[2,1,2,1664]{3,2,1,0:T(2,128)(2,1)S(1)}, bf16[2,1,2,1664]{3,2,1,0:T(2,128)(2,1)S(1)}, u32[]{:S(2)}, u32[]{:S(2)}) collective-permute-start(bf16[2,1,2,1664]{3,2,1,0:T(2,128)(2,1)S(1)} %get-tuple-element.80), channel_id=1, source_target_pairs={{0,2},{1,3},{2,0},{3,1},{4,6},{5,7},{6,4},{7,5},{8,10},{9,11},{10,... | collective-permute-start | bytes 39944 | tf_op jit(solution)/shard_map/ppermute | solution.py:49
  61.9 0.9 %collective-permute-start.14 = (bf16[2,16,3072]{2,1,0:T(8,128)(2,1)S(1)}, bf16[2,16,3072]{2,1,0:T(8,128)(2,1)S(1)}, u32[]{:S(2)}, u32[]{:S(2)}) collective-permute-start(bf16[2,16,3072]{2,1,0:T(8,128)(2,1)S(1)} %get-tuple-element.87), channel_id=1, source_target_pairs={{0,8},{4,12},{8,0},{12,4},{16,24},{20,28},{24,16},{28,20},{1,9},{5... | collective-permute-start | bytes 589832 | tf_op jit(solution)/shard_map/ppermute | solution.py:49
  62.8 0.0 collective-permute-done.12.refs_1_
  62.8 1.2 %collective-permute-start.16 = (bf16[1,16,3072]{2,1,0:T(8,128)(2,1)S(1)}, bf16[1,16,3072]{2,1,0:T(8,128)(2,1)S(1)}, u32[]{:S(2)}, u32[]{:S(2)}) collective-permute-start(bf16[1,16,3072]{2,1,0:T(8,128)(2,1)S(1)} %get-tuple-element.91), channel_id=1, source_target_pairs={{0,16},{4,20},{8,24},{12,28},{16,0},{20,4},{24,8},{28,12},{1,17},{... | collective-permute-start | bytes 294920 | tf_op jit(solution)/shard_map/ppermute | solution.py:49
  64.0 0.3 collective-permute-done.11.arrived_ref
  64.3 0.0 collective-permute-start.18
  64.3 1.7 %collective-permute-done.8.refs_1_ = bf16[4,16,2304]{2,1,0:T(8,128)(2,1)S(1)} collective-permute-done((bf16[4,16,2304]{2,1,0:T(8,128)(2,1)S(1)}, bf16[4,16,2304]{2,1,0:T(8,128)(2,1)S(1)}, u32[]{:S(2)}, u32[]{:S(2)}) %collective-permute-start.8) | collective-permute-done | bytes 294944 | tf_op jit(solution)/shard_map/ppermute | solution.py:49
  66.1 1.0 %collective-permute-start.13 = (bf16[2,16,2304]{2,1,0:T(8,128)(2,1)S(1)}, bf16[2,16,2304]{2,1,0:T(8,128)(2,1)S(1)}, u32[]{:S(2)}, u32[]{:S(2)}) collective-permute-start(bf16[2,16,2304]{2,1,0:T(8,128)(2,1)S(1)} %get-tuple-element.86), channel_id=1, source_target_pairs={{0,8},{4,12},{8,0},{12,4},{16,24},{20,28},{24,16},{28,20},{1,9},{5... | collective-permute-start | bytes 442376 | tf_op jit(solution)/shard_map/ppermute | solution.py:49
  67.0 1.4 %collective-permute-done.14.refs_1_ = bf16[2,16,3072]{2,1,0:T(8,128)(2,1)S(1)} collective-permute-done((bf16[2,16,3072]{2,1,0:T(8,128)(2,1)S(1)}, bf16[2,16,3072]{2,1,0:T(8,128)(2,1)S(1)}, u32[]{:S(2)}, u32[]{:S(2)}) %collective-permute-start.14) | collective-permute-done | bytes 196640 | tf_op jit(solution)/shard_map/ppermute | solution.py:49
  68.4 0.1 combine_3072.7
  68.5 0.3 collective-permute-start.17
  68.8 0.0 collective-permute-done.18.arrived_ref
  68.8 0.0 copy-done.1
  68.8 2.1 %attention.1 = bf16[2,6144]{1,0:T(2,128)(2,1)} custom-call(s32[2]{0:T(128)S(1)} %copy-done.3, bf16[1,2,2,1664]{3,2,1,0:T(2,128)(2,1)S(1)} %get-tuple-element.84.refs_2_.own_ref, bf16[1,2,2,1664]{3,2,1,0:T(2,128)(2,1)S(1)} %collective-permute-done.18.arrived_ref, bf16[2,512,256]{2,1,0:T(8,128)(2,1)S(1)} %copy-done.1, bf16[2,512,256]{2,1,0:T(8,128)(2,1)S(1)} %copy-done.2, ...), custom_call_target="tpu_custom_call" | custom-call | flops 25165824 | bytes 1048576 | tf_op jit(solution)/shard_map/attention/pallas_call | solution.py:383
  70.9 1.9 %collective-permute-done.13.refs_1_ = bf16[2,16,2304]{2,1,0:T(8,128)(2,1)S(1)} collective-permute-done((bf16[2,16,2304]{2,1,0:T(8,128)(2,1)S(1)}, bf16[2,16,2304]{2,1,0:T(8,128)(2,1)S(1)}, u32[]{:S(2)}, u32[]{:S(2)}) %collective-permute-start.13) | collective-permute-done | bytes 147488 | tf_op jit(solution)/shard_map/ppermute | solution.py:49
  72.8 1.2 %collective-permute-start.15 = (bf16[1,16,2304]{2,1,0:T(8,128)(2,1)S(1)}, bf16[1,16,2304]{2,1,0:T(8,128)(2,1)S(1)}, u32[]{:S(2)}, u32[]{:S(2)}) collective-permute-start(bf16[1,16,2304]{2,1,0:T(8,128)(2,1)S(1)} %get-tuple-element.90), channel_id=1, source_target_pairs={{0,16},{4,20},{8,24},{12,28},{16,0},{20,4},{24,8},{28,12},{1,17},{... | collective-permute-start | bytes 221192 | tf_op jit(solution)/shard_map/ppermute | solution.py:49
  74.0 0.0 collective-permute-done.16.arrived_ref
  74.0 0.1 finish_3072.2.refs_0_.refs_1_
  74.1 2.3 %collective-permute-done.17.arrived_ref = bf16[1,16,3072]{2,1,0:T(8,128)(2,1)S(1)} collective-permute-done((bf16[1,16,3072]{2,1,0:T(8,128)(2,1)S(1)}, bf16[1,16,3072]{2,1,0:T(8,128)(2,1)S(1)}, u32[]{:S(2)}, u32[]{:S(2)}) %collective-permute-start.17) | collective-permute-done | bytes 98336 | tf_op jit(solution)/shard_map/ppermute | solution.py:49
  76.4 0.1 finish_3072.3.refs_2_.refs_3_
  76.4 2.5 %collective-permute-done.15.arrived_ref = bf16[1,16,2304]{2,1,0:T(8,128)(2,1)S(1)} collective-permute-done((bf16[1,16,2304]{2,1,0:T(8,128)(2,1)S(1)}, bf16[1,16,2304]{2,1,0:T(8,128)(2,1)S(1)}, u32[]{:S(2)}, u32[]{:S(2)}) %collective-permute-start.15) | collective-permute-done | bytes 73760 | tf_op jit(solution)/shard_map/ppermute | solution.py:49
  78.9 0.7 finish_2304.1
  (17 shorter events, 0.3 us)
Async XLA Ops:
  2.1 6.1 %collective-permute-start = (bf16[4,1,2,2304]{3,2,1,0:T(2,128)(2,1)S(1)}, bf16[4,1,2,2304]{3,2,1,0:T(2,128)(2,1)S(1)}, u32[]{:S(2)}, u32[]{:S(2)}) collective-permute-start(bf16[4,1,2,2304]{3,2,1,0:T(2,128)(2,1)S(1)} %get-tuple-element.48.after_ref), channel_id=1, source_target_pairs={{0,4},{4,0},{8,12},{12,8},{16,20},{20,16},{24,28},{28,24},{1,5},{5... | collective-permute-start | bytes 110600 | tf_op jit(solution)/shard_map/ppermute | solution.py:49
  8.2 4.7 %collective-permute-start.1 = (bf16[2,2,2,2304]{3,2,1,0:T(2,128)(2,1)S(1)}, bf16[2,2,2,2304]{3,2,1,0:T(2,128)(2,1)S(1)}, u32[]{:S(2)}, u32[]{:S(2)}) collective-permute-start(bf16[2,2,2,2304]{3,2,1,0:T(2,128)(2,1)S(1)} %get-tuple-element.51.after_ref), channel_id=1, source_target_pairs={{0,8},{4,12},{8,0},{12,4},{16,24},{20,28},{24,16},{28,20},{1,9},{5... | collective-permute-start | bytes 110600 | tf_op jit(solution)/shard_map/ppermute | solution.py:49
  12.9 5.7 %collective-permute-start.2 = (bf16[1,4,2,2304]{3,2,1,0:T(2,128)(2,1)S(1)}, bf16[1,4,2,2304]{3,2,1,0:T(2,128)(2,1)S(1)}, u32[]{:S(2)}, u32[]{:S(2)}) collective-permute-start(bf16[1,4,2,2304]{3,2,1,0:T(2,128)(2,1)S(1)} %get-tuple-element.54.after_ref), channel_id=1, source_target_pairs={{0,16},{4,20},{8,24},{12,28},{16,0},{20,4},{24,8},{28,12},{1,17},{... | collective-permute-start | bytes 110600 | tf_op jit(solution)/shard_map/ppermute | solution.py:49
  18.7 4.6 %collective-permute-start.3 = (bf16[16,2304]{1,0:T(8,128)(2,1)S(1)}, bf16[16,2304]{1,0:T(8,128)(2,1)S(1)}, u32[]{:S(2)}, u32[]{:S(2)}) collective-permute-start(bf16[16,2304]{1,0:T(8,128)(2,1)S(1)} %join_1_2304.1.after_ref), channel_id=1, source_target_pairs={{0,2},{1,3},{2,0},{3,1},{4,6},{5,7},{6,4},{7,5},{8,10},{9,11},{10,... | collective-permute-start | bytes 221192 | tf_op jit(solution)/shard_map/ppermute | solution.py:49
  23.3 3.3 %slice-start = ((s8[7077888]{0:T(1024)(128)(4,1)}), s8[4194304]{0:T(1024)(128)(4,1)S(1)}, s32[]{:S(2)}) async-start(s8[7077888]{0:T(1024)(128)(4,1)} %bitcast.1), calls=%async_computation | async-start | bytes 8388608
  23.3 4.2 %slice-start.1 = ((s8[7077888]{0:T(1024)(128)(4,1)}), s8[2883584]{0:T(1024)(128)(4,1)S(1)}, s32[]{:S(2)}) async-start(s8[7077888]{0:T(1024)(128)(4,1)} %bitcast.1), calls=%async_computation.1 | async-start | bytes 5767168
  23.3 4.2 %copy-start = (bf16[2304,128]{1,0:T(8,128)(2,1)S(1)}, bf16[2304,128]{1,0:T(8,128)(2,1)}, u32[]{:S(2)}) copy-start(bf16[2304,128]{1,0:T(8,128)(2,1)} %refs_4_.1) | copy-start | bytes 1769476
  23.3 2.3 %collective-permute-start.4 = (bf16[32,2304]{1,0:T(8,128)(2,1)S(1)}, bf16[32,2304]{1,0:T(8,128)(2,1)S(1)}, u32[]{:S(2)}, u32[]{:S(2)}) collective-permute-start(bf16[32,2304]{1,0:T(8,128)(2,1)S(1)} %constant_dynamic-update-slice_fusion.after_ref), channel_id=1, source_target_pairs={{0,1},{1,0},{2,3},{3,2},{4,5},{5,4},{6,7},{7,6},{8,9},{9,8},{10,11... | collective-permute-start | bytes 442376 | tf_op jit(solution)/shard_map/ppermute | solution.py:49
  31.6 8.7 %collective-permute-start.6 = (bf16[4,16,2432]{2,1,0:T(8,128)(2,1)S(1)}, bf16[4,16,2432]{2,1,0:T(8,128)(2,1)S(1)}, u32[]{:S(2)}, u32[]{:S(2)}) collective-permute-start(bf16[4,16,2432]{2,1,0:T(8,128)(2,1)S(1)} %get-tuple-element.66), channel_id=1, source_target_pairs={{0,4},{4,0},{8,12},{12,8},{16,20},{20,16},{24,28},{28,24},{1,5},{5... | collective-permute-start | bytes 933896 | tf_op jit(solution)/shard_map/ppermute | solution.py:49
  39.1 12.5 %collective-permute-start.5 = (bf16[4,16,3072]{2,1,0:T(8,128)(2,1)S(1)}, bf16[4,16,3072]{2,1,0:T(8,128)(2,1)S(1)}, u32[]{:S(2)}, u32[]{:S(2)}) collective-permute-start(bf16[4,16,3072]{2,1,0:T(8,128)(2,1)S(1)} %get-tuple-element.65), channel_id=1, source_target_pairs={{0,4},{4,0},{8,12},{12,8},{16,20},{20,16},{24,28},{28,24},{1,5},{5... | collective-permute-start | bytes 1179656 | tf_op jit(solution)/shard_map/ppermute | solution.py:49
  40.3 9.3 %collective-permute-start.7 = (bf16[2,16,2432]{2,1,0:T(8,128)(2,1)S(1)}, bf16[2,16,2432]{2,1,0:T(8,128)(2,1)S(1)}, u32[]{:S(2)}, u32[]{:S(2)}) collective-permute-start(bf16[2,16,2432]{2,1,0:T(8,128)(2,1)S(1)} %get-tuple-element.68), channel_id=1, source_target_pairs={{0,8},{4,12},{8,0},{12,4},{16,24},{20,28},{24,16},{28,20},{1,9},{5... | collective-permute-start | bytes 466952 | tf_op jit(solution)/shard_map/ppermute | solution.py:49
  48.7 11.7 %collective-permute-start.10 = (bf16[4,16,3072]{2,1,0:T(8,128)(2,1)S(1)}, bf16[4,16,3072]{2,1,0:T(8,128)(2,1)S(1)}, u32[]{:S(2)}, u32[]{:S(2)}) collective-permute-start(bf16[4,16,3072]{2,1,0:T(8,128)(2,1)S(1)} %get-tuple-element.77), channel_id=1, source_target_pairs={{0,4},{4,0},{8,12},{12,8},{16,20},{20,16},{24,28},{28,24},{1,5},{5... | collective-permute-start | bytes 1179656 | tf_op jit(solution)/shard_map/ppermute | solution.py:49
  49.7 10.8 %collective-permute-start.9 = (bf16[1,16,2432]{2,1,0:T(8,128)(2,1)S(1)}, bf16[1,16,2432]{2,1,0:T(8,128)(2,1)S(1)}, u32[]{:S(2)}, u32[]{:S(2)}) collective-permute-start(bf16[1,16,2432]{2,1,0:T(8,128)(2,1)S(1)} %get-tuple-element.76), channel_id=1, source_target_pairs={{0,16},{4,20},{8,24},{12,28},{16,0},{20,4},{24,8},{28,12},{1,17},{... | collective-permute-start | bytes 233480 | tf_op jit(solution)/shard_map/ppermute | solution.py:49
  51.7 11.1 %collective-permute-start.12 = (bf16[2,16,3072]{2,1,0:T(8,128)(2,1)S(1)}, bf16[2,16,3072]{2,1,0:T(8,128)(2,1)S(1)}, u32[]{:S(2)}, u32[]{:S(2)}) collective-permute-start(bf16[2,16,3072]{2,1,0:T(8,128)(2,1)S(1)} %get-tuple-element.81), channel_id=1, source_target_pairs={{0,8},{4,12},{8,0},{12,4},{16,24},{20,28},{24,16},{28,20},{1,9},{5... | collective-permute-start | bytes 589832 | tf_op jit(solution)/shard_map/ppermute | solution.py:49
  59.2 6.8 %collective-permute-start.8 = (bf16[4,16,2304]{2,1,0:T(8,128)(2,1)S(1)}, bf16[4,16,2304]{2,1,0:T(8,128)(2,1)S(1)}, u32[]{:S(2)}, u32[]{:S(2)}) collective-permute-start(bf16[4,16,2304]{2,1,0:T(8,128)(2,1)S(1)} %get-tuple-element.75), channel_id=1, source_target_pairs={{0,4},{4,0},{8,12},{12,8},{16,20},{20,16},{24,28},{28,24},{1,5},{5... | collective-permute-start | bytes 884744 | tf_op jit(solution)/shard_map/ppermute | solution.py:49
  60.5 3.8 %collective-permute-start.11 = (bf16[2,1,2,1664]{3,2,1,0:T(2,128)(2,1)S(1)}, bf16[2,1,2,1664]{3,2,1,0:T(2,128)(2,1)S(1)}, u32[]{:S(2)}, u32[]{:S(2)}) collective-permute-start(bf16[2,1,2,1664]{3,2,1,0:T(2,128)(2,1)S(1)} %get-tuple-element.80), channel_id=1, source_target_pairs={{0,2},{1,3},{2,0},{3,1},{4,6},{5,7},{6,4},{7,5},{8,10},{9,11},{10,... | collective-permute-start | bytes 39944 | tf_op jit(solution)/shard_map/ppermute | solution.py:49
  61.9 6.5 %collective-permute-start.14 = (bf16[2,16,3072]{2,1,0:T(8,128)(2,1)S(1)}, bf16[2,16,3072]{2,1,0:T(8,128)(2,1)S(1)}, u32[]{:S(2)}, u32[]{:S(2)}) collective-permute-start(bf16[2,16,3072]{2,1,0:T(8,128)(2,1)S(1)} %get-tuple-element.87), channel_id=1, source_target_pairs={{0,8},{4,12},{8,0},{12,4},{16,24},{20,28},{24,16},{28,20},{1,9},{5... | collective-permute-start | bytes 589832 | tf_op jit(solution)/shard_map/ppermute | solution.py:49
  62.8 11.2 %collective-permute-start.16 = (bf16[1,16,3072]{2,1,0:T(8,128)(2,1)S(1)}, bf16[1,16,3072]{2,1,0:T(8,128)(2,1)S(1)}, u32[]{:S(2)}, u32[]{:S(2)}) collective-permute-start(bf16[1,16,3072]{2,1,0:T(8,128)(2,1)S(1)} %get-tuple-element.91), channel_id=1, source_target_pairs={{0,16},{4,20},{8,24},{12,28},{16,0},{20,4},{24,8},{28,12},{1,17},{... | collective-permute-start | bytes 294920 | tf_op jit(solution)/shard_map/ppermute | solution.py:49
  64.3 4.5 %collective-permute-start.18 = (bf16[1,2,2,1664]{3,2,1,0:T(2,128)(2,1)S(1)}, bf16[1,2,2,1664]{3,2,1,0:T(2,128)(2,1)S(1)}, u32[]{:S(2)}, u32[]{:S(2)}) collective-permute-start(bf16[1,2,2,1664]{3,2,1,0:T(2,128)(2,1)S(1)} %get-tuple-element.93), channel_id=1, source_target_pairs={{0,1},{1,0},{2,3},{3,2},{4,5},{5,4},{6,7},{7,6},{8,9},{9,8},{10,11... | collective-permute-start | bytes 39944 | tf_op jit(solution)/shard_map/ppermute | solution.py:49
  66.0 2.8 %copy-start.1 = (bf16[2,512,256]{2,1,0:T(8,128)(2,1)S(1)}, bf16[2,512,256]{2,1,0:T(8,128)(2,1)}, u32[]{:S(2)}) copy-start(bf16[2,512,256]{2,1,0:T(8,128)(2,1)} %k_ref.1) | copy-start | bytes 1572868
  66.0 2.8 %copy-start.2 = (bf16[2,512,256]{2,1,0:T(8,128)(2,1)S(1)}, bf16[2,512,256]{2,1,0:T(8,128)(2,1)}, u32[]{:S(2)}) copy-start(bf16[2,512,256]{2,1,0:T(8,128)(2,1)} %v_ref.1) | copy-start | bytes 1572868
  66.0 2.8 %copy-start.3 = (s32[2]{0:T(128)S(1)}, s32[2]{0:T(128)}, u32[]{:S(2)}) copy-start(s32[2]{0:T(128)} %lengths_ref.1) | copy-start | bytes 28
  66.1 6.8 %collective-permute-start.13 = (bf16[2,16,2304]{2,1,0:T(8,128)(2,1)S(1)}, bf16[2,16,2304]{2,1,0:T(8,128)(2,1)S(1)}, u32[]{:S(2)}, u32[]{:S(2)}) collective-permute-start(bf16[2,16,2304]{2,1,0:T(8,128)(2,1)S(1)} %get-tuple-element.86), channel_id=1, source_target_pairs={{0,8},{4,12},{8,0},{12,4},{16,24},{20,28},{24,16},{28,20},{1,9},{5... | collective-permute-start | bytes 442376 | tf_op jit(solution)/shard_map/ppermute | solution.py:49
  68.5 7.9 %collective-permute-start.17 = (bf16[1,16,3072]{2,1,0:T(8,128)(2,1)S(1)}, bf16[1,16,3072]{2,1,0:T(8,128)(2,1)S(1)}, u32[]{:S(2)}, u32[]{:S(2)}) collective-permute-start(bf16[1,16,3072]{2,1,0:T(8,128)(2,1)S(1)} %get-tuple-element.92), channel_id=1, source_target_pairs={{0,16},{4,20},{8,24},{12,28},{16,0},{20,4},{24,8},{28,12},{1,17},{... | collective-permute-start | bytes 294920 | tf_op jit(solution)/shard_map/ppermute | solution.py:49
  72.8 6.1 %collective-permute-start.15 = (bf16[1,16,2304]{2,1,0:T(8,128)(2,1)S(1)}, bf16[1,16,2304]{2,1,0:T(8,128)(2,1)S(1)}, u32[]{:S(2)}, u32[]{:S(2)}) collective-permute-start(bf16[1,16,2304]{2,1,0:T(8,128)(2,1)S(1)} %get-tuple-element.90), channel_id=1, source_target_pairs={{0,16},{4,20},{8,24},{12,28},{16,0},{20,4},{24,8},{28,12},{1,17},{... | collective-permute-start | bytes 221192 | tf_op jit(solution)/shard_map/ppermute | solution.py:49
